TPU v7x, 32 devices: a whole 2x2x4 slice. The times are simulated.
32 devices in a mesh: obs: 2 (over core), horiz: 16 (over z, y, x).
Axes of the slice: x: 2, y: 2, z: 4, core: 2. Of those that a mesh axis runs over, the one named last changes fastest.
Arguments:
- control: float32 [128, 16, 4096], P(None, 'obs', 'horiz'), may hold values from -6 to 6
- spread: float32 [128, 16, 4096], P(None, 'obs', 'horiz'), may hold values from 0.3 to 3
- vert_root: float32 [128, 128], replicated, as said below
- wind_lon: float32 [128, 16, 4096], P('horiz', 'obs'), may hold values from -0.45 to 0.45
- wind_lat: float32 [128, 16, 4096], P('horiz', 'obs'), may hold values from -0.45 to 0.45
- obs_dest: int32 [32768, 1], P(('obs', 'horiz')), may hold values from 0 to 15; in each aligned block of 1024 rows (0 to 1023, 1024 to 2047, ...) at most 64 rows name the same one
- obs_cells: int32 [4, 32768], P(None, ('obs', 'horiz')), may hold values from 0 to 262143
- obs_time: int32 [32768], P(('obs', 'horiz')), may hold values from 0 to 4
- obs_value: float32 [32768], P(('obs', 'horiz')), may hold values from -6 to 6
- obs_weight: float32 [4, 32768], P(None, ('obs', 'horiz')), may hold values from 0 to 1
- obs_rinv: float32 [32768], P(('obs', 'horiz')), may hold values from 0.3 to 3
Outputs:
- gradient: float32 [128, 16, 4096], P(None, 'obs', 'horiz')
- departure: float32 [32768], P(('obs', 'horiz'))
Inputs may be any that keep to these rules, and one draw needn't show every extreme that they name: `obs_dest`: in the rows of one device at most 64 observations name the same level group, a bound that some block reaches. `obs_cells`: cell index within the owner's block of 128 / 16 levels, 8 rows and 4096 longitudes, flattened in that order. `vert_root`: zero beyond 12 places from the diagonal; diagonal entries from 1 to 1.5.
All inputs are finite; a program needn't handle non-finite values.
Results may differ from a plain program's by a relative error of at most 0.00012.
Values sent between devices are 32-bit elements; how exact they have to be, the bound alone decides.
No kernel may reach another device: no remote copies, remote signals or barrier semaphores. Data moves between devices by JAX's collectives and lax.ppermute only.
A program may use at most 64 MiB of HBM per device.

v0:
```python
import functools

import jax
import jax.numpy as jnp
from jax import lax
from jax.experimental import pallas as pl
from jax.experimental.pallas import tpu as pltpu
from jax.sharding import PartitionSpec as P

NT = 4
CAP = 64
ROWS = 8
LANES = 128
FIELDS = 16
F32 = jnp.float32
I32 = jnp.int32
ANY = pl.BlockSpec(memory_space=pl.ANY)
VM = pl.BlockSpec(memory_space=pltpu.VMEM)


def call(body, out_shape, in_specs, out_specs, scratch=(), limit=40, cost=(1e6, 1e6)):
    return pl.pallas_call(
        body,
        out_shape=out_shape,
        in_specs=in_specs,
        out_specs=out_specs,
        scratch_shapes=list(scratch),
        compiler_params=pltpu.CompilerParams(vmem_limit_bytes=limit * 2**20),
        cost_estimate=pl.CostEstimate(
            flops=int(cost[0]), bytes_accessed=int(cost[1]), transcendentals=0
        ),
    )


def exchange(tile_rows, toward):
    count = lax.axis_size("obs")
    if count == 2:
        return lax.ppermute(tile_rows, "obs", [(0, 1), (1, 0)])
    below = lax.ppermute(tile_rows, "obs", [(i, i + 1) for i in range(count - 1)])
    above = lax.ppermute(tile_rows, "obs", [(i + 1, i) for i in range(count - 1)])
    first = (jnp.arange(ROWS) < ROWS // 2)[None, :, None]
    return jnp.where(first, above, below) if toward else jnp.where(first, below, above)


def halo_masks():
    first = (jnp.arange(ROWS) < ROWS // 2)[:, None]
    if lax.axis_size("obs") == 2:
        lower = lax.axis_index("obs") == 0
        front = jnp.where(lower, first, ~first)
        back = ~front
    else:
        front = back = jnp.ones_like(first)
    wide = lambda m: jnp.broadcast_to(m, (ROWS, LANES)).astype(F32)
    return wide(front), wide(back)


def wind_kernel(tiles, u_ref, uh_ref, v_ref, vh_ref, mask_ref, uo_ref, vo_ref, scr):
    levels = u_ref.shape[0]

    def level(l, carry):
        for src, rim, dst in ((u_ref, uh_ref, uo_ref), (v_ref, vh_ref, vo_ref)):
            for c in range(tiles):
                cols = pl.ds(c * LANES, LANES)
                scr[pl.ds(c * 16, 8), :] = src[l, :, cols]
                scr[pl.ds(c * 16 + 8, 8), :] = rim[l, :, cols] * mask_ref[...]
            for c in range(tiles):
                dst[l, pl.ds(c * 16, 8), :] = scr[pl.ds(c * 16, 8, stride=2), :]
                dst[l, pl.ds(c * 16 + 8, 8), :] = scr[pl.ds(c * 16 + 1, 8, stride=2), :]
        return carry

    lax.fori_loop(0, levels, level, 0)


def split3(x):
    a = x.astype(jnp.bfloat16)
    r = x - a.astype(F32)
    b = r.astype(jnp.bfloat16)
    return a, b, (r - b.astype(F32)).astype(jnp.bfloat16)


def bin_kernel(groups, dest_ref, data_ref, out_ref, placed_ref, hit):
    count = dest_ref.shape[0]
    slots = groups * CAP
    width = -(-groups // LANES) * LANES
    below = (
        lax.broadcasted_iota(I32, (LANES, LANES), 0) > lax.broadcasted_iota(I32, (LANES, LANES), 1)
    ).astype(jnp.bfloat16)
    lane = lax.broadcasted_iota(I32, (LANES, width), 1)
    slot_lane = lax.broadcasted_iota(I32, (LANES, slots), 1)
    seen = jnp.zeros((1, width), F32)
    for b in range(count // LANES):
        rows = pl.ds(b * LANES, LANES)
        owner = dest_ref[rows, :]
        mine = (lane == owner).astype(F32)
        before = (
            jnp.dot(below, mine.astype(jnp.bfloat16), preferred_element_type=F32) + seen
        )
        rank = jnp.sum(before * mine, axis=1, keepdims=True)
        seen = seen + jnp.sum(mine, axis=0, keepdims=True)
        placed = owner * CAP + rank.astype(I32)
        placed_ref[rows, :] = placed
        hit[rows, :] = jnp.where(slot_lane == placed, 1.0, 0.0).astype(jnp.bfloat16)
    parts = jnp.concatenate(split3(data_ref[...]), axis=0)
    got = jnp.dot(parts, hit[...], preferred_element_type=F32)
    sums = got[:FIELDS] + got[FIELDS : 2 * FIELDS] + got[2 * FIELDS :]
    for r in range(groups):
        out_ref[r] = sums[:, r * CAP : (r + 1) * CAP]


def hypercube(blocks):
    groups = blocks.shape[0]
    step = 1
    while step < groups:
        pairs = [(i, i ^ step) for i in range(groups)]
        view = blocks.reshape((groups // (2 * step), 2, step) + blocks.shape[1:])
        got = lax.ppermute(view[:, 1], "horiz", pairs)
        blocks = jnp.stack([view[:, 0], got], axis=1).reshape(blocks.shape)
        step *= 2
    return blocks


def prep_kernel(levels, tiles, got_ref, idx_ref, w_ref, vr_ref, scr):
    groups = got_ref.shape[0]
    lon = tiles * LANES
    for r in range(groups):
        part = pl.ds(r * CAP, CAP)
        block = got_ref[r]
        ints = block[0:8].astype(I32)
        cell = ints[0:4]
        time = ints[4:5]
        lev = cell // (ROWS * lon)
        row = (cell // lon) % ROWS
        col = cell % lon
        tile = (time * levels + lev) * tiles + col // LANES
        idx_ref[0:4, part] = tile * 16 + (row % 2) * 8 + row // 2
        idx_ref[4:8, part] = tile * 8 + (row % 2) * 4 + row // 2
        scr[0:4, part] = (col % LANES).astype(F32)
        scr[4:8, part] = jnp.zeros((4, CAP), F32)
        scr[8:16, part] = block[8:16]
    slots = groups * CAP
    lane = lax.broadcasted_iota(I32, (LANES, LANES), 1)
    for b in range(slots // LANES):
        rows = pl.ds(b * LANES, LANES)
        cols = jnp.transpose(scr[:, rows], (1, 0))
        for k in range(4):
            at = cols[:, k : k + 1].astype(I32)
            w_ref[k, rows, :] = jnp.where(lane == at, cols[:, 8 + k : 9 + k], 0.0)
        vr_ref[0, rows, :] = jnp.broadcast_to(cols[:, 12:13], (LANES, LANES))
        vr_ref[1, rows, :] = jnp.broadcast_to(cols[:, 13:14], (LANES, LANES))


def cycle_kernel(
    levels,
    tiles,
    field,
    halo,
    uw_hbm,
    vw_hbm,
    idx_hbm,
    w_hbm,
    vr_hbm,
    front_ref,
    own_out,
    rim_out,
    dep_out,
    uw,
    vw,
    states,
    f0,
    f1,
    f2,
    f3,
    w,
    vr,
    scr,
    picked,
    acc,
    flux,
    idx,
    sems,
    lsems,
):
    forcing = (f0, f1, f2, f3)
    slots = acc.shape[0]
    per = field.shape[2] // LANES
    block = tiles * 16
    loads = [
        pltpu.make_async_copy(idx_hbm, idx, sems.at[0]),
        pltpu.make_async_copy(w_hbm, w, sems.at[1]),
        pltpu.make_async_copy(vr_hbm, vr, sems.at[2]),
    ]

    def wind_loads(l):
        return (
            pltpu.make_async_copy(uw_hbm.at[l], uw.at[l], lsems.at[0, l]),
            pltpu.make_async_copy(vw_hbm.at[l], vw.at[l], lsems.at[1, l]),
        )

    for l in range(levels):
        for copy in wind_loads(l):
            copy.start()
    for copy in loads:
        copy.start()

    lane = lax.broadcasted_iota(I32, (8, LANES), 1)
    first = lane == 0
    last = lane == LANES - 1
    sub = lax.broadcasted_iota(I32, (8, LANES), 0)
    own = sub < 4
    zero = jnp.zeros((8, LANES), F32)
    east_of = lambda x: pltpu.roll(x, LANES - 1, 1)
    west_of = lambda x: pltpu.roll(x, 1, 1)

    def forward(l, carry):
        for copy in wind_loads(l):
            copy.wait()
        start = pl.multiple_of(l * block, block)
        for c in range(tiles):
            j, h = divmod(c, per)
            cols = pl.ds(h * LANES, LANES)
            scr[pl.ds(c * 16, 8), :] = field[j * levels + l, :, cols]
            scr[pl.ds(c * 16 + 8, 8), :] = halo[j * levels + l, :, cols] * front_ref[...]
        for c in range(tiles):
            states[pl.ds(start + c * 16, 8), :] = scr[pl.ds(c * 16, 8, stride=2), :]
            states[pl.ds(start + c * 16 + 8, 8), :] = scr[pl.ds(c * 16 + 1, 8, stride=2), :]
        fstart = pl.multiple_of(l * tiles * 8, tiles * 8)
        fstep = levels * tiles * 8
        for t in range(NT):
            src = pl.multiple_of(start + t * levels * block, block)
            dst = pl.multiple_of(start + (t + 1) * levels * block, block)

            def tile(c):
                c = c % tiles
                return (
                    states[pl.ds(src + c * 16, 8), :],
                    states[pl.ds(src + c * 16 + 8, 8), :],
                )

            q_w, q, q_e = tile(-1), tile(0), tile(1)
            w_w = [west_of(x) for x in q_w]
            w_c = [west_of(x) for x in q]
            e_c = [east_of(x) for x in q]
            for c in range(tiles):
                e_e = [east_of(x) for x in q_e]
                even, odd = q
                souths = (pltpu.roll(odd, 1, 0), even)
                norths = (odd, pltpu.roll(even, 7, 0))
                for side in range(2):
                    here = q[side]
                    at = pl.ds(c * 16 + side * 8, 8)
                    u = uw[l, at, :]
                    v = vw[l, at, :]
                    west = jnp.where(first, w_w[side], w_c[side])
                    east = jnp.where(last, e_e[side], e_c[side])
                    lon = jnp.where(u > 0, west, east)
                    lat = jnp.where(v > 0, souths[side], norths[side])
                    states[pl.ds(dst + c * 16 + side * 8, 8), :] = (
                        here + jnp.abs(u) * (lon - here) + jnp.abs(v) * (lat - here)
                    )
                for f in forcing:
                    f[pl.ds(pl.multiple_of(fstart + t * fstep, 8) + c * 8, 8), :] = zero
                    if t == NT - 1:
                        f[pl.ds(pl.multiple_of(fstart + NT * fstep, 8) + c * 8, 8), :] = zero
                w_w, w_c, e_c = w_c, [west_of(x) for x in q_e], e_e
                q, q_e = q_e, tile(c + 2)
        return carry

    lax.fori_loop(0, levels, forward, 0)

    for copy in loads:
        copy.wait()

    def gather(i, carry):
        base = pl.multiple_of(i * 8, 8)
        for k in range(4):
            for j in range(8):
                r = idx[k, base + j]
                picked[pl.ds(k * 8 + j, 1), :] = states[pl.ds(r, 1), :]
        total = w[0, pl.ds(base, 8), :] * picked[pl.ds(0, 8), :]
        for k in range(1, 4):
            total = total + w[k, pl.ds(base, 8), :] * picked[pl.ds(k * 8, 8), :]
        acc[pl.ds(base, 8), :] = total
        return carry

    lax.fori_loop(0, slots // 8, gather, 0)

    hx = jnp.sum(acc[...], axis=1, keepdims=True)
    dep_out[...] = vr[1] * (hx - vr[0])

    def scatter(i, carry):
        base = pl.multiple_of(i * 8, 8)
        dep = dep_out[pl.ds(base, 8), :]
        for k in range(4):
            flux[pl.ds(k * 8, 8), :] = w[k, pl.ds(base, 8), :] * dep
        for j in range(8):
            for k in range(4):
                r = idx[4 + k, base + j]
                at = pl.ds(r, 1)
                forcing[k][at, :] = forcing[k][at, :] + flux[pl.ds(k * 8 + j, 1), :]
        return carry

    lax.fori_loop(0, slots // 8, scatter, 0)

    def backward(l, carry):
        fstart = pl.multiple_of(l * tiles * 8, tiles * 8)
        fstep = levels * tiles * 8

        def force(t, c):
            at = pl.ds(pl.multiple_of(fstart + t * fstep, 8) + c * 8, 8)
            total = (f0[at, :] + f1[at, :]) + (f2[at, :] + f3[at, :])
            return (jnp.where(own, total, 0.0), jnp.where(own, pltpu.roll(total, 4, 0), 0.0))

        def fluxes(ref, c):
            c = c % tiles
            out = []
            for side in range(2):
                at = pl.ds(c * 16 + side * 8, 8)
                a = ref[at, :]
                u = uw[l, at, :]
                v = vw[l, at, :]
                x = jnp.abs(u) * a
                y = jnp.abs(v) * a
                p = jnp.where(u > 0, x, 0.0)
                s = jnp.where(v > 0, y, 0.0)
                out.append((a - x - y, east_of(p), west_of(x - p), s, y - s))
            return out

        for c in range(tiles):
            even, odd = force(NT, c)
            scr[pl.ds(c * 16, 8), :] = even
            scr[pl.ds(c * 16 + 8, 8), :] = odd
        half = tiles * 16
        for t in range(NT - 1, -1, -1):
            src = scr.at[pl.ds(0 if t % 2 else half, half)]
            dst = scr.at[pl.ds(half if t % 2 else 0, half)]
            before, now = fluxes(src, -1), fluxes(src, 0)
            head = now
            for c in range(tiles):
                after = head if c == tiles - 1 else fluxes(src, c + 1)
                fine = force(t, c)
                (_, _, _, s_e, n_e), (_, _, _, s_o, n_o) = now
                lats = (s_o + pltpu.roll(n_o, 1, 0), pltpu.roll(s_e, 7, 0) + n_e)
                for side in range(2):
                    stay, p, m, _, _ = now[side]
                    value = (
                        stay
                        + jnp.where(last, after[side][1], p)
                        + jnp.where(first, before[side][2], m)
                        + lats[side]
                        + fine[side]
                    )
                    dst[pl.ds(c * 16 + side * 8, 8), :] = value
                before, now = now, after
        for c in range(tiles):
            even = scr[pl.ds(c * 16, 8), :]
            odd = scr[pl.ds(c * 16 + 8, 8), :]
            scr[pl.ds(half + c * 16, 8, stride=2), :] = even
            scr[pl.ds(half + c * 16 + 1, 8, stride=2), :] = odd
        for c in range(tiles):
            j, h = divmod(c, per)
            cols = pl.ds(h * LANES, LANES)
            own_out[j * levels + l, :, cols] = scr[pl.ds(half + c * 16, 8), :]
            rim_out[j * levels + l, :, cols] = scr[pl.ds(half + c * 16 + 8, 8), :]
        return carry

    lax.fori_loop(0, levels, backward, 0)


def per_device(
    control,
    spread,
    vert_root,
    wind_lon,
    wind_lat,
    obs_dest,
    obs_cells,
    obs_time,
    obs_value,
    obs_weight,
    obs_rinv,
):
    levels_all = control.shape[0]
    width = control.shape[2]
    groups = lax.axis_size("horiz")
    levels, _, lon = wind_lon.shape
    tiles = lon // LANES
    slots = groups * CAP
    count = obs_value.shape[0]
    front, back = halo_masks()

    increment = spread * jnp.einsum(
        "lm,mrc->lrc",
        vert_root,
        control,
        precision=lax.Precision.HIGHEST,
        preferred_element_type=F32,
    )
    field = lax.all_to_all(increment, "horiz", split_axis=0, concat_axis=0, tiled=True)

    ring = jax.ShapeDtypeStruct((levels, tiles * 16, LANES), F32)
    uw, vw = call(
        functools.partial(wind_kernel, tiles),
        (ring, ring),
        [VM] * 5,
        (VM, VM),
        [pltpu.VMEM((tiles * 16, LANES), F32)],
        cost=(1e6, 8e6),
    )(wind_lon, exchange(wind_lon, True), wind_lat, exchange(wind_lat, True), front)

    target = obs_dest ^ lax.axis_index("horiz")
    blank = jnp.zeros((1, count), F32)
    data = jnp.concatenate(
        [obs_cells.astype(F32), obs_time[None].astype(F32)]
        + [blank] * 3
        + [obs_weight, obs_value[None], obs_rinv[None]]
        + [blank] * 2,
        axis=0,
    )
    binned, placed = call(
        functools.partial(bin_kernel, groups),
        (
            jax.ShapeDtypeStruct((groups, FIELDS, CAP), F32),
            jax.ShapeDtypeStruct((count, 1), I32),
        ),
        [VM] * 2,
        (VM, VM),
        [pltpu.VMEM((count, slots), jnp.bfloat16)],
        cost=(1e8, 4e6),
    )(target, data)
    got = hypercube(binned)
    idx, weights, pair = call(
        functools.partial(prep_kernel, levels, tiles),
        (
            jax.ShapeDtypeStruct((8, slots), I32),
            jax.ShapeDtypeStruct((4, slots, LANES), F32),
            jax.ShapeDtypeStruct((2, slots, LANES), F32),
        ),
        [VM],
        (VM, VM, VM),
        [pltpu.VMEM((FIELDS, slots), F32)],
        cost=(1e6, 6e6),
    )(got)

    halo = exchange(field, True)
    block = jax.ShapeDtypeStruct((groups * levels, ROWS, width), F32)
    forcing = pltpu.VMEM(((NT + 1) * levels * tiles * 8, LANES), F32)
    adjoint, rim, dep = call(
        functools.partial(cycle_kernel, levels, tiles),
        (block, block, jax.ShapeDtypeStruct((slots, LANES), F32)),
        [VM, VM, ANY, ANY, ANY, ANY, ANY, VM],
        (VM, VM, VM),
        [
            pltpu.VMEM((levels, tiles * 16, LANES), F32),
            pltpu.VMEM((levels, tiles * 16, LANES), F32),
            pltpu.VMEM(((NT + 1) * levels * tiles * 16, LANES), F32),
            forcing,
            forcing,
            forcing,
            forcing,
            pltpu.VMEM((4, slots, LANES), F32),
            pltpu.VMEM((2, slots, LANES), F32),
            pltpu.VMEM((2 * tiles * 16, LANES), F32),
            pltpu.VMEM((32, LANES), F32),
            pltpu.VMEM((slots, LANES), F32),
            pltpu.VMEM((32, LANES), F32),
            pltpu.SMEM((8, slots), I32),
            pltpu.SemaphoreType.DMA((3,)),
            pltpu.SemaphoreType.DMA((2, levels)),
        ],
        limit=56,
        cost=(1e8, 16e6),
    )(field, halo, uw, vw, idx, weights, pair, front)

    total = adjoint + exchange(rim, False) * back[:, :1][None]
    column = lax.all_to_all(total, "horiz", split_axis=0, concat_axis=0, tiled=True)

    back_home = hypercube(dep[:, 0].reshape(groups, CAP)).reshape(1, slots)
    departure = jnp.sum(
        jnp.where(placed == jnp.arange(slots, dtype=I32)[None, :], back_home, 0.0), axis=1
    )

    gradient = control + jnp.einsum(
        "lm,lrc->mrc",
        vert_root,
        spread * column,
        precision=lax.Precision.HIGHEST,
        preferred_element_type=F32,
    )
    return (gradient, departure)


def solution(mesh):
    in_specs = (
        P(None, "obs", "horiz"),
        P(None, "obs", "horiz"),
        P(),
        P("horiz", "obs", None),
        P("horiz", "obs", None),
        P(("obs", "horiz"), None),
        P(None, ("obs", "horiz")),
        P(("obs", "horiz")),
        P(("obs", "horiz")),
        P(None, ("obs", "horiz")),
        P(("obs", "horiz")),
    )
    out_specs = (P(None, "obs", "horiz"), P(("obs", "horiz")))
    return jax.shard_map(
        per_device, mesh=mesh, in_specs=in_specs, out_specs=out_specs, check_vma=False
    )
```

profile of v0, /device:TPU:0, one launch (start us, length us, event | category | flops | bytes accessed | tf_op | source)
XLA Modules:
  0.0 134.9 jit_solution(8608944884349249797)
XLA Ops:
  0.7 1.7 %copy.76 = f32[128,8,256]{0,2,1:T(8,128)S(1)} copy(f32[128,8,256]{2,1,0:T(8,128)} %param.11) | data formatting | bytes 2097152 | tf_op args[0]
  3.4 1.6 %copy_multiply_fusion = f32[128,8,256]{2,1,0:T(8,128)} fusion(f32[128,8,256]{2,1,0:T(8,128)S(1)} %copy-done.13, f32[128,8,256]{2,0,1:T(8,128)S(1)} %fusion.6), kind=kLoop, calls=%fused_computation.5 | loop fusion | flops 262144 | bytes 3145728 | tf_op jit(solution)/shard_map/mul | solution.py:391
  5.1 8.5 %all-to-all-start = ((f32[128,8,256]{2,1,0:T(8,128)}), f32[128,8,256]{2,1,0:T(8,128)}, u32[]{:S(2)}, u32[]{:S(2)}) async-start(f32[128,8,256]{2,1,0:T(8,128)} %copy_multiply_fusion), calls=%async_computation | async-start | bytes 2097152 | tf_op jit(solution)/shard_map/all_to_all | solution.py:398
  15.2 1.9 %collective-permute-start.3 = (f32[8,1,16,64]{3,2,0,1:T(8,128)S(1)}, f32[8,1,16,64]{3,2,0,1:T(8,128)S(1)}, u32[]{:S(2)}, u32[]{:S(2)}) collective-permute-start(f32[8,1,16,64]{3,2,0,1:T(8,128)S(1)} %get-tuple-element.37), channel_id=1, source_target_pairs={{0,1},{1,0},{2,3},{3,2},{4,5},{5,4},{6,7},{7,6},{8,9},{9,8},{10,11... | collective-permute-start | bytes 98312 | tf_op jit(solution)/shard_map/ppermute | solution.py:116
  17.1 2.9 %collective-permute-done.3 = f32[8,1,16,64]{3,2,0,1:T(8,128)S(1)} collective-permute-done((f32[8,1,16,64]{3,2,0,1:T(8,128)S(1)}, f32[8,1,16,64]{3,2,0,1:T(8,128)S(1)}, u32[]{:S(2)}, u32[]{:S(2)}) %collective-permute-start.3) | collective-permute-done | bytes 32800 | tf_op jit(solution)/shard_map/ppermute | solution.py:116
  20.0 1.5 %collective-permute-start.4 = (f32[4,2,16,64]{3,2,0,1:T(8,128)S(1)}, f32[4,2,16,64]{3,2,0,1:T(8,128)S(1)}, u32[]{:S(2)}, u32[]{:S(2)}) collective-permute-start(f32[4,2,16,64]{3,2,0,1:T(8,128)S(1)} %get-tuple-element.35), channel_id=1, source_target_pairs={{0,2},{1,3},{2,0},{3,1},{4,6},{5,7},{6,4},{7,5},{8,10},{9,11},{10,... | collective-permute-start | bytes 98312 | tf_op jit(solution)/shard_map/ppermute | solution.py:116
  22.1 16.0 %all-to-all-done.field = f32[128,8,256]{2,1,0:T(8,128)} async-done(((f32[128,8,256]{2,1,0:T(8,128)}), f32[128,8,256]{2,1,0:T(8,128)}, u32[]{:S(2)}, u32[]{:S(2)}) %all-to-all-start) | async-done | bytes 1048608 | tf_op jit(solution)/shard_map/all_to_all | solution.py:398
  38.1 3.1 %collective-permute-start.5 = (f32[2,4,16,64]{3,2,1,0:T(8,128)S(1)}, f32[2,4,16,64]{3,2,1,0:T(8,128)S(1)}, u32[]{:S(2)}, u32[]{:S(2)}) collective-permute-start(f32[2,4,16,64]{3,2,1,0:T(8,128)S(1)} %slice_bitcast_fusion.1), channel_id=1, source_target_pairs={{0,4},{1,5},{2,6},{3,7},{4,0},{5,1},{6,2},{7,3},{8,12},{9,13},{10,... | collective-permute-start | bytes 98312 | tf_op jit(solution)/shard_map/ppermute | solution.py:116
  41.2 2.8 %collective-permute-done.5 = f32[2,4,16,64]{3,2,1,0:T(8,128)S(1)} collective-permute-done((f32[2,4,16,64]{3,2,1,0:T(8,128)S(1)}, f32[2,4,16,64]{3,2,1,0:T(8,128)S(1)}, u32[]{:S(2)}, u32[]{:S(2)}) %collective-permute-start.5) | collective-permute-done | bytes 32800 | tf_op jit(solution)/shard_map/ppermute | solution.py:116
  45.5 5.1 %collective-permute-done.6 = f32[1,8,16,64]{3,2,1,0:T(8,128)S(1)} collective-permute-done((f32[1,8,16,64]{3,2,1,0:T(8,128)S(1)}, f32[1,8,16,64]{3,2,1,0:T(8,128)S(1)}, u32[]{:S(2)}, u32[]{:S(2)}) %collective-permute-start.6) | collective-permute-done | bytes 32800 | tf_op jit(solution)/shard_map/ppermute | solution.py:116
  50.6 2.0 %shard_map.124 = (s32[8,1024]{1,0:T(8,128)S(1)}, f32[4,1024,128]{2,1,0:T(8,128)S(1)}, f32[2,1024,128]{2,1,0:T(8,128)S(1)}) custom-call(f32[16,16,64]{2,1,0:T(8,128)S(1)} %bitcast.53), custom_call_target="tpu_custom_call" | custom-call | flops 1000000 | bytes 6000000 | tf_op jit(solution)/shard_map/pallas_call | solution.py:431
  55.1 1.8 %shard_map.122 = (f32[8,512,128]{2,1,0:T(8,128)S(1)}, f32[8,512,128]{2,1,0:T(8,128)S(1)}) custom-call(f32[8,8,4096]{2,1,0:T(8,128)S(1)} %copy-done.4, f32[8,8,4096]{2,1,0:T(8,128)S(1)} %collective-permute-done.1.uh_ref, f32[8,8,4096]{2,1,0:T(8,128)S(1)} %copy-done.5, f32[8,8,4096]{2,1,0:T(8,128)} %collective-permute-done.2.vh_ref, ...), custom_call_target="tpu_custom_call" | custom-call | flops 1000000 | bytes 8000000 | tf_op jit(solution)/shard_map/pallas_call | solution.py:401
  59.6 33.1 %shard_map.125 = (f32[128,8,256]{2,1,0:T(8,128)}, f32[128,8,256]{2,1,0:T(8,128)}, f32[1024,128]{1,0:T(8,128)}) custom-call(f32[128,8,256]{2,1,0:T(8,128)} %all-to-all-done.field, f32[128,8,256]{2,1,0:T(8,128)} %collective-permute-done.halo, f32[8,512,128]{2,1,0:T(8,128)} %copy-done.2, f32[8,512,128]{2,1,0:T(8,128)} %copy-done.3, s32[8,1024]{1,0:T(8,128)} %copy-done.10, ...), custom_call_target="tpu_custom_call" | custom-call | flops 100000000 | bytes 16000000 | tf_op jit(solution)/shard_map/pallas_call | solution.py:447
  92.8 2.8 %collective-permute-done.7 = f32[128,8,256]{2,1,0:T(8,128)S(1)} collective-permute-done((f32[128,8,256]{2,1,0:T(8,128)}, f32[128,8,256]{2,1,0:T(8,128)S(1)}, u32[]{:S(2)}, u32[]{:S(2)}) %collective-permute-start.7) | collective-permute-done | bytes 1048608 | tf_op jit(solution)/shard_map/ppermute | solution.py:38
  95.6 2.4 %multiply_add_fusion = f32[128,8,256]{2,1,0:T(8,128)} fusion(f32[128,8,256]{2,1,0:T(8,128)} %get-tuple-element.18, f32[128,8,256]{2,1,0:T(8,128)S(1)} %collective-permute-done.7, f32[8]{0:T(128)S(1)} %not_convert_fusion), kind=kLoop, calls=%fused_computation.6 | loop fusion | flops 524288 | bytes 3145760 | tf_op jit(solution)/shard_map/add | solution.py:474
  98.1 4.7 %all-to-all-start.1 = ((f32[128,8,256]{2,1,0:T(8,128)}), f32[128,8,256]{2,1,0:T(8,128)}, u32[]{:S(2)}, u32[]{:S(2)}) async-start(f32[128,8,256]{2,1,0:T(8,128)} %multiply_add_fusion), calls=%async_computation.1 | async-start | bytes 2097152 | tf_op jit(solution)/shard_map/all_to_all | solution.py:475
  103.1 1.6 %collective-permute-start.8 = (f32[8,1,64]{2,0,1:T(8,128)S(1)}, f32[8,1,64]{2,0,1:T(8,128)S(1)}, u32[]{:S(2)}, u32[]{:S(2)}) collective-permute-start(f32[8,1,64]{2,0,1:T(8,128)S(1)} %bitcast.76), channel_id=1, source_target_pairs={{0,1},{1,0},{2,3},{3,2},{4,5},{5,4},{6,7},{7,6},{8,9},{9,8},{10,11... | collective-permute-start | bytes 6152 | tf_op jit(solution)/shard_map/ppermute | solution.py:116
  104.7 3.5 %collective-permute-done.8 = f32[8,1,64]{2,0,1:T(8,128)S(1)} collective-permute-done((f32[8,1,64]{2,0,1:T(8,128)S(1)}, f32[8,1,64]{2,0,1:T(8,128)S(1)}, u32[]{:S(2)}, u32[]{:S(2)}) %collective-permute-start.8) | collective-permute-done | bytes 2080 | tf_op jit(solution)/shard_map/ppermute | solution.py:116
  108.2 1.5 %collective-permute-start.9 = (f32[4,2,64]{2,0,1:T(4,128)S(1)}, f32[4,2,64]{2,0,1:T(4,128)S(1)}, u32[]{:S(2)}, u32[]{:S(2)}) collective-permute-start(f32[4,2,64]{2,0,1:T(4,128)S(1)} %bitcast.75), channel_id=1, source_target_pairs={{0,2},{1,3},{2,0},{3,1},{4,6},{5,7},{6,4},{7,5},{8,10},{9,11},{10,... | collective-permute-start | bytes 6152 | tf_op jit(solution)/shard_map/ppermute | solution.py:116
  109.8 2.2 %collective-permute-done.9 = f32[4,2,64]{2,0,1:T(4,128)S(1)} collective-permute-done((f32[4,2,64]{2,0,1:T(4,128)S(1)}, f32[4,2,64]{2,0,1:T(4,128)S(1)}, u32[]{:S(2)}, u32[]{:S(2)}) %collective-permute-start.9) | collective-permute-done | bytes 2080 | tf_op jit(solution)/shard_map/ppermute | solution.py:116
  113.5 7.0 %collective-permute-done.10 = f32[2,4,64]{2,0,1:T(2,128)S(1)} collective-permute-done((f32[2,4,64]{2,0,1:T(2,128)S(1)}, f32[2,4,64]{2,0,1:T(2,128)S(1)}, u32[]{:S(2)}, u32[]{:S(2)}) %collective-permute-start.10) | collective-permute-done | bytes 2080 | tf_op jit(solution)/shard_map/ppermute | solution.py:116
  120.4 4.4 %collective-permute-start.11 = (f32[1,8,64]{2,1,0:T(8,128)S(1)}, f32[1,8,64]{2,1,0:T(8,128)S(1)}, u32[]{:S(2)}, u32[]{:S(2)}) collective-permute-start(f32[1,8,64]{2,1,0:T(8,128)S(1)} %bitcast.72), channel_id=1, source_target_pairs={{0,8},{1,9},{2,10},{3,11},{4,12},{5,13},{6,14},{7,15},{8,0},{9,1},... | collective-permute-start | bytes 6152 | tf_op jit(solution)/shard_map/ppermute | solution.py:116
  125.0 3.8 %collective-permute-done.11 = f32[1,8,64]{2,1,0:T(8,128)S(1)} collective-permute-done((f32[1,8,64]{2,1,0:T(8,128)S(1)}, f32[1,8,64]{2,1,0:T(8,128)S(1)}, u32[]{:S(2)}, u32[]{:S(2)}) %collective-permute-start.11) | collective-permute-done | bytes 2080 | tf_op jit(solution)/shard_map/ppermute | solution.py:116
  131.6 1.9 %fusion = f32[128,8,256]{0,2,1:T(8,128)S(1)} fusion(f32[128,8,256]{0,2,1:T(8,128)S(1)} %copy-done.12, f32[128,8,256]{2,1,0:T(8,128)S(1)} %mul.17, f32[128,128]{1,0:T(8,128)S(1)} %copy-done), kind=kOutput, calls=%fused_computation.3 | convolution fusion | flops 402915328 | bytes 3211264 | tf_op jit(solution)/shard_map/lm,lrc->mrc/dot_general | solution.py:482
  (90 shorter events, 15.9 us)
Async XLA Ops:
  3.4 10.2 %copy-start.21 = (s32[1024]{0:T(1024)S(1)}, s32[1024]{0:T(1024)}, u32[]{:S(2)}) copy-start(s32[1024]{0:T(1024)} %param.18) | copy-start | bytes 12292
  3.4 10.2 %copy-start.17 = (s32[4,1024]{1,0:T(4,128)S(1)}, s32[4,1024]{1,0:T(4,128)}, u32[]{:S(2)}) copy-start(s32[4,1024]{1,0:T(4,128)} %param.17) | copy-start | bytes 49156
  3.4 10.2 %copy-start.18 = (s32[1024,1]{0,1:T(1,128)S(1)}, s32[1024,1]{0,1:T(1,128)}, u32[]{:S(2)}) copy-start(s32[1024,1]{0,1:T(1,128)} %param.16) | copy-start | bytes 12292
  5.1 8.9 %copy-start.19 = (f32[1024]{0:T(1024)S(1)}, f32[1024]{0:T(1024)}, u32[]{:S(2)}) copy-start(f32[1024]{0:T(1024)} %param.19) | copy-start | bytes 12292
  5.1 8.9 %copy-start.20 = (f32[1024]{0:T(1024)S(1)}, f32[1024]{0:T(1024)}, u32[]{:S(2)}) copy-start(f32[1024]{0:T(1024)} %param.21) | copy-start | bytes 12292
  5.1 16.5 %copy-start.4 = (f32[8,8,4096]{2,1,0:T(8,128)S(1)}, f32[8,8,4096]{2,1,0:T(8,128)}, u32[]{:S(2)}) copy-start(f32[8,8,4096]{2,1,0:T(8,128)} %u_ref.1) | copy-start | bytes 3145732
  5.1 16.5 %copy-start.5 = (f32[8,8,4096]{2,1,0:T(8,128)S(1)}, f32[8,8,4096]{2,1,0:T(8,128)}, u32[]{:S(2)}) copy-start(f32[8,8,4096]{2,1,0:T(8,128)} %v_ref.1) | copy-start | bytes 3145732
  5.1 33.0 %all-to-all-start = ((f32[128,8,256]{2,1,0:T(8,128)}), f32[128,8,256]{2,1,0:T(8,128)}, u32[]{:S(2)}, u32[]{:S(2)}) async-start(f32[128,8,256]{2,1,0:T(8,128)} %copy_multiply_fusion), calls=%async_computation | async-start | bytes 2097152 | tf_op jit(solution)/shard_map/all_to_all | solution.py:398
  15.2 4.8 %collective-permute-start.3 = (f32[8,1,16,64]{3,2,0,1:T(8,128)S(1)}, f32[8,1,16,64]{3,2,0,1:T(8,128)S(1)}, u32[]{:S(2)}, u32[]{:S(2)}) collective-permute-start(f32[8,1,16,64]{3,2,0,1:T(8,128)S(1)} %get-tuple-element.37), channel_id=1, source_target_pairs={{0,1},{1,0},{2,3},{3,2},{4,5},{5,4},{6,7},{7,6},{8,9},{9,8},{10,11... | collective-permute-start | bytes 98312 | tf_op jit(solution)/shard_map/ppermute | solution.py:116
  20.0 18.1 %collective-permute-start.4 = (f32[4,2,16,64]{3,2,0,1:T(8,128)S(1)}, f32[4,2,16,64]{3,2,0,1:T(8,128)S(1)}, u32[]{:S(2)}, u32[]{:S(2)}) collective-permute-start(f32[4,2,16,64]{3,2,0,1:T(8,128)S(1)} %get-tuple-element.35), channel_id=1, source_target_pairs={{0,2},{1,3},{2,0},{3,1},{4,6},{5,7},{6,4},{7,5},{8,10},{9,11},{10,... | collective-permute-start | bytes 98312 | tf_op jit(solution)/shard_map/ppermute | solution.py:116
  21.6 33.4 %collective-permute-start.1 = (f32[8,8,4096]{2,1,0:T(8,128)S(1)}, f32[8,8,4096]{2,1,0:T(8,128)S(1)}, u32[]{:S(2)}, u32[]{:S(2)}) collective-permute-start(f32[8,8,4096]{2,1,0:T(8,128)S(1)} %copy-done.4), channel_id=1, source_target_pairs={{0,16},{16,0},{1,17},{17,1},{2,18},{18,2},{3,19},{19,3},{4,20},{20... | collective-permute-start | bytes 3145736 | tf_op jit(solution)/shard_map/ppermute | solution.py:38
  21.6 33.4 %collective-permute-start.2 = (f32[8,8,4096]{2,1,0:T(8,128)S(1)}, f32[8,8,4096]{2,1,0:T(8,128)}, u32[]{:S(2)}, u32[]{:S(2)}) collective-permute-start(f32[8,8,4096]{2,1,0:T(8,128)S(1)} %copy-done.5), channel_id=1, source_target_pairs={{0,16},{16,0},{1,17},{17,1},{2,18},{18,2},{3,19},{19,3},{4,20},{20... | collective-permute-start | bytes 3145736 | tf_op jit(solution)/shard_map/ppermute | solution.py:38
  38.1 21.5 %collective-permute-start = (f32[128,8,256]{2,1,0:T(8,128)}, f32[128,8,256]{2,1,0:T(8,128)}, u32[]{:S(2)}, u32[]{:S(2)}) collective-permute-start(f32[128,8,256]{2,1,0:T(8,128)} %all-to-all-done.field), channel_id=1, source_target_pairs={{0,16},{16,0},{1,17},{17,1},{2,18},{18,2},{3,19},{19,3},{4,20},{20... | collective-permute-start | bytes 3145736 | tf_op jit(solution)/shard_map/ppermute | solution.py:38
  38.1 5.9 %collective-permute-start.5 = (f32[2,4,16,64]{3,2,1,0:T(8,128)S(1)}, f32[2,4,16,64]{3,2,1,0:T(8,128)S(1)}, u32[]{:S(2)}, u32[]{:S(2)}) collective-permute-start(f32[2,4,16,64]{3,2,1,0:T(8,128)S(1)} %slice_bitcast_fusion.1), channel_id=1, source_target_pairs={{0,4},{1,5},{2,6},{3,7},{4,0},{5,1},{6,2},{7,3},{8,12},{9,13},{10,... | collective-permute-start | bytes 98312 | tf_op jit(solution)/shard_map/ppermute | solution.py:116
  44.1 6.6 %collective-permute-start.6 = (f32[1,8,16,64]{3,2,1,0:T(8,128)S(1)}, f32[1,8,16,64]{3,2,1,0:T(8,128)S(1)}, u32[]{:S(2)}, u32[]{:S(2)}) collective-permute-start(f32[1,8,16,64]{3,2,1,0:T(8,128)S(1)} %get-tuple-element.33), channel_id=1, source_target_pairs={{0,8},{1,9},{2,10},{3,11},{4,12},{5,13},{6,14},{7,15},{8,0},{9,1},... | collective-permute-start | bytes 98312 | tf_op jit(solution)/shard_map/ppermute | solution.py:116
  92.7 2.9 %collective-permute-start.7 = (f32[128,8,256]{2,1,0:T(8,128)}, f32[128,8,256]{2,1,0:T(8,128)S(1)}, u32[]{:S(2)}, u32[]{:S(2)}) collective-permute-start(f32[128,8,256]{2,1,0:T(8,128)} %get-tuple-element.19), channel_id=1, source_target_pairs={{0,16},{16,0},{1,17},{17,1},{2,18},{18,2},{3,19},{19,3},{4,20},{20... | collective-permute-start | bytes 3145736 | tf_op jit(solution)/shard_map/ppermute | solution.py:38
  98.1 26.7 %copy-start.8 = (s32[1024,1]{1,0:T(8,128)S(1)}, s32[1024,1]{1,0:T(8,128)}, u32[]{:S(2)}) copy-start(s32[1024,1]{1,0:T(8,128)} %copy-done.7) | copy-start | bytes 12292
  98.1 32.1 %copy-start.14 = (f32[128,8,256]{2,1,0:T(8,128)S(1)}, f32[128,8,256]{2,1,0:T(8,128)}, u32[]{:S(2)}) copy-start(f32[128,8,256]{2,1,0:T(8,128)} %param.12) | copy-start | bytes 3145732
  98.1 32.1 %all-to-all-start.1 = ((f32[128,8,256]{2,1,0:T(8,128)}), f32[128,8,256]{2,1,0:T(8,128)}, u32[]{:S(2)}, u32[]{:S(2)}) async-start(f32[128,8,256]{2,1,0:T(8,128)} %multiply_add_fusion), calls=%async_computation.1 | async-start | bytes 2097152 | tf_op jit(solution)/shard_map/all_to_all | solution.py:475
  102.8 28.8 %copy-start.12 = (f32[128,8,256]{0,2,1:T(8,128)S(1)}, f32[128,8,256]{0,2,1:T(8,128)}, u32[]{:S(2)}) copy-start(f32[128,8,256]{0,2,1:T(8,128)} %copy-done.11) | copy-start | bytes 3145732
  103.1 5.1 %collective-permute-start.8 = (f32[8,1,64]{2,0,1:T(8,128)S(1)}, f32[8,1,64]{2,0,1:T(8,128)S(1)}, u32[]{:S(2)}, u32[]{:S(2)}) collective-permute-start(f32[8,1,64]{2,0,1:T(8,128)S(1)} %bitcast.76), channel_id=1, source_target_pairs={{0,1},{1,0},{2,3},{3,2},{4,5},{5,4},{6,7},{7,6},{8,9},{9,8},{10,11... | collective-permute-start | bytes 6152 | tf_op jit(solution)/shard_map/ppermute | solution.py:116
  108.2 3.7 %collective-permute-start.9 = (f32[4,2,64]{2,0,1:T(4,128)S(1)}, f32[4,2,64]{2,0,1:T(4,128)S(1)}, u32[]{:S(2)}, u32[]{:S(2)}) collective-permute-start(f32[4,2,64]{2,0,1:T(4,128)S(1)} %bitcast.75), channel_id=1, source_target_pairs={{0,2},{1,3},{2,0},{3,1},{4,6},{5,7},{6,4},{7,5},{8,10},{9,11},{10,... | collective-permute-start | bytes 6152 | tf_op jit(solution)/shard_map/ppermute | solution.py:116
  111.9 8.5 %collective-permute-start.10 = (f32[2,4,64]{2,0,1:T(2,128)S(1)}, f32[2,4,64]{2,0,1:T(2,128)S(1)}, u32[]{:S(2)}, u32[]{:S(2)}) collective-permute-start(f32[2,4,64]{2,0,1:T(2,128)S(1)} %bitcast.78), channel_id=1, source_target_pairs={{0,4},{1,5},{2,6},{3,7},{4,0},{5,1},{6,2},{7,3},{8,12},{9,13},{10,... | collective-permute-start | bytes 6152 | tf_op jit(solution)/shard_map/ppermute | solution.py:116
  120.4 8.4 %collective-permute-start.11 = (f32[1,8,64]{2,1,0:T(8,128)S(1)}, f32[1,8,64]{2,1,0:T(8,128)S(1)}, u32[]{:S(2)}, u32[]{:S(2)}) collective-permute-start(f32[1,8,64]{2,1,0:T(8,128)S(1)} %bitcast.72), channel_id=1, source_target_pairs={{0,8},{1,9},{2,10},{3,11},{4,12},{5,13},{6,14},{7,15},{8,0},{9,1},... | collective-permute-start | bytes 6152 | tf_op jit(solution)/shard_map/ppermute | solution.py:116
  (12 other events, 36.7 us)
where the time goes:
time: 135 us
  waiting for transfers between devices  46.1 us (34%)
  Pallas kernels  37.9 us (28%)
  starting transfers between devices  30.8 us (23%)
  local copies, waits for them, and re-layouts  9.03 us (7%)
  other arithmetic  7.02 us (5%)
  matrix products  2.93 us (2%)
    pallas_call x1, Pallas kernels, per_device(): call(functools.partial(cycle_kernel, levels, tiles), (block, block, jax.S...  33.1 us
    ppermute x8, waiting for transfers between devices, hypercube(): got = lax.ppermute(view[:, 1], 'horiz', pairs)  27.2 us
    ppermute x8, starting transfers between devices, hypercube(): got = lax.ppermute(view[:, 1], 'horiz', pairs)  17.1 us
    all_to_all x1, waiting for transfers between devices, per_device(): lax.all_to_all(increment, 'horiz', split_axis=0, concat_axis=0, tiled=True)  16 us
    all_to_all x1, starting transfers between devices, per_device(): lax.all_to_all(increment, 'horiz', split_axis=0, concat_axis=0, tiled=True)  8.51 us
    unnamed x47, local copies, waits for them, and re-layouts  8.44 us
    all_to_all x1, starting transfers between devices, per_device(): lax.all_to_all(total, 'horiz', split_axis=0, concat_axis=0, tiled=True)  4.65 us
    ppermute x4, waiting for transfers between devices, exchange(): return lax.ppermute(tile_rows, 'obs', [(0, 1), (1, 0)])  2.85 us
  transfers between devices with their start and end apart: 14, of which 9 were waited for; matrix products, arithmetic and copies ran while one was open for 2% of the time, Pallas kernels for 4%

commit v1 on v0

--- a/solution.py
+++ b/solution.py
@@ -18,10 +18,11 @@
 VM = pl.BlockSpec(memory_space=pltpu.VMEM)
 
 
-def call(body, out_shape, in_specs, out_specs, scratch=(), limit=40, cost=(1e6, 1e6)):
+def call(body, out_shape, in_specs, out_specs, scratch=(), limit=40, cost=(1e6, 1e6), grid=()):
     return pl.pallas_call(
         body,
         out_shape=out_shape,
+        grid=grid,
         in_specs=in_specs,
         out_specs=out_specs,
         scratch_shapes=list(scratch),
@@ -32,13 +33,166 @@
     )
 
 
+def split2(x):
+    a = x.astype(jnp.bfloat16)
+    return a, (x - a.astype(F32)).astype(jnp.bfloat16)
+
+
+def wide_root(root):
+    high, low = split2(root)
+    return jnp.concatenate([high, high, low], axis=1)
+
+
+def apply_root(wide, columns):
+    high, low = split2(columns)
+    return jnp.dot(wide, jnp.concatenate([high, low, high], axis=0), preferred_element_type=F32)
+
+
+def level_rows(r, levels):
+    return pl.ds(r, levels, stride=ROWS)
+
+
+def start_kernel(
+    groups,
+    root_hbm,
+    control_hbm,
+    spread_hbm,
+    dest_hbm,
+    cells_hbm,
+    time_hbm,
+    value_hbm,
+    weight_hbm,
+    rinv_hbm,
+    out_hbm,
+    placed_ref,
+    root,
+    control,
+    spread,
+    dest,
+    cells,
+    time,
+    value,
+    weight,
+    rinv,
+    out,
+    data,
+    hit,
+    small_sems,
+    sems,
+    out_sems,
+):
+    levels_all = root.shape[0]
+    levels = levels_all // groups
+    halves = control.shape[0]
+    smalls = [
+        pltpu.make_async_copy(a, b, small_sems.at[i])
+        for i, (a, b) in enumerate(
+            (
+                (dest_hbm, dest),
+                (cells_hbm, cells),
+                (time_hbm, time),
+                (value_hbm, value),
+                (weight_hbm, weight),
+                (rinv_hbm, rinv),
+                (root_hbm, root),
+            )
+        )
+    ]
+    for copy in smalls:
+        copy.start()
+
+    def part(h):
+        cols = pl.ds(h * LANES, LANES)
+        return (
+            pltpu.make_async_copy(control_hbm.at[:, cols], control.at[h], sems.at[0, h]),
+            pltpu.make_async_copy(spread_hbm.at[:, cols], spread.at[h], sems.at[1, h]),
+        )
+
+    parts = [part(h) for h in range(halves)]
+    for i in range(2):
+        for h in range(halves):
+            parts[h][i].start()
+    for copy in smalls:
+        copy.wait()
+    bin_observations(groups, dest, cells, time, value, weight, rinv, placed_ref, out, data, hit)
+    wide = wide_root(root[...])
+    block = levels * ROWS
+    outs = []
+    for h in range(halves):
+        parts[h][0].wait()
+        results = [apply_root(wide, control[h, level_rows(r, levels_all), :]) for r in range(ROWS)]
+        parts[h][1].wait()
+        for r in range(ROWS):
+            value_r = spread[h, level_rows(r, levels_all), :] * results[r]
+            for g in range(groups):
+                out[g, pl.ds(h * block + r, levels, stride=ROWS), :] = value_r[
+                    g * levels : (g + 1) * levels
+                ]
+        rows = pl.ds(h * block, block + (ROWS if h == halves - 1 else 0))
+        outs.append(
+            pltpu.make_async_copy(out.at[:, rows, :], out_hbm.at[:, rows, :], out_sems.at[h])
+        )
+        outs[-1].start()
+    for copy in outs:
+        copy.wait()
+
+
+def end_kernel(groups, root_ref, control_ref, spread_ref, got_ref, placed_ref, out_hbm, dep_ref, control, spread, out, row, sems):
+    levels_all = root_ref.shape[0]
+    levels = levels_all // groups
+    halves = out.shape[0]
+    block = levels * ROWS
+    wide = wide_root(root_ref[...])
+    outs = []
+    for h in range(halves):
+        cols = pl.ds(h * LANES, LANES)
+        control[h] = control_ref[:, cols]
+        spread[h] = spread_ref[:, cols]
+        for r in range(ROWS):
+            at = level_rows(r, levels_all)
+            adjoint = jnp.concatenate(
+                [
+                    got_ref[g, pl.ds(h * block + r, levels, stride=ROWS), :]
+                    for g in range(groups)
+                ],
+                axis=0,
+            )
+            out[h, at, :] = control[h, at, :] + apply_root(wide, spread[h, at, :] * adjoint)
+        outs.append(pltpu.make_async_copy(out.at[h], out_hbm.at[:, cols], sems.at[h]))
+        outs[-1].start()
+    for r in range(groups):
+        row[0:1, r * CAP : (r + 1) * CAP] = got_ref[r, pl.ds(halves * block, 1), 0:CAP]
+    lane = lax.broadcasted_iota(I32, (LANES, LANES), 1)
+    for b in range(dep_ref.shape[0]):
+        placed = to_column(placed_ref[pl.ds(b, 1), :]).astype(I32)
+        total = jnp.zeros((LANES, LANES), F32)
+        for c in range(groups * CAP // LANES):
+            value = row[0:1, c * LANES : (c + 1) * LANES]
+            total = total + jnp.where(lane + c * LANES == placed, value, 0.0)
+        dep_ref[pl.ds(b, 1), :] = to_row(
+            jnp.broadcast_to(jnp.sum(total, axis=1, keepdims=True), (LANES, LANES))
+        )
+    for copy in outs:
+        copy.wait()
+
+
+def rim_kernel(own_ref, rim_ref, mask_ref, out_ref):
+    mask = mask_ref[...]
+    rows = rim_ref.shape[1]
+    for c in range(rows // ROWS):
+        at = pl.ds(c * ROWS, ROWS)
+        out_ref[:, at, :] = own_ref[:, at, :] + rim_ref[:, at, :] * mask[None]
+    rest = pl.ds(rows, ROWS)
+    out_ref[:, rest, :] = own_ref[:, rest, :]
+
+
 def exchange(tile_rows, toward):
     count = lax.axis_size("obs")
     if count == 2:
         return lax.ppermute(tile_rows, "obs", [(0, 1), (1, 0)])
     below = lax.ppermute(tile_rows, "obs", [(i, i + 1) for i in range(count - 1)])
     above = lax.ppermute(tile_rows, "obs", [(i + 1, i) for i in range(count - 1)])
-    first = (jnp.arange(ROWS) < ROWS // 2)[None, :, None]
+    first = (jnp.arange(tile_rows.shape[1]) % ROWS < ROWS // 2)[None, :, None]
     return jnp.where(first, above, below) if toward else jnp.where(first, below, above)
 
 
@@ -78,8 +232,20 @@
     return a, b, (r - b.astype(F32)).astype(jnp.bfloat16)
 
 
-def bin_kernel(groups, dest_ref, data_ref, out_ref, placed_ref, hit):
-    count = dest_ref.shape[0]
+def to_row(wide):
+    at = lax.broadcasted_iota(I32, (LANES, LANES), 0) == lax.broadcasted_iota(I32, (LANES, LANES), 1)
+    return jnp.sum(jnp.where(at, wide, 0.0), axis=0, keepdims=True)
+
+
+def to_column(row):
+    at = lax.broadcasted_iota(I32, (LANES, LANES), 0) == lax.broadcasted_iota(I32, (LANES, LANES), 1)
+    return jnp.sum(jnp.where(at, row, 0.0), axis=1, keepdims=True)
+
+
+def bin_observations(
+    groups, dest_ref, cells_ref, time_ref, value_ref, weight_ref, rinv_ref, placed_ref, out, data, hit
+):
+    count = dest_ref.shape[1]
     slots = groups * CAP
     width = -(-groups // LANES) * LANES
     below = (
@@ -88,9 +254,10 @@
     lane = lax.broadcasted_iota(I32, (LANES, width), 1)
     slot_lane = lax.broadcasted_iota(I32, (LANES, slots), 1)
     seen = jnp.zeros((1, width), F32)
+    target = dest_ref[...].astype(F32)
     for b in range(count // LANES):
         rows = pl.ds(b * LANES, LANES)
-        owner = dest_ref[rows, :]
+        owner = to_column(target[:, b * LANES : (b + 1) * LANES]).astype(I32)
         mine = (lane == owner).astype(F32)
         before = (
             jnp.dot(below, mine.astype(jnp.bfloat16), preferred_element_type=F32) + seen
@@ -98,109 +265,94 @@
         rank = jnp.sum(before * mine, axis=1, keepdims=True)
         seen = seen + jnp.sum(mine, axis=0, keepdims=True)
         placed = owner * CAP + rank.astype(I32)
-        placed_ref[rows, :] = placed
+        placed_ref[pl.ds(b, 1), :] = to_row(
+            jnp.broadcast_to(placed.astype(F32), (LANES, LANES))
+        )
         hit[rows, :] = jnp.where(slot_lane == placed, 1.0, 0.0).astype(jnp.bfloat16)
-    parts = jnp.concatenate(split3(data_ref[...]), axis=0)
+    data[0:4, :] = cells_ref[...].astype(F32)
+    data[4:5, :] = time_ref[...].astype(F32)
+    data[5:8, :] = jnp.zeros((3, count), F32)
+    data[8:12, :] = weight_ref[...]
+    data[12:13, :] = value_ref[...]
+    data[13:14, :] = rinv_ref[...]
+    data[14:16, :] = jnp.zeros((2, count), F32)
+    parts = jnp.concatenate(split3(data[...]), axis=0)
     got = jnp.dot(parts, hit[...], preferred_element_type=F32)
     sums = got[:FIELDS] + got[FIELDS : 2 * FIELDS] + got[2 * FIELDS :]
-    for r in range(groups):
-        out_ref[r] = sums[:, r * CAP : (r + 1) * CAP]
-
-
-def hypercube(blocks):
-    groups = blocks.shape[0]
-    step = 1
-    while step < groups:
-        pairs = [(i, i ^ step) for i in range(groups)]
-        view = blocks.reshape((groups // (2 * step), 2, step) + blocks.shape[1:])
-        got = lax.ppermute(view[:, 1], "horiz", pairs)
-        blocks = jnp.stack([view[:, 0], got], axis=1).reshape(blocks.shape)
-        step *= 2
-    return blocks
-
-
-def prep_kernel(levels, tiles, got_ref, idx_ref, w_ref, vr_ref, scr):
-    groups = got_ref.shape[0]
+    last = out.shape[1] - ROWS
+    for g in range(groups):
+        part = sums[:, g * CAP : (g + 1) * CAP]
+        out[g, pl.ds(last, ROWS), 0:CAP] = part[0:ROWS]
+        out[g, pl.ds(last, ROWS), CAP : 2 * CAP] = part[ROWS:FIELDS]
+
+
+def prep_kernel(groups, levels, tiles, got_hbm, idx_ref, w_ref, vr_ref, got, scr, columns, sem):
+    last = got_hbm.shape[1] - ROWS
+    load = pltpu.make_async_copy(got_hbm.at[:, pl.ds(last, ROWS), :], got, sem)
+    load.start()
+    scr[...] = jnp.zeros_like(scr)
+    load.wait()
     lon = tiles * LANES
-    for r in range(groups):
-        part = pl.ds(r * CAP, CAP)
-        block = got_ref[r]
-        ints = block[0:8].astype(I32)
+    for g in range(groups):
+        part = pl.ds(g * CAP, CAP)
+        ints = got[g, :, 0:CAP].astype(I32)
         cell = ints[0:4]
         time = ints[4:5]
         lev = cell // (ROWS * lon)
         row = (cell // lon) % ROWS
         col = cell % lon
         tile = (time * levels + lev) * tiles + col // LANES
-        idx_ref[0:4, part] = tile * 16 + (row % 2) * 8 + row // 2
-        idx_ref[4:8, part] = tile * 8 + (row % 2) * 4 + row // 2
-        scr[0:4, part] = (col % LANES).astype(F32)
-        scr[4:8, part] = jnp.zeros((4, CAP), F32)
-        scr[8:16, part] = block[8:16]
+        scr[0:4, part] = (tile * 16 + (row % 2) * 8 + row // 2).astype(F32)
+        scr[8:12, part] = (col % LANES).astype(F32)
+        scr[16:24, part] = got[g, :, CAP : 2 * CAP]
+        scr[32:36, part] = (tile * 8 + (row % 2) * 4 + row // 2).astype(F32)
     slots = groups * CAP
     lane = lax.broadcasted_iota(I32, (LANES, LANES), 1)
+    few = LANES // 8
+    narrow = lax.broadcasted_iota(I32, (few, LANES), 1)
     for b in range(slots // LANES):
         rows = pl.ds(b * LANES, LANES)
         cols = jnp.transpose(scr[:, rows], (1, 0))
         for k in range(4):
-            at = cols[:, k : k + 1].astype(I32)
-            w_ref[k, rows, :] = jnp.where(lane == at, cols[:, 8 + k : 9 + k], 0.0)
-        vr_ref[0, rows, :] = jnp.broadcast_to(cols[:, 12:13], (LANES, LANES))
-        vr_ref[1, rows, :] = jnp.broadcast_to(cols[:, 13:14], (LANES, LANES))
+            at = cols[:, 8 + k : 9 + k].astype(I32)
+            w_ref[k, rows, :] = jnp.where(lane == at, cols[:, 16 + k : 17 + k], 0.0)
+        vr_ref[0, rows, :] = jnp.broadcast_to(cols[:, 20:21], (LANES, LANES))
+        vr_ref[1, rows, :] = jnp.broadcast_to(cols[:, 21:22], (LANES, LANES))
+        columns[...] = cols
+        index = jnp.zeros((few, LANES), F32)
+        for j in range(8):
+            here = columns[pl.ds(j, few, stride=8), :]
+            index = jnp.where((narrow // 4) % 8 == j, pltpu.roll(here, 4 * j, 1) if j else here, index)
+        idx_ref[pl.ds(b * few, few), :] = index.astype(I32)
+
+
+NSCRATCH = 12
 
 
 def cycle_kernel(
+    groups,
     levels,
     tiles,
     field,
     halo,
-    uw_hbm,
-    vw_hbm,
-    idx_hbm,
-    w_hbm,
-    vr_hbm,
-    front_ref,
-    own_out,
-    rim_out,
-    dep_out,
     uw,
     vw,
-    states,
-    f0,
-    f1,
-    f2,
-    f3,
+    idx_ref,
     w,
     vr,
-    scr,
-    picked,
-    acc,
-    flux,
-    idx,
-    sems,
-    lsems,
+    front_ref,
+    *refs,
 ):
+    own_out, rim_out = refs[: -NSCRATCH]
+    (states, f0, f1, f2, f3, scr, picked, acc, dep_ref, flux, idx, sem) = refs[
+        -NSCRATCH:
+    ]
     forcing = (f0, f1, f2, f3)
     slots = acc.shape[0]
-    per = field.shape[2] // LANES
+    per = tiles // groups
     block = tiles * 16
-    loads = [
-        pltpu.make_async_copy(idx_hbm, idx, sems.at[0]),
-        pltpu.make_async_copy(w_hbm, w, sems.at[1]),
-        pltpu.make_async_copy(vr_hbm, vr, sems.at[2]),
-    ]
-
-    def wind_loads(l):
-        return (
-            pltpu.make_async_copy(uw_hbm.at[l], uw.at[l], lsems.at[0, l]),
-            pltpu.make_async_copy(vw_hbm.at[l], vw.at[l], lsems.at[1, l]),
-        )
-
-    for l in range(levels):
-        for copy in wind_loads(l):
-            copy.start()
-    for copy in loads:
-        copy.start()
+    load = pltpu.make_async_copy(idx_ref, idx, sem)
+    load.start()
 
     lane = lax.broadcasted_iota(I32, (8, LANES), 1)
     first = lane == 0
@@ -212,14 +364,12 @@
     west_of = lambda x: pltpu.roll(x, 1, 1)
 
     def forward(l, carry):
-        for copy in wind_loads(l):
-            copy.wait()
         start = pl.multiple_of(l * block, block)
         for c in range(tiles):
             j, h = divmod(c, per)
-            cols = pl.ds(h * LANES, LANES)
-            scr[pl.ds(c * 16, 8), :] = field[j * levels + l, :, cols]
-            scr[pl.ds(c * 16 + 8, 8), :] = halo[j * levels + l, :, cols] * front_ref[...]
+            at = pl.ds(pl.multiple_of((h * levels + l) * 8, 8), 8)
+            scr[pl.ds(c * 16, 8), :] = field[j, at, :]
+            scr[pl.ds(c * 16 + 8, 8), :] = halo[j, at, :] * front_ref[...]
         for c in range(tiles):
             states[pl.ds(start + c * 16, 8), :] = scr[pl.ds(c * 16, 8, stride=2), :]
             states[pl.ds(start + c * 16 + 8, 8), :] = scr[pl.ds(c * 16 + 1, 8, stride=2), :]
@@ -267,14 +417,13 @@
 
     lax.fori_loop(0, levels, forward, 0)
 
-    for copy in loads:
-        copy.wait()
+    load.wait()
 
     def gather(i, carry):
         base = pl.multiple_of(i * 8, 8)
         for k in range(4):
             for j in range(8):
-                r = idx[k, base + j]
+                r = idx[i, j * 4 + k]
                 picked[pl.ds(k * 8 + j, 1), :] = states[pl.ds(r, 1), :]
         total = w[0, pl.ds(base, 8), :] * picked[pl.ds(0, 8), :]
         for k in range(1, 4):
@@ -285,16 +434,24 @@
     lax.fori_loop(0, slots // 8, gather, 0)
 
     hx = jnp.sum(acc[...], axis=1, keepdims=True)
-    dep_out[...] = vr[1] * (hx - vr[0])
+    dep_ref[...] = vr[1] * (hx - vr[0])
+    tail = pl.ds(per * levels * 8, 8)
+    for b in range(slots // LANES):
+        row = to_row(dep_ref[pl.ds(b * LANES, LANES), :])
+        for h in range(LANES // CAP):
+            own_out[b * (LANES // CAP) + h, tail, 0:CAP] = jnp.broadcast_to(
+                row[:, h * CAP : (h + 1) * CAP], (8, CAP)
+            )
+            own_out[b * (LANES // CAP) + h, tail, CAP:LANES] = jnp.zeros((8, LANES - CAP), F32)
 
     def scatter(i, carry):
         base = pl.multiple_of(i * 8, 8)
-        dep = dep_out[pl.ds(base, 8), :]
+        dep = dep_ref[pl.ds(base, 8), :]
         for k in range(4):
             flux[pl.ds(k * 8, 8), :] = w[k, pl.ds(base, 8), :] * dep
         for j in range(8):
             for k in range(4):
-                r = idx[4 + k, base + j]
+                r = idx[i, 32 + j * 4 + k]
                 at = pl.ds(r, 1)
                 forcing[k][at, :] = forcing[k][at, :] + flux[pl.ds(k * 8 + j, 1), :]
         return carry
@@ -358,9 +515,9 @@
             scr[pl.ds(half + c * 16 + 1, 8, stride=2), :] = odd
         for c in range(tiles):
             j, h = divmod(c, per)
-            cols = pl.ds(h * LANES, LANES)
-            own_out[j * levels + l, :, cols] = scr[pl.ds(half + c * 16, 8), :]
-            rim_out[j * levels + l, :, cols] = scr[pl.ds(half + c * 16 + 8, 8), :]
+            at = pl.ds(pl.multiple_of((h * levels + l) * 8, 8), 8)
+            own_out[j, at, :] = scr[pl.ds(half + c * 16, 8), :]
+            rim_out[j, at, :] = scr[pl.ds(half + c * 16 + 8, 8), :]
         return carry
 
     lax.fori_loop(0, levels, backward, 0)
@@ -379,23 +536,56 @@
     obs_weight,
     obs_rinv,
 ):
-    levels_all = control.shape[0]
-    width = control.shape[2]
+    levels_all, _, width = control.shape
     groups = lax.axis_size("horiz")
     levels, _, lon = wind_lon.shape
     tiles = lon // LANES
     slots = groups * CAP
     count = obs_value.shape[0]
+    halves = width // LANES
+    rows = halves * levels * ROWS
     front, back = halo_masks()
-
-    increment = spread * jnp.einsum(
-        "lm,mrc->lrc",
+    flat = (levels_all * ROWS, width)
+    payload = jax.ShapeDtypeStruct((groups, rows + ROWS, LANES), F32)
+    vmem = lambda *shape: pltpu.VMEM(shape, F32)
+    ivmem = lambda *shape: pltpu.VMEM(shape, I32)
+
+    outgoing, placed = call(
+        functools.partial(start_kernel, groups),
+        (payload, jax.ShapeDtypeStruct((count // LANES, LANES), F32)),
+        [ANY] * 9,
+        (ANY, VM),
+        [
+            vmem(*vert_root.shape),
+            vmem(halves, flat[0], LANES),
+            vmem(halves, flat[0], LANES),
+            ivmem(1, count),
+            ivmem(4, count),
+            ivmem(1, count),
+            vmem(1, count),
+            vmem(4, count),
+            vmem(1, count),
+            vmem(*payload.shape),
+            vmem(FIELDS, count),
+            pltpu.VMEM((count, slots), jnp.bfloat16),
+            pltpu.SemaphoreType.DMA((7,)),
+            pltpu.SemaphoreType.DMA((2, halves)),
+            pltpu.SemaphoreType.DMA((halves,)),
+        ],
+        limit=56,
+        cost=(4e8, 4e6),
+    )(
         vert_root,
-        control,
-        precision=lax.Precision.HIGHEST,
-        preferred_element_type=F32,
+        control.reshape(flat),
+        spread.reshape(flat),
+        obs_dest.reshape(1, count),
+        obs_cells,
+        obs_time[None],
+        obs_value[None],
+        obs_weight,
+        obs_rinv[None],
     )
-    field = lax.all_to_all(increment, "horiz", split_axis=0, concat_axis=0, tiled=True)
+    field = lax.all_to_all(outgoing, "horiz", split_axis=0, concat_axis=0, tiled=True)
 
     ring = jax.ShapeDtypeStruct((levels, tiles * 16, LANES), F32)
     uw, vw = call(
@@ -403,90 +593,85 @@
         (ring, ring),
         [VM] * 5,
         (VM, VM),
-        [pltpu.VMEM((tiles * 16, LANES), F32)],
+        [vmem(tiles * 16, LANES)],
+        limit=14,
         cost=(1e6, 8e6),
     )(wind_lon, exchange(wind_lon, True), wind_lat, exchange(wind_lat, True), front)
-
-    target = obs_dest ^ lax.axis_index("horiz")
-    blank = jnp.zeros((1, count), F32)
-    data = jnp.concatenate(
-        [obs_cells.astype(F32), obs_time[None].astype(F32)]
-        + [blank] * 3
-        + [obs_weight, obs_value[None], obs_rinv[None]]
-        + [blank] * 2,
-        axis=0,
-    )
-    binned, placed = call(
-        functools.partial(bin_kernel, groups),
+    field, uw, vw, front, back = lax.optimization_barrier((field, uw, vw, front, back))
+
+    halo = exchange(field, True)
+    idx, weights, pair = call(
+        functools.partial(prep_kernel, groups, levels, tiles),
         (
-            jax.ShapeDtypeStruct((groups, FIELDS, CAP), F32),
-            jax.ShapeDtypeStruct((count, 1), I32),
-        ),
-        [VM] * 2,
-        (VM, VM),
-        [pltpu.VMEM((count, slots), jnp.bfloat16)],
-        cost=(1e8, 4e6),
-    )(target, data)
-    got = hypercube(binned)
-    idx, weights, pair = call(
-        functools.partial(prep_kernel, levels, tiles),
-        (
-            jax.ShapeDtypeStruct((8, slots), I32),
+            jax.ShapeDtypeStruct((slots // 8, LANES), I32),
             jax.ShapeDtypeStruct((4, slots, LANES), F32),
             jax.ShapeDtypeStruct((2, slots, LANES), F32),
         ),
-        [VM],
-        (VM, VM, VM),
-        [pltpu.VMEM((FIELDS, slots), F32)],
-        cost=(1e6, 6e6),
-    )(got)
-
-    halo = exchange(field, True)
-    block = jax.ShapeDtypeStruct((groups * levels, ROWS, width), F32)
-    forcing = pltpu.VMEM(((NT + 1) * levels * tiles * 8, LANES), F32)
-    adjoint, rim, dep = call(
-        functools.partial(cycle_kernel, levels, tiles),
-        (block, block, jax.ShapeDtypeStruct((slots, LANES), F32)),
-        [VM, VM, ANY, ANY, ANY, ANY, ANY, VM],
+        [ANY],
         (VM, VM, VM),
         [
-            pltpu.VMEM((levels, tiles * 16, LANES), F32),
-            pltpu.VMEM((levels, tiles * 16, LANES), F32),
-            pltpu.VMEM(((NT + 1) * levels * tiles * 16, LANES), F32),
+            vmem(groups, ROWS, LANES),
+            vmem(LANES, slots),
+            vmem(LANES, LANES),
+            pltpu.SemaphoreType.DMA,
+        ],
+        limit=8,
+        cost=(1e6, 6e6),
+    )(field)
+
+    forcing = vmem((NT + 1) * levels * tiles * 8, LANES)
+    adjoint, rim = call(
+        functools.partial(cycle_kernel, groups, levels, tiles),
+        (payload, jax.ShapeDtypeStruct((groups, rows, LANES), F32)),
+        [VM] * 8,
+        (VM, VM),
+        [
+            vmem((NT + 1) * levels * tiles * 16, LANES),
             forcing,
             forcing,
             forcing,
             forcing,
-            pltpu.VMEM((4, slots, LANES), F32),
-            pltpu.VMEM((2, slots, LANES), F32),
-            pltpu.VMEM((2 * tiles * 16, LANES), F32),
-            pltpu.VMEM((32, LANES), F32),
-            pltpu.VMEM((slots, LANES), F32),
-            pltpu.VMEM((32, LANES), F32),
-            pltpu.SMEM((8, slots), I32),
-            pltpu.SemaphoreType.DMA((3,)),
-            pltpu.SemaphoreType.DMA((2, levels)),
+            vmem(2 * tiles * 16, LANES),
+            vmem(32, LANES),
+            vmem(slots, LANES),
+            vmem(slots, LANES),
+            vmem(32, LANES),
+            pltpu.SMEM((slots // 8, LANES), I32),
+            pltpu.SemaphoreType.DMA,
         ],
-        limit=56,
+        limit=34,
         cost=(1e8, 16e6),
     )(field, halo, uw, vw, idx, weights, pair, front)
 
-    total = adjoint + exchange(rim, False) * back[:, :1][None]
+    part = groups // 4
+    total = call(
+        rim_kernel,
+        payload,
+        [
+            pl.BlockSpec((part, rows + ROWS, LANES), lambda i: (i, 0, 0)),
+            pl.BlockSpec((part, rows, LANES), lambda i: (i, 0, 0)),
+            pl.BlockSpec((ROWS, LANES), lambda i: (0, 0)),
+        ],
+        pl.BlockSpec((part, rows + ROWS, LANES), lambda i: (i, 0, 0)),
+        limit=8,
+        cost=(1e6, 3e6),
+        grid=(4,),
+    )(adjoint, exchange(rim, False), back)
     column = lax.all_to_all(total, "horiz", split_axis=0, concat_axis=0, tiled=True)
 
-    back_home = hypercube(dep[:, 0].reshape(groups, CAP)).reshape(1, slots)
-    departure = jnp.sum(
-        jnp.where(placed == jnp.arange(slots, dtype=I32)[None, :], back_home, 0.0), axis=1
-    )
-
-    gradient = control + jnp.einsum(
-        "lm,lrc->mrc",
-        vert_root,
-        spread * column,
-        precision=lax.Precision.HIGHEST,
-        preferred_element_type=F32,
-    )
-    return (gradient, departure)
+    gradient, departure = call(
+        functools.partial(end_kernel, groups),
+        (
+            jax.ShapeDtypeStruct(flat, F32),
+            jax.ShapeDtypeStruct((count // LANES, LANES), F32),
+        ),
+        [VM] * 5,
+        (ANY, VM),
+        [vmem(halves, flat[0], LANES)] * 3 + [vmem(8, slots), pltpu.SemaphoreType.DMA((halves,))],
+        limit=14,
+        cost=(4e8, 4e6),
+    )(vert_root.T, control.reshape(flat), spread.reshape(flat), column, placed)
+    return (gradient.reshape(control.shape), departure.reshape(count))
 
 
 def solution(mesh):

time: 135 us -> 111 us (0.82)
  starting transfers between devices: 30.8 us -> 15.3 us
  other arithmetic: 7.02 us -> 0.01 us
  local copies, waits for them, and re-layouts: 9.03 us -> 5.61 us
  matrix products: 2.93 us -> 0 us
  Pallas kernels: 37.9 us -> 40.7 us
  waiting for transfers between devices: 46.1 us -> 48 us
    ppermute x8 -> x0, waiting for transfers between devices: 27.2 us -> none  [hypercube(): got = lax.ppermute(view[:, 1], 'horiz', pairs)]
    all_to_all x1, waiting for transfers between devices: 0.01 us -> 25.8 us  [per_device(): lax.all_to_all(total, 'horiz', split_axis=0, concat_axis=0, tiled=True)]
    ppermute x8 -> x0, starting transfers between devices: 17.1 us -> none  [hypercube(): got = lax.ppermute(view[:, 1], 'horiz', pairs)]
    ppermute x4, waiting for transfers between devices: 2.85 us -> 6.87 us  [exchange(): return lax.ppermute(tile_rows, 'obs', [(0, 1), (1, 0)])]
    mul x2 -> x0, other arithmetic: 2.97 us -> none  [the longest x1 1.61 us: per_device(): spread * jnp.einsum('lm,mrc->lrc', vert_root, control, precision=lax.Prec...]
    unnamed x47 -> x21, local copies, waits for them, and re-layouts: 8.44 us -> 5.47 us
    dot_general x2 -> x0, matrix products: 2.93 us -> none  [the longest x1 1.91 us: per_device(): jnp.einsum('lm,lrc->mrc', vert_root, spread * column, precision=lax.Preci...]
    pallas_call x3 -> x5, Pallas kernels: 36.1 us -> 38.6 us  [the longest x1 27 us: per_device(): call(functools.partial(cycle_kernel, groups, levels, tiles), (payload, ja...]
  transfers between devices with their start and end apart: 14 -> 6, of which waited for: 9 -> 6; matrix products, arithmetic and copies ran while one was open for 2% -> 0% of each run, Pallas kernels for 4% -> 4%
where the time goes in v1:
time: 111 us; the launch traced here: 110 us
  waiting for transfers between devices  48 us (43%)
  Pallas kernels  40.7 us (37%)
  starting transfers between devices  15.3 us (14%)
  local copies, waits for them, and re-layouts  5.61 us (5%)
    pallas_call x1, Pallas kernels, per_device(): call(functools.partial(cycle_kernel, groups, levels, tiles), (payload, ja...  27 us
    all_to_all x1, waiting for transfers between devices, per_device(): lax.all_to_all(total, 'horiz', split_axis=0, concat_axis=0, tiled=True)  25.8 us
    all_to_all x1, waiting for transfers between devices, per_device(): lax.all_to_all(outgoing, 'horiz', split_axis=0, concat_axis=0, tiled=True)  15.4 us
    all_to_all x1, starting transfers between devices, per_device(): lax.all_to_all(outgoing, 'horiz', split_axis=0, concat_axis=0, tiled=True)  8.46 us
    ppermute x4, waiting for transfers between devices, exchange(): return lax.ppermute(tile_rows, 'obs', [(0, 1), (1, 0)])  6.87 us
    all_to_all x1, starting transfers between devices, per_device(): lax.all_to_all(total, 'horiz', split_axis=0, concat_axis=0, tiled=True)  6.07 us
    unnamed x21, local copies, waits for them, and re-layouts  5.47 us
    pallas_call x1, Pallas kernels, per_device(): call(functools.partial(start_kernel, groups), (payload, jax.ShapeDtypeStr...  4.98 us
  transfers between devices with their start and end apart: 6, of which 6 were waited for; matrix products, arithmetic and copies ran while one was open for 0% of the time, Pallas kernels for 4%

profile of v1, /device:TPU:0, one launch (start us, length us, event | category | flops | bytes accessed | tf_op | source)
XLA Modules:
  0.0 110.4 jit_solution(9328819140486117980)
XLA Ops:
  0.6 5.0 %shard_map.122 = (f32[16,136,128]{2,1,0:T(8,128)}, f32[8,128]{1,0:T(8,128)}) custom-call(f32[128,128]{1,0:T(8,128)} %root_hbm.1, f32[1024,256]{1,0:T(8,128)} %bitcast.9, f32[1024,256]{1,0:T(8,128)} %bitcast.11, s32[1,1024]{1,0:T(1,128)} %bitcast.14, s32[4,1024]{1,0:T(4,128)} %cells_hbm.1, s32[1,1024]{1,0:T(1,128)} %bitcast.15, f32[1,1024]{1,0:T(1,128)} %bitcast.16, ...), custom_call_target="tpu_custom_call" | custom-call | flops 400000000 | bytes 4000000 | tf_op jit(solution)/shard_map/pallas_call | solution.py:553
  5.6 8.5 %all-to-all-start = ((f32[16,136,128]{2,1,0:T(8,128)}), f32[16,136,128]{2,1,0:T(8,128)S(1)}, u32[]{:S(2)}, u32[]{:S(2)}) async-start(f32[16,136,128]{2,1,0:T(8,128)} %get-tuple-element.18), calls=%async_computation | async-start | bytes 2228224 | tf_op jit(solution)/shard_map/all_to_all | solution.py:588
  14.1 0.1 collective-permute-start
  14.2 0.5 collective-permute-start.1
  14.7 2.3 %collective-permute-done.uh_ref = f32[8,8,4096]{2,1,0:T(8,128)} collective-permute-done((f32[8,8,4096]{2,1,0:T(8,128)S(1)}, f32[8,8,4096]{2,1,0:T(8,128)}, u32[]{:S(2)}, u32[]{:S(2)}) %collective-permute-start) | collective-permute-done | bytes 1048608 | tf_op jit(solution)/shard_map/ppermute | solution.py:192
  17.0 1.5 %collective-permute-done.1.vh_ref = f32[8,8,4096]{2,1,0:T(8,128)} collective-permute-done((f32[8,8,4096]{2,1,0:T(8,128)S(1)}, f32[8,8,4096]{2,1,0:T(8,128)}, u32[]{:S(2)}, u32[]{:S(2)}) %collective-permute-start.1) | collective-permute-done | bytes 1048608 | tf_op jit(solution)/shard_map/ppermute | solution.py:192
  18.5 0.1 broadcast_in_dim.23.mask_ref.front_ref
  18.5 1.2 %copy-done.5 = f32[8,8,4096]{2,1,0:T(8,128)S(1)} copy-done((f32[8,8,4096]{2,1,0:T(8,128)S(1)}, f32[8,8,4096]{2,1,0:T(8,128)}, u32[]{:S(2)}) %copy-start.5) | copy-done | bytes 1048600
  19.8 1.2 %copy-done.7 = f32[8,8,4096]{2,1,0:T(8,128)S(1)} copy-done((f32[8,8,4096]{2,1,0:T(8,128)S(1)}, f32[8,8,4096]{2,1,0:T(8,128)}, u32[]{:S(2)}) %copy-start.7) | copy-done | bytes 1048600
  21.0 2.1 %shard_map.123 = (f32[8,512,128]{2,1,0:T(8,128)S(1)}, f32[8,512,128]{2,1,0:T(8,128)S(1)}) custom-call(f32[8,8,4096]{2,1,0:T(8,128)S(1)} %copy-done.5, f32[8,8,4096]{2,1,0:T(8,128)} %collective-permute-done.uh_ref, f32[8,8,4096]{2,1,0:T(8,128)S(1)} %copy-done.7, f32[8,8,4096]{2,1,0:T(8,128)} %collective-permute-done.1.vh_ref, ...), custom_call_target="tpu_custom_call" | custom-call | flops 1000000 | bytes 8000000 | tf_op jit(solution)/shard_map/pallas_call | solution.py:591
  23.1 1.3 %copy-done.2 = f32[8,512,128]{2,1,0:T(8,128)} copy-done((f32[8,512,128]{2,1,0:T(8,128)}, f32[8,512,128]{2,1,0:T(8,128)S(1)}, u32[]{:S(2)}) %copy-start.2) | copy-done | bytes 2097176
  24.4 15.4 %all-to-all-done.got_hbm.field = f32[16,136,128]{2,1,0:T(8,128)S(1)} async-done(((f32[16,136,128]{2,1,0:T(8,128)}), f32[16,136,128]{2,1,0:T(8,128)S(1)}, u32[]{:S(2)}, u32[]{:S(2)}) %all-to-all-start) | async-done | bytes 1114144 | tf_op jit(solution)/shard_map/all_to_all | solution.py:588
  39.8 0.1 broadcast_in_dim.24.mask_ref
  39.9 2.2 %shard_map.124 = (s32[128,128]{1,0:T(8,128)S(1)}, f32[4,1024,128]{2,1,0:T(8,128)S(1)}, f32[2,1024,128]{2,1,0:T(8,128)S(1)}) custom-call(f32[16,136,128]{2,1,0:T(8,128)S(1)} %all-to-all-done.got_hbm.field), custom_call_target="tpu_custom_call" | custom-call | flops 1000000 | bytes 6000000 | tf_op jit(solution)/shard_map/pallas_call | solution.py:603
  42.1 0.6 collective-permute-done.2.halo
  42.7 1.6 %copy-done.3 = f32[8,512,128]{2,1,0:T(8,128)S(1)} copy-done((f32[8,512,128]{2,1,0:T(8,128)S(1)}, f32[8,512,128]{2,1,0:T(8,128)}, u32[]{:S(2)}) %copy-start.3) | copy-done | bytes 2097176
  44.3 27.0 %shard_map.125 = (f32[16,136,128]{2,1,0:T(8,128)S(1)}, f32[16,128,128]{2,1,0:T(8,128)S(1)}) custom-call(f32[16,136,128]{2,1,0:T(8,128)S(1)} %all-to-all-done.got_hbm.field, f32[16,136,128]{2,1,0:T(8,128)S(1)} %collective-permute-done.2.halo, f32[8,512,128]{2,1,0:T(8,128)S(1)} %get-tuple-element.22.uw, f32[8,512,128]{2,1,0:T(8,128)S(1)} %copy-done.3, ...), custom_call_target="tpu_custom_call" | custom-call | flops 100000000 | bytes 16000000 | tf_op jit(solution)/shard_map/pallas_call | solution.py:623
  71.3 0.2 collective-permute-start.3
  71.5 2.5 %collective-permute-done.3.rim_ref = f32[16,128,128]{2,1,0:T(8,128)S(1)} collective-permute-done((f32[16,128,128]{2,1,0:T(8,128)S(1)}, f32[16,128,128]{2,1,0:T(8,128)S(1)}, u32[]{:S(2)}, u32[]{:S(2)}) %collective-permute-start.3) | collective-permute-done | bytes 1048608 | tf_op jit(solution)/shard_map/ppermute | solution.py:192
  74.0 1.6 %shard_map.126 = f32[16,136,128]{2,1,0:T(8,128)} custom-call(f32[16,136,128]{2,1,0:T(8,128)S(1)} %get-tuple-element.28.own_ref, f32[16,128,128]{2,1,0:T(8,128)S(1)} %collective-permute-done.3.rim_ref, f32[8,128]{1,0:T(8,128)S(1)} %broadcast_in_dim.24.mask_ref), custom_call_target="tpu_custom_call" | custom-call | flops 1000000 | bytes 3000000 | tf_op jit(solution)/shard_map/pallas_call | solution.py:647
  75.6 6.1 %all-to-all-start.1 = ((f32[16,136,128]{2,1,0:T(8,128)}), f32[16,136,128]{2,1,0:T(8,128)S(1)}, u32[]{:S(2)}, u32[]{:S(2)}) async-start(f32[16,136,128]{2,1,0:T(8,128)} %shard_map.126), calls=%async_computation.1 | async-start | bytes 2228224 | tf_op jit(solution)/shard_map/all_to_all | solution.py:660
  81.7 0.1 copy.13
  81.8 25.8 %all-to-all-done.1.got_ref = f32[16,136,128]{2,1,0:T(8,128)S(1)} async-done(((f32[16,136,128]{2,1,0:T(8,128)}), f32[16,136,128]{2,1,0:T(8,128)S(1)}, u32[]{:S(2)}, u32[]{:S(2)}) %all-to-all-start.1) | async-done | bytes 1114144 | tf_op jit(solution)/shard_map/all_to_all | solution.py:660
  107.6 2.8 %shard_map.127 = (f32[1024,256]{1,0:T(8,128)}, f32[8,128]{1,0:T(8,128)}) custom-call(f32[128,128]{1,0:T(8,128)S(1)} %bitcast.13, f32[1024,256]{1,0:T(8,128)S(1)} %bitcast.10, f32[1024,256]{1,0:T(8,128)S(1)} %bitcast.12, f32[16,136,128]{2,1,0:T(8,128)S(1)} %all-to-all-done.1.got_ref, f32[8,128]{1,0:T(8,128)S(1)} %copy-done.8), custom_call_target="tpu_custom_call" | custom-call | flops 400000000 | bytes 4000000 | tf_op jit(solution)/shard_map/pallas_call | solution.py:662
  (18 shorter events, 0.0 us)
Async XLA Ops:
  5.6 8.5 %copy-start.4 = (f32[8,8,4096]{2,1,0:T(8,128)S(1)}, f32[8,8,4096]{2,1,0:T(8,128)}, u32[]{:S(2)}) copy-start(f32[8,8,4096]{2,1,0:T(8,128)} %u_ref.1) | copy-start | bytes 3145732
  5.6 8.6 %copy-start.6 = (f32[8,8,4096]{2,1,0:T(8,128)S(1)}, f32[8,8,4096]{2,1,0:T(8,128)}, u32[]{:S(2)}) copy-start(f32[8,8,4096]{2,1,0:T(8,128)} %v_ref.1) | copy-start | bytes 3145732
  5.6 34.2 %all-to-all-start = ((f32[16,136,128]{2,1,0:T(8,128)}), f32[16,136,128]{2,1,0:T(8,128)S(1)}, u32[]{:S(2)}, u32[]{:S(2)}) async-start(f32[16,136,128]{2,1,0:T(8,128)} %get-tuple-element.18), calls=%async_computation | async-start | bytes 2228224 | tf_op jit(solution)/shard_map/all_to_all | solution.py:588
  14.1 2.9 %collective-permute-start = (f32[8,8,4096]{2,1,0:T(8,128)S(1)}, f32[8,8,4096]{2,1,0:T(8,128)}, u32[]{:S(2)}, u32[]{:S(2)}) collective-permute-start(f32[8,8,4096]{2,1,0:T(8,128)S(1)} %copy-done.4), channel_id=1, source_target_pairs={{0,16},{16,0},{1,17},{17,1},{2,18},{18,2},{3,19},{19,3},{4,20},{20... | collective-permute-start | bytes 3145736 | tf_op jit(solution)/shard_map/ppermute | solution.py:192
  14.2 4.3 %collective-permute-start.1 = (f32[8,8,4096]{2,1,0:T(8,128)S(1)}, f32[8,8,4096]{2,1,0:T(8,128)}, u32[]{:S(2)}, u32[]{:S(2)}) collective-permute-start(f32[8,8,4096]{2,1,0:T(8,128)S(1)} %copy-done.6), channel_id=1, source_target_pairs={{0,16},{16,0},{1,17},{17,1},{2,18},{18,2},{3,19},{19,3},{4,20},{20... | collective-permute-start | bytes 3145736 | tf_op jit(solution)/shard_map/ppermute | solution.py:192
  18.5 1.2 %copy-start.5 = (f32[8,8,4096]{2,1,0:T(8,128)S(1)}, f32[8,8,4096]{2,1,0:T(8,128)}, u32[]{:S(2)}) copy-start(f32[8,8,4096]{2,1,0:T(8,128)} %u_ref.1) | copy-start | bytes 3145732
  19.8 1.2 %copy-start.7 = (f32[8,8,4096]{2,1,0:T(8,128)S(1)}, f32[8,8,4096]{2,1,0:T(8,128)}, u32[]{:S(2)}) copy-start(f32[8,8,4096]{2,1,0:T(8,128)} %v_ref.1) | copy-start | bytes 3145732
  23.1 1.3 %copy-start.2 = (f32[8,512,128]{2,1,0:T(8,128)}, f32[8,512,128]{2,1,0:T(8,128)S(1)}, u32[]{:S(2)}) copy-start(f32[8,512,128]{2,1,0:T(8,128)S(1)} %get-tuple-element.23.vw) | copy-start | bytes 6291460
  39.9 2.8 %collective-permute-start.2 = (f32[16,136,128]{2,1,0:T(8,128)S(1)}, f32[16,136,128]{2,1,0:T(8,128)S(1)}, u32[]{:S(2)}, u32[]{:S(2)}) collective-permute-start(f32[16,136,128]{2,1,0:T(8,128)S(1)} %all-to-all-done.got_hbm.field), channel_id=1, source_target_pairs={{0,16},{16,0},{1,17},{17,1},{2,18},{18,2},{3,19},{19,3},{4,20},{20... | collective-permute-start | bytes 3342344 | tf_op jit(solution)/shard_map/ppermute | solution.py:192
  42.7 1.6 %copy-start.3 = (f32[8,512,128]{2,1,0:T(8,128)S(1)}, f32[8,512,128]{2,1,0:T(8,128)}, u32[]{:S(2)}) copy-start(f32[8,512,128]{2,1,0:T(8,128)} %copy-done.2) | copy-start | bytes 6291460
  71.3 2.7 %collective-permute-start.3 = (f32[16,128,128]{2,1,0:T(8,128)S(1)}, f32[16,128,128]{2,1,0:T(8,128)S(1)}, u32[]{:S(2)}, u32[]{:S(2)}) collective-permute-start(f32[16,128,128]{2,1,0:T(8,128)S(1)} %get-tuple-element.29), channel_id=1, source_target_pairs={{0,16},{16,0},{1,17},{17,1},{2,18},{18,2},{3,19},{19,3},{4,20},{20... | collective-permute-start | bytes 3145736 | tf_op jit(solution)/shard_map/ppermute | solution.py:192
  75.6 6.1 %copy-start.9 = (f32[128,128]{1,0:T(8,128)S(1)}, f32[128,128]{1,0:T(8,128)}, u32[]{:S(2)}) copy-start(f32[128,128]{1,0:T(8,128)} %root_hbm.1) | copy-start | bytes 196612
  75.6 32.0 %copy-start = (f32[128,8,256]{2,1,0:T(8,128)S(1)}, f32[128,8,256]{2,1,0:T(8,128)}, u32[]{:S(2)}) copy-start(f32[128,8,256]{2,1,0:T(8,128)} %param.11) | copy-start | bytes 3145732
  75.6 32.0 %copy-start.1 = (f32[128,8,256]{2,1,0:T(8,128)S(1)}, f32[128,8,256]{2,1,0:T(8,128)}, u32[]{:S(2)}) copy-start(f32[128,8,256]{2,1,0:T(8,128)} %param.12) | copy-start | bytes 3145732
  75.6 32.0 %copy-start.8 = (f32[8,128]{1,0:T(8,128)S(1)}, f32[8,128]{1,0:T(8,128)}, u32[]{:S(2)}) copy-start(f32[8,128]{1,0:T(8,128)} %get-tuple-element.31.placed_ref) | copy-start | bytes 12292
  75.6 31.9 %all-to-all-start.1 = ((f32[16,136,128]{2,1,0:T(8,128)}), f32[16,136,128]{2,1,0:T(8,128)S(1)}, u32[]{:S(2)}, u32[]{:S(2)}) async-start(f32[16,136,128]{2,1,0:T(8,128)} %shard_map.126), calls=%async_computation.1 | async-start | bytes 2228224 | tf_op jit(solution)/shard_map/all_to_all | solution.py:660

commit v2 on v1

--- a/solution.py
+++ b/solution.py
@@ -118,21 +118,30 @@
     wide = wide_root(root[...])
     block = levels * ROWS
     outs = []
+    pairs = halves % 2 == 0
     for h in range(halves):
         parts[h][0].wait()
-        results = [apply_root(wide, control[h, level_rows(r, levels_all), :]) for r in range(ROWS)]
+    for h in range(halves):
         parts[h][1].wait()
+    for m in range(0, halves, 2 if pairs else 1):
         for r in range(ROWS):
-            value_r = spread[h, level_rows(r, levels_all), :] * results[r]
-            for g in range(groups):
-                out[g, pl.ds(h * block + r, levels, stride=ROWS), :] = value_r[
-                    g * levels : (g + 1) * levels
-                ]
-        rows = pl.ds(h * block, block + (ROWS if h == halves - 1 else 0))
-        outs.append(
-            pltpu.make_async_copy(out.at[:, rows, :], out_hbm.at[:, rows, :], out_sems.at[h])
-        )
-        outs[-1].start()
+            at = level_rows(r, levels_all)
+            if pairs:
+                both = apply_root(
+                    wide, jnp.concatenate([control[m, at, :], control[m + 1, at, :]], axis=1)
+                )
+                both = both * jnp.concatenate([spread[m, at, :], spread[m + 1, at, :]], axis=1)
+                both = reorder(both, even_odd(), split2)
+                values = [both[:, 0:LANES], both[:, LANES:]]
+            else:
+                values = [spread[m, at, :] * apply_root(wide, control[m, at, :])]
+            for i, value_r in enumerate(values):
+                for g in range(groups):
+                    out[g, pl.ds((m + i) * block + r, levels, stride=ROWS), :] = value_r[
+                        g * levels : (g + 1) * levels
+                    ]
+    outs.append(pltpu.make_async_copy(out, out_hbm, out_sems.at[0]))
+    outs[-1].start()
     for copy in outs:
         copy.wait()
 
@@ -144,22 +153,38 @@
     block = levels * ROWS
     wide = wide_root(root_ref[...])
     outs = []
+    pairs = halves % 2 == 0
     for h in range(halves):
         cols = pl.ds(h * LANES, LANES)
         control[h] = control_ref[:, cols]
         spread[h] = spread_ref[:, cols]
+    for m in range(0, halves, 2 if pairs else 1):
         for r in range(ROWS):
             at = level_rows(r, levels_all)
-            adjoint = jnp.concatenate(
-                [
-                    got_ref[g, pl.ds(h * block + r, levels, stride=ROWS), :]
-                    for g in range(groups)
-                ],
-                axis=0,
-            )
-            out[h, at, :] = control[h, at, :] + apply_root(wide, spread[h, at, :] * adjoint)
-        outs.append(pltpu.make_async_copy(out.at[h], out_hbm.at[:, cols], sems.at[h]))
-        outs[-1].start()
+            half = [
+                jnp.concatenate(
+                    [
+                        got_ref[g, pl.ds(h * block + r, levels, stride=ROWS), :]
+                        for g in range(groups)
+                    ],
+                    axis=0,
+                )
+                for h in range(m, m + (2 if pairs else 1))
+            ]
+            if pairs:
+                adjoint = reorder(jnp.concatenate(half, axis=1), even_odd(back=True), split2)
+                both = apply_root(
+                    wide, jnp.concatenate([spread[m, at, :], spread[m + 1, at, :]], axis=1) * adjoint
+                )
+                values = [both[:, 0:LANES], both[:, LANES:]]
+            else:
+                values = [apply_root(wide, spread[m, at, :] * half[0])]
+            for i, value in enumerate(values):
+                out[m + i, at, :] = control[m + i, at, :] + value
+        for h in range(m, m + (2 if pairs else 1)):
+            cols = pl.ds(h * LANES, LANES)
+            outs.append(pltpu.make_async_copy(out.at[h], out_hbm.at[:, cols], sems.at[h]))
+            outs[-1].start()
     for r in range(groups):
         row[0:1, r * CAP : (r + 1) * CAP] = got_ref[r, pl.ds(halves * block, 1), 0:CAP]
     lane = lax.broadcasted_iota(I32, (LANES, LANES), 1)
@@ -186,6 +211,48 @@
     out_ref[:, rest, :] = own_ref[:, rest, :]
 
 
+def even_odd(back=False):
+    row = lax.broadcasted_iota(I32, (2 * LANES, 2 * LANES), 0)
+    col = lax.broadcasted_iota(I32, (2 * LANES, 2 * LANES), 1)
+    if back:
+        row, col = col, row
+    return jnp.where(row == 2 * (col % LANES) + col // LANES, 1.0, 0.0).astype(jnp.bfloat16)
+
+
+def reorder(x, order, split):
+    parts = split(x)
+    count = x.shape[0]
+    got = jnp.dot(jnp.concatenate(parts, axis=0), order, preferred_element_type=F32)
+    total = got[0:count]
+    for i in range(1, len(parts)):
+        total = total + got[i * count : (i + 1) * count]
+    return total
+
+
+def neighbours(value, pairs, first, last):
+    made = {}
+
+    def rolled(c, side, amount):
+        key = (c, side, amount)
+        if key not in made:
+            made[key] = pltpu.roll(value(c, side), amount, 1)
+        return made[key]
+
+    def east(c, side):
+        if pairs and c % 2 == 0:
+            return value(c + 1, side)
+        same, after = (c - 1, c + 1) if pairs else (c, c + 1)
+        return jnp.where(last, rolled(after, side, LANES - 1), rolled(same, side, LANES - 1))
+
+    def west(c, side):
+        if pairs and c % 2:
+            return value(c - 1, side)
+        same, before = (c + 1, c - 1) if pairs else (c, c - 1)
+        return jnp.where(first, rolled(before, side, 1), rolled(same, side, 1))
+
+    return east, west
+
+
 def exchange(tile_rows, toward):
     count = lax.axis_size("obs")
     if count == 2:
@@ -208,15 +275,21 @@
     return wide(front), wide(back)
 
 
-def wind_kernel(tiles, u_ref, uh_ref, v_ref, vh_ref, mask_ref, uo_ref, vo_ref, scr):
+def wind_kernel(tiles, pairs, u_ref, uh_ref, v_ref, vh_ref, mask_ref, uo_ref, vo_ref, scr):
     levels = u_ref.shape[0]
 
     def level(l, carry):
         for src, rim, dst in ((u_ref, uh_ref, uo_ref), (v_ref, vh_ref, vo_ref)):
-            for c in range(tiles):
-                cols = pl.ds(c * LANES, LANES)
-                scr[pl.ds(c * 16, 8), :] = src[l, :, cols]
-                scr[pl.ds(c * 16 + 8, 8), :] = rim[l, :, cols] * mask_ref[...]
+            step = 2 if pairs else 1
+            for c in range(0, tiles, step):
+                cols = pl.ds(c * LANES, step * LANES)
+                both = jnp.concatenate([src[l, :, cols], rim[l, :, cols]], axis=0)
+                if pairs:
+                    both = reorder(both, even_odd(), split3)
+                for i in range(step):
+                    lanes = slice(i * LANES, (i + 1) * LANES)
+                    scr[pl.ds((c + i) * 16, 8), :] = both[0:8, lanes]
+                    scr[pl.ds((c + i) * 16 + 8, 8), :] = both[8:16, lanes] * mask_ref[...]
             for c in range(tiles):
                 dst[l, pl.ds(c * 16, 8), :] = scr[pl.ds(c * 16, 8, stride=2), :]
                 dst[l, pl.ds(c * 16 + 8, 8), :] = scr[pl.ds(c * 16 + 1, 8, stride=2), :]
@@ -286,7 +359,7 @@
         out[g, pl.ds(last, ROWS), CAP : 2 * CAP] = part[ROWS:FIELDS]
 
 
-def prep_kernel(groups, levels, tiles, got_hbm, idx_ref, w_ref, vr_ref, got, scr, columns, sem):
+def prep_kernel(groups, levels, tiles, pairs, got_hbm, idx_ref, w_ref, vr_ref, got, scr, columns, sem):
     last = got_hbm.shape[1] - ROWS
     load = pltpu.make_async_copy(got_hbm.at[:, pl.ds(last, ROWS), :], got, sem)
     load.start()
@@ -301,9 +374,13 @@
         lev = cell // (ROWS * lon)
         row = (cell // lon) % ROWS
         col = cell % lon
-        tile = (time * levels + lev) * tiles + col // LANES
+        if pairs:
+            side, lane_at = col // (2 * LANES) * 2 + col % 2, col % (2 * LANES) // 2
+        else:
+            side, lane_at = col // LANES, col % LANES
+        tile = (time * levels + lev) * tiles + side
         scr[0:4, part] = (tile * 16 + (row % 2) * 8 + row // 2).astype(F32)
-        scr[8:12, part] = (col % LANES).astype(F32)
+        scr[8:12, part] = lane_at.astype(F32)
         scr[16:24, part] = got[g, :, CAP : 2 * CAP]
         scr[32:36, part] = (tile * 8 + (row % 2) * 4 + row // 2).astype(F32)
     slots = groups * CAP
@@ -326,7 +403,7 @@
         idx_ref[pl.ds(b * few, few), :] = index.astype(I32)
 
 
-NSCRATCH = 12
+NSCRATCH = 13
 
 
 def cycle_kernel(
@@ -335,8 +412,8 @@
     tiles,
     field,
     halo,
-    uw,
-    vw,
+    uw_hbm,
+    vw_hbm,
     idx_ref,
     w,
     vr,
@@ -344,13 +421,23 @@
     *refs,
 ):
     own_out, rim_out = refs[: -NSCRATCH]
-    (states, f0, f1, f2, f3, scr, picked, acc, dep_ref, flux, idx, sem) = refs[
+    (uw, vw, states, f0, f1, f2, f3, scr, acc, dep_ref, idx, sem, lsems) = refs[
         -NSCRATCH:
     ]
     forcing = (f0, f1, f2, f3)
     slots = acc.shape[0]
     per = tiles // groups
+    pairs = per % 2 == 0
     block = tiles * 16
+    def wind_loads(l):
+        return (
+            pltpu.make_async_copy(uw_hbm.at[l], uw.at[l], lsems.at[0, l]),
+            pltpu.make_async_copy(vw_hbm.at[l], vw.at[l], lsems.at[1, l]),
+        )
+
+    for l in range(levels):
+        for copy in wind_loads(l):
+            copy.start()
     load = pltpu.make_async_copy(idx_ref, idx, sem)
     load.start()
 
@@ -360,10 +447,10 @@
     sub = lax.broadcasted_iota(I32, (8, LANES), 0)
     own = sub < 4
     zero = jnp.zeros((8, LANES), F32)
-    east_of = lambda x: pltpu.roll(x, LANES - 1, 1)
-    west_of = lambda x: pltpu.roll(x, 1, 1)
 
     def forward(l, carry):
+        for copy in wind_loads(l):
+            copy.wait()
         start = pl.multiple_of(l * block, block)
         for c in range(tiles):
             j, h = divmod(c, per)
@@ -379,30 +466,24 @@
             src = pl.multiple_of(start + t * levels * block, block)
             dst = pl.multiple_of(start + (t + 1) * levels * block, block)
 
-            def tile(c):
-                c = c % tiles
-                return (
-                    states[pl.ds(src + c * 16, 8), :],
-                    states[pl.ds(src + c * 16 + 8, 8), :],
-                )
-
-            q_w, q, q_e = tile(-1), tile(0), tile(1)
-            w_w = [west_of(x) for x in q_w]
-            w_c = [west_of(x) for x in q]
-            e_c = [east_of(x) for x in q]
+            held = {}
+
+            def tile(c, side):
+                if (c, side) not in held:
+                    held[c, side] = states[pl.ds(src + c % tiles * 16 + side * 8, 8), :]
+                return held[c, side]
+
+            east, west = neighbours(tile, pairs, first, last)
             for c in range(tiles):
-                e_e = [east_of(x) for x in q_e]
-                even, odd = q
+                even, odd = tile(c, 0), tile(c, 1)
                 souths = (pltpu.roll(odd, 1, 0), even)
                 norths = (odd, pltpu.roll(even, 7, 0))
                 for side in range(2):
-                    here = q[side]
+                    here = tile(c, side)
                     at = pl.ds(c * 16 + side * 8, 8)
                     u = uw[l, at, :]
                     v = vw[l, at, :]
-                    west = jnp.where(first, w_w[side], w_c[side])
-                    east = jnp.where(last, e_e[side], e_c[side])
-                    lon = jnp.where(u > 0, west, east)
+                    lon = jnp.where(u > 0, west(c, side), east(c, side))
                     lat = jnp.where(v > 0, souths[side], norths[side])
                     states[pl.ds(dst + c * 16 + side * 8, 8), :] = (
                         here + jnp.abs(u) * (lon - here) + jnp.abs(v) * (lat - here)
@@ -411,8 +492,6 @@
                     f[pl.ds(pl.multiple_of(fstart + t * fstep, 8) + c * 8, 8), :] = zero
                     if t == NT - 1:
                         f[pl.ds(pl.multiple_of(fstart + NT * fstep, 8) + c * 8, 8), :] = zero
-                w_w, w_c, e_c = w_c, [west_of(x) for x in q_e], e_e
-                q, q_e = q_e, tile(c + 2)
         return carry
 
     lax.fori_loop(0, levels, forward, 0)
@@ -421,17 +500,15 @@
 
     def gather(i, carry):
         base = pl.multiple_of(i * 8, 8)
-        for k in range(4):
-            for j in range(8):
-                r = idx[i, j * 4 + k]
-                picked[pl.ds(k * 8 + j, 1), :] = states[pl.ds(r, 1), :]
-        total = w[0, pl.ds(base, 8), :] * picked[pl.ds(0, 8), :]
-        for k in range(1, 4):
-            total = total + w[k, pl.ds(base, 8), :] * picked[pl.ds(k * 8, 8), :]
-        acc[pl.ds(base, 8), :] = total
+        for j in range(8):
+            total = None
+            for k in range(4):
+                term = w[k, pl.ds(base + j, 1), :] * states[pl.ds(idx[i, j * 4 + k], 1), :]
+                total = term if total is None else total + term
+            acc[pl.ds(base + j, 1), :] = total
         return carry
 
-    lax.fori_loop(0, slots // 8, gather, 0)
+    lax.fori_loop(0, slots // 8, gather, 0, unroll=4)
 
     hx = jnp.sum(acc[...], axis=1, keepdims=True)
     dep_ref[...] = vr[1] * (hx - vr[0])
@@ -446,17 +523,14 @@
 
     def scatter(i, carry):
         base = pl.multiple_of(i * 8, 8)
-        dep = dep_ref[pl.ds(base, 8), :]
-        for k in range(4):
-            flux[pl.ds(k * 8, 8), :] = w[k, pl.ds(base, 8), :] * dep
         for j in range(8):
+            dep = dep_ref[pl.ds(base + j, 1), :]
             for k in range(4):
-                r = idx[i, 32 + j * 4 + k]
-                at = pl.ds(r, 1)
-                forcing[k][at, :] = forcing[k][at, :] + flux[pl.ds(k * 8 + j, 1), :]
+                at = pl.ds(idx[i, 32 + j * 4 + k], 1)
+                forcing[k][at, :] = forcing[k][at, :] + w[k, pl.ds(base + j, 1), :] * dep
         return carry
 
-    lax.fori_loop(0, slots // 8, scatter, 0)
+    lax.fori_loop(0, slots // 8, scatter, 0, unroll=2)
 
     def backward(l, carry):
         fstart = pl.multiple_of(l * tiles * 8, tiles * 8)
@@ -467,20 +541,23 @@
             total = (f0[at, :] + f1[at, :]) + (f2[at, :] + f3[at, :])
             return (jnp.where(own, total, 0.0), jnp.where(own, pltpu.roll(total, 4, 0), 0.0))
 
-        def fluxes(ref, c):
-            c = c % tiles
-            out = []
-            for side in range(2):
-                at = pl.ds(c * 16 + side * 8, 8)
-                a = ref[at, :]
-                u = uw[l, at, :]
-                v = vw[l, at, :]
-                x = jnp.abs(u) * a
-                y = jnp.abs(v) * a
-                p = jnp.where(u > 0, x, 0.0)
-                s = jnp.where(v > 0, y, 0.0)
-                out.append((a - x - y, east_of(p), west_of(x - p), s, y - s))
-            return out
+        def fluxes(ref):
+            held = {}
+
+            def flux(c, side):
+                if (c, side) not in held:
+                    at = pl.ds(c % tiles * 16 + side * 8, 8)
+                    a = ref[at, :]
+                    u = uw[l, at, :]
+                    v = vw[l, at, :]
+                    x = jnp.abs(u) * a
+                    y = jnp.abs(v) * a
+                    p = jnp.where(u > 0, x, 0.0)
+                    s = jnp.where(v > 0, y, 0.0)
+                    held[c, side] = (a - x - y, p, x - p, s, y - s)
+                return held[c, side]
+
+            return flux
 
         for c in range(tiles):
             even, odd = force(NT, c)
@@ -490,24 +567,20 @@
         for t in range(NT - 1, -1, -1):
             src = scr.at[pl.ds(0 if t % 2 else half, half)]
             dst = scr.at[pl.ds(half if t % 2 else 0, half)]
-            before, now = fluxes(src, -1), fluxes(src, 0)
-            head = now
+            flux = fluxes(src)
+            east, _ = neighbours(lambda c, side: flux(c, side)[1], pairs, first, last)
+            _, west = neighbours(lambda c, side: flux(c, side)[2], pairs, first, last)
             for c in range(tiles):
-                after = head if c == tiles - 1 else fluxes(src, c + 1)
                 fine = force(t, c)
-                (_, _, _, s_e, n_e), (_, _, _, s_o, n_o) = now
+                (_, _, _, s_e, n_e), (_, _, _, s_o, n_o) = flux(c, 0), flux(c, 1)
                 lats = (s_o + pltpu.roll(n_o, 1, 0), pltpu.roll(s_e, 7, 0) + n_e)
                 for side in range(2):
-                    stay, p, m, _, _ = now[side]
                     value = (
-                        stay
-                        + jnp.where(last, after[side][1], p)
-                        + jnp.where(first, before[side][2], m)
-                        + lats[side]
+                        (flux(c, side)[0] + east(c, side))
+                        + (west(c, side) + lats[side])
                         + fine[side]
                     )
                     dst[pl.ds(c * 16 + side * 8, 8), :] = value
-                before, now = now, after
         for c in range(tiles):
             even = scr[pl.ds(c * 16, 8), :]
             odd = scr[pl.ds(c * 16 + 8, 8), :]
@@ -589,7 +662,7 @@
 
     ring = jax.ShapeDtypeStruct((levels, tiles * 16, LANES), F32)
     uw, vw = call(
-        functools.partial(wind_kernel, tiles),
+        functools.partial(wind_kernel, tiles, halves % 2 == 0),
         (ring, ring),
         [VM] * 5,
         (VM, VM),
@@ -601,7 +674,7 @@
 
     halo = exchange(field, True)
     idx, weights, pair = call(
-        functools.partial(prep_kernel, groups, levels, tiles),
+        functools.partial(prep_kernel, groups, levels, tiles, halves % 2 == 0),
         (
             jax.ShapeDtypeStruct((slots // 8, LANES), I32),
             jax.ShapeDtypeStruct((4, slots, LANES), F32),
@@ -623,23 +696,24 @@
     adjoint, rim = call(
         functools.partial(cycle_kernel, groups, levels, tiles),
         (payload, jax.ShapeDtypeStruct((groups, rows, LANES), F32)),
-        [VM] * 8,
+        [VM, VM, ANY, ANY] + [VM] * 4,
         (VM, VM),
         [
+            vmem(levels, tiles * 16, LANES),
+            vmem(levels, tiles * 16, LANES),
             vmem((NT + 1) * levels * tiles * 16, LANES),
             forcing,
             forcing,
             forcing,
             forcing,
             vmem(2 * tiles * 16, LANES),
-            vmem(32, LANES),
             vmem(slots, LANES),
             vmem(slots, LANES),
-            vmem(32, LANES),
             pltpu.SMEM((slots // 8, LANES), I32),
             pltpu.SemaphoreType.DMA,
+            pltpu.SemaphoreType.DMA((2, levels)),
         ],
-        limit=34,
+        limit=38,
         cost=(1e8, 16e6),
     )(field, halo, uw, vw, idx, weights, pair, front)
 

time: 111 us -> 107 us (0.964)
  waiting for transfers between devices: 48 us -> 42 us
  Pallas kernels: 40.7 us -> 42.9 us
    pallas_call x2, Pallas kernels: 4.27 us -> 10.3 us  [the longest x1 8.09 us: per_device(): call(functools.partial(wind_kernel, tiles, halves % 2 == 0), (ring, ring)...]
    all_to_all x1, waiting for transfers between devices: 15.4 us -> 9.42 us  [per_device(): lax.all_to_all(outgoing, 'horiz', split_axis=0, concat_axis=0, tiled=True)]
    pallas_call x1, Pallas kernels: 27 us -> 22.6 us  [per_device(): call(functools.partial(cycle_kernel, groups, levels, tiles), (payload, ja...]
  transfers between devices with their start and end apart: 6 -> 6, of which waited for: 6 -> 6; matrix products, arithmetic and copies ran while one was open for 0% -> 0% of each run, Pallas kernels for 4% -> 10%
where the time goes in v2:
time: 107 us
  Pallas kernels  42.9 us (40%)
  waiting for transfers between devices  42 us (39%)
  starting transfers between devices  15.3 us (14%)
  local copies, waits for them, and re-layouts  5.63 us (5%)
    all_to_all x1, waiting for transfers between devices, per_device(): lax.all_to_all(total, 'horiz', split_axis=0, concat_axis=0, tiled=True)  25.7 us
    pallas_call x1, Pallas kernels, per_device(): call(functools.partial(cycle_kernel, groups, levels, tiles), (payload, ja...  22.6 us
    all_to_all x1, waiting for transfers between devices, per_device(): lax.all_to_all(outgoing, 'horiz', split_axis=0, concat_axis=0, tiled=True)  9.42 us
    all_to_all x1, starting transfers between devices, per_device(): lax.all_to_all(outgoing, 'horiz', split_axis=0, concat_axis=0, tiled=True)  8.46 us
    pallas_call x1, Pallas kernels, per_device(): call(functools.partial(wind_kernel, tiles, halves % 2 == 0), (ring, ring)...  8.09 us
    ppermute x4, waiting for transfers between devices, exchange(): return lax.ppermute(tile_rows, 'obs', [(0, 1), (1, 0)])  6.82 us
    all_to_all x1, starting transfers between devices, per_device(): lax.all_to_all(total, 'horiz', split_axis=0, concat_axis=0, tiled=True)  6.08 us
    unnamed x21, local copies, waits for them, and re-layouts  5.49 us
  transfers between devices with their start and end apart: 6, of which 6 were waited for; matrix products, arithmetic and copies ran while one was open for 0% of the time, Pallas kernels for 10%

profile of v2, /device:TPU:0, one launch (start us, length us, event | category | flops | bytes accessed | tf_op | source)
XLA Modules:
  0.0 106.6 jit_solution(2450325715313105506)
XLA Ops:
  0.6 5.1 %shard_map.122 = (f32[16,136,128]{2,1,0:T(8,128)}, f32[8,128]{1,0:T(8,128)}) custom-call(f32[128,128]{1,0:T(8,128)} %root_hbm.1, f32[1024,256]{1,0:T(8,128)} %bitcast.9, f32[1024,256]{1,0:T(8,128)} %bitcast.11, s32[1,1024]{1,0:T(1,128)} %bitcast.14, s32[4,1024]{1,0:T(4,128)} %cells_hbm.1, s32[1,1024]{1,0:T(1,128)} %bitcast.15, f32[1,1024]{1,0:T(1,128)} %bitcast.16, ...), custom_call_target="tpu_custom_call" | custom-call | flops 400000000 | bytes 4000000 | tf_op jit(solution)/shard_map/pallas_call | solution.py:626
  5.7 8.5 %all-to-all-start = ((f32[16,136,128]{2,1,0:T(8,128)}), f32[16,136,128]{2,1,0:T(8,128)S(1)}, u32[]{:S(2)}, u32[]{:S(2)}) async-start(f32[16,136,128]{2,1,0:T(8,128)} %get-tuple-element.18), calls=%async_computation | async-start | bytes 2228224 | tf_op jit(solution)/shard_map/all_to_all | solution.py:661
  14.2 0.1 collective-permute-start
  14.3 0.5 collective-permute-start.1
  14.8 2.3 %collective-permute-done.uh_ref = f32[8,8,4096]{2,1,0:T(8,128)} collective-permute-done((f32[8,8,4096]{2,1,0:T(8,128)S(1)}, f32[8,8,4096]{2,1,0:T(8,128)}, u32[]{:S(2)}, u32[]{:S(2)}) %collective-permute-start) | collective-permute-done | bytes 1048608 | tf_op jit(solution)/shard_map/ppermute | solution.py:259
  17.1 1.5 %collective-permute-done.1.vh_ref = f32[8,8,4096]{2,1,0:T(8,128)} collective-permute-done((f32[8,8,4096]{2,1,0:T(8,128)S(1)}, f32[8,8,4096]{2,1,0:T(8,128)}, u32[]{:S(2)}, u32[]{:S(2)}) %collective-permute-start.1) | collective-permute-done | bytes 1048608 | tf_op jit(solution)/shard_map/ppermute | solution.py:259
  18.6 0.1 broadcast_in_dim.23.mask_ref.front_ref
  18.6 1.2 %copy-done.5 = f32[8,8,4096]{2,1,0:T(8,128)S(1)} copy-done((f32[8,8,4096]{2,1,0:T(8,128)S(1)}, f32[8,8,4096]{2,1,0:T(8,128)}, u32[]{:S(2)}) %copy-start.5) | copy-done | bytes 1048600
  19.9 1.2 %copy-done.7 = f32[8,8,4096]{2,1,0:T(8,128)S(1)} copy-done((f32[8,8,4096]{2,1,0:T(8,128)S(1)}, f32[8,8,4096]{2,1,0:T(8,128)}, u32[]{:S(2)}) %copy-start.7) | copy-done | bytes 1048600
  21.1 8.1 %shard_map.123 = (f32[8,512,128]{2,1,0:T(8,128)S(1)}, f32[8,512,128]{2,1,0:T(8,128)S(1)}) custom-call(f32[8,8,4096]{2,1,0:T(8,128)S(1)} %copy-done.5, f32[8,8,4096]{2,1,0:T(8,128)} %collective-permute-done.uh_ref, f32[8,8,4096]{2,1,0:T(8,128)S(1)} %copy-done.7, f32[8,8,4096]{2,1,0:T(8,128)} %collective-permute-done.1.vh_ref, ...), custom_call_target="tpu_custom_call" | custom-call | flops 1000000 | bytes 8000000 | tf_op jit(solution)/shard_map/pallas_call | solution.py:664
  29.2 1.3 %copy-done.2 = f32[8,512,128]{2,1,0:T(8,128)} copy-done((f32[8,512,128]{2,1,0:T(8,128)}, f32[8,512,128]{2,1,0:T(8,128)S(1)}, u32[]{:S(2)}) %copy-start.2) | copy-done | bytes 2097176
  30.5 9.4 %all-to-all-done.got_hbm.field = f32[16,136,128]{2,1,0:T(8,128)S(1)} async-done(((f32[16,136,128]{2,1,0:T(8,128)}), f32[16,136,128]{2,1,0:T(8,128)S(1)}, u32[]{:S(2)}, u32[]{:S(2)}) %all-to-all-start) | async-done | bytes 1114144 | tf_op jit(solution)/shard_map/all_to_all | solution.py:661
  39.9 0.1 broadcast_in_dim.24.mask_ref
  40.0 2.2 %shard_map.124 = (s32[128,128]{1,0:T(8,128)S(1)}, f32[4,1024,128]{2,1,0:T(8,128)S(1)}, f32[2,1024,128]{2,1,0:T(8,128)S(1)}) custom-call(f32[16,136,128]{2,1,0:T(8,128)S(1)} %all-to-all-done.got_hbm.field), custom_call_target="tpu_custom_call" | custom-call | flops 1000000 | bytes 6000000 | tf_op jit(solution)/shard_map/pallas_call | solution.py:676
  42.2 0.5 collective-permute-done.2.halo
  42.8 1.6 %copy-done.3 = f32[8,512,128]{2,1,0:T(8,128)S(1)} copy-done((f32[8,512,128]{2,1,0:T(8,128)S(1)}, f32[8,512,128]{2,1,0:T(8,128)}, u32[]{:S(2)}) %copy-start.3) | copy-done | bytes 2097176
  44.4 22.6 %shard_map.125 = (f32[16,136,128]{2,1,0:T(8,128)S(1)}, f32[16,128,128]{2,1,0:T(8,128)S(1)}) custom-call(f32[16,136,128]{2,1,0:T(8,128)S(1)} %all-to-all-done.got_hbm.field, f32[16,136,128]{2,1,0:T(8,128)S(1)} %collective-permute-done.2.halo, f32[8,512,128]{2,1,0:T(8,128)S(1)} %get-tuple-element.22.uw_hbm, f32[8,512,128]{2,1,0:T(8,128)S(1)} %copy-done.3, ...), custom_call_target="tpu_custom_call" | custom-call | flops 100000000 | bytes 16000000 | tf_op jit(solution)/shard_map/pallas_call | solution.py:696
  67.0 0.2 collective-permute-start.3
  67.2 2.5 %collective-permute-done.3.rim_ref = f32[16,128,128]{2,1,0:T(8,128)S(1)} collective-permute-done((f32[16,128,128]{2,1,0:T(8,128)S(1)}, f32[16,128,128]{2,1,0:T(8,128)S(1)}, u32[]{:S(2)}, u32[]{:S(2)}) %collective-permute-start.3) | collective-permute-done | bytes 1048608 | tf_op jit(solution)/shard_map/ppermute | solution.py:259
  69.7 1.6 %shard_map.126 = f32[16,136,128]{2,1,0:T(8,128)} custom-call(f32[16,136,128]{2,1,0:T(8,128)S(1)} %get-tuple-element.28.own_ref, f32[16,128,128]{2,1,0:T(8,128)S(1)} %collective-permute-done.3.rim_ref, f32[8,128]{1,0:T(8,128)S(1)} %broadcast_in_dim.24.mask_ref), custom_call_target="tpu_custom_call" | custom-call | flops 1000000 | bytes 3000000 | tf_op jit(solution)/shard_map/pallas_call | solution.py:721
  71.3 6.1 %all-to-all-start.1 = ((f32[16,136,128]{2,1,0:T(8,128)}), f32[16,136,128]{2,1,0:T(8,128)S(1)}, u32[]{:S(2)}, u32[]{:S(2)}) async-start(f32[16,136,128]{2,1,0:T(8,128)} %shard_map.126), calls=%async_computation.1 | async-start | bytes 2228224 | tf_op jit(solution)/shard_map/all_to_all | solution.py:734
  77.4 0.1 copy.13
  77.5 25.7 %all-to-all-done.1.got_ref = f32[16,136,128]{2,1,0:T(8,128)S(1)} async-done(((f32[16,136,128]{2,1,0:T(8,128)}), f32[16,136,128]{2,1,0:T(8,128)S(1)}, u32[]{:S(2)}, u32[]{:S(2)}) %all-to-all-start.1) | async-done | bytes 1114144 | tf_op jit(solution)/shard_map/all_to_all | solution.py:734
  103.2 3.3 %shard_map.127 = (f32[1024,256]{1,0:T(8,128)}, f32[8,128]{1,0:T(8,128)}) custom-call(f32[128,128]{1,0:T(8,128)S(1)} %bitcast.13, f32[1024,256]{1,0:T(8,128)S(1)} %bitcast.10, f32[1024,256]{1,0:T(8,128)S(1)} %bitcast.12, f32[16,136,128]{2,1,0:T(8,128)S(1)} %all-to-all-done.1.got_ref, f32[8,128]{1,0:T(8,128)S(1)} %copy-done.8), custom_call_target="tpu_custom_call" | custom-call | flops 400000000 | bytes 4000000 | tf_op jit(solution)/shard_map/pallas_call | solution.py:736
  (18 shorter events, 0.0 us)
Async XLA Ops:
  5.7 8.5 %copy-start.4 = (f32[8,8,4096]{2,1,0:T(8,128)S(1)}, f32[8,8,4096]{2,1,0:T(8,128)}, u32[]{:S(2)}) copy-start(f32[8,8,4096]{2,1,0:T(8,128)} %u_ref.1) | copy-start | bytes 3145732
  5.7 8.6 %copy-start.6 = (f32[8,8,4096]{2,1,0:T(8,128)S(1)}, f32[8,8,4096]{2,1,0:T(8,128)}, u32[]{:S(2)}) copy-start(f32[8,8,4096]{2,1,0:T(8,128)} %v_ref.1) | copy-start | bytes 3145732
  5.7 34.2 %all-to-all-start = ((f32[16,136,128]{2,1,0:T(8,128)}), f32[16,136,128]{2,1,0:T(8,128)S(1)}, u32[]{:S(2)}, u32[]{:S(2)}) async-start(f32[16,136,128]{2,1,0:T(8,128)} %get-tuple-element.18), calls=%async_computation | async-start | bytes 2228224 | tf_op jit(solution)/shard_map/all_to_all | solution.py:661
  14.2 2.9 %collective-permute-start = (f32[8,8,4096]{2,1,0:T(8,128)S(1)}, f32[8,8,4096]{2,1,0:T(8,128)}, u32[]{:S(2)}, u32[]{:S(2)}) collective-permute-start(f32[8,8,4096]{2,1,0:T(8,128)S(1)} %copy-done.4), channel_id=1, source_target_pairs={{0,16},{16,0},{1,17},{17,1},{2,18},{18,2},{3,19},{19,3},{4,20},{20... | collective-permute-start | bytes 3145736 | tf_op jit(solution)/shard_map/ppermute | solution.py:259
  14.3 4.3 %collective-permute-start.1 = (f32[8,8,4096]{2,1,0:T(8,128)S(1)}, f32[8,8,4096]{2,1,0:T(8,128)}, u32[]{:S(2)}, u32[]{:S(2)}) collective-permute-start(f32[8,8,4096]{2,1,0:T(8,128)S(1)} %copy-done.6), channel_id=1, source_target_pairs={{0,16},{16,0},{1,17},{17,1},{2,18},{18,2},{3,19},{19,3},{4,20},{20... | collective-permute-start | bytes 3145736 | tf_op jit(solution)/shard_map/ppermute | solution.py:259
  18.6 1.2 %copy-start.5 = (f32[8,8,4096]{2,1,0:T(8,128)S(1)}, f32[8,8,4096]{2,1,0:T(8,128)}, u32[]{:S(2)}) copy-start(f32[8,8,4096]{2,1,0:T(8,128)} %u_ref.1) | copy-start | bytes 3145732
  19.9 1.2 %copy-start.7 = (f32[8,8,4096]{2,1,0:T(8,128)S(1)}, f32[8,8,4096]{2,1,0:T(8,128)}, u32[]{:S(2)}) copy-start(f32[8,8,4096]{2,1,0:T(8,128)} %v_ref.1) | copy-start | bytes 3145732
  29.2 1.3 %copy-start.2 = (f32[8,512,128]{2,1,0:T(8,128)}, f32[8,512,128]{2,1,0:T(8,128)S(1)}, u32[]{:S(2)}) copy-start(f32[8,512,128]{2,1,0:T(8,128)S(1)} %get-tuple-element.23.vw_hbm) | copy-start | bytes 6291460
  40.0 2.8 %collective-permute-start.2 = (f32[16,136,128]{2,1,0:T(8,128)S(1)}, f32[16,136,128]{2,1,0:T(8,128)S(1)}, u32[]{:S(2)}, u32[]{:S(2)}) collective-permute-start(f32[16,136,128]{2,1,0:T(8,128)S(1)} %all-to-all-done.got_hbm.field), channel_id=1, source_target_pairs={{0,16},{16,0},{1,17},{17,1},{2,18},{18,2},{3,19},{19,3},{4,20},{20... | collective-permute-start | bytes 3342344 | tf_op jit(solution)/shard_map/ppermute | solution.py:259
  42.8 1.6 %copy-start.3 = (f32[8,512,128]{2,1,0:T(8,128)S(1)}, f32[8,512,128]{2,1,0:T(8,128)}, u32[]{:S(2)}) copy-start(f32[8,512,128]{2,1,0:T(8,128)} %copy-done.2) | copy-start | bytes 6291460
  67.0 2.7 %collective-permute-start.3 = (f32[16,128,128]{2,1,0:T(8,128)S(1)}, f32[16,128,128]{2,1,0:T(8,128)S(1)}, u32[]{:S(2)}, u32[]{:S(2)}) collective-permute-start(f32[16,128,128]{2,1,0:T(8,128)S(1)} %get-tuple-element.29), channel_id=1, source_target_pairs={{0,16},{16,0},{1,17},{17,1},{2,18},{18,2},{3,19},{19,3},{4,20},{20... | collective-permute-start | bytes 3145736 | tf_op jit(solution)/shard_map/ppermute | solution.py:259
  71.3 6.1 %copy-start.9 = (f32[128,128]{1,0:T(8,128)S(1)}, f32[128,128]{1,0:T(8,128)}, u32[]{:S(2)}) copy-start(f32[128,128]{1,0:T(8,128)} %root_hbm.1) | copy-start | bytes 196612
  71.3 31.9 %copy-start = (f32[128,8,256]{2,1,0:T(8,128)S(1)}, f32[128,8,256]{2,1,0:T(8,128)}, u32[]{:S(2)}) copy-start(f32[128,8,256]{2,1,0:T(8,128)} %param.11) | copy-start | bytes 3145732
  71.3 31.9 %copy-start.1 = (f32[128,8,256]{2,1,0:T(8,128)S(1)}, f32[128,8,256]{2,1,0:T(8,128)}, u32[]{:S(2)}) copy-start(f32[128,8,256]{2,1,0:T(8,128)} %param.12) | copy-start | bytes 3145732
  71.3 31.9 %copy-start.8 = (f32[8,128]{1,0:T(8,128)S(1)}, f32[8,128]{1,0:T(8,128)}, u32[]{:S(2)}) copy-start(f32[8,128]{1,0:T(8,128)} %get-tuple-element.31.placed_ref) | copy-start | bytes 12292
  71.3 31.9 %all-to-all-start.1 = ((f32[16,136,128]{2,1,0:T(8,128)}), f32[16,136,128]{2,1,0:T(8,128)S(1)}, u32[]{:S(2)}, u32[]{:S(2)}) async-start(f32[16,136,128]{2,1,0:T(8,128)} %shard_map.126), calls=%async_computation.1 | async-start | bytes 2228224 | tf_op jit(solution)/shard_map/all_to_all | solution.py:734

commit v3 on v2

--- a/solution.py
+++ b/solution.py
@@ -359,10 +359,34 @@
         out[g, pl.ds(last, ROWS), CAP : 2 * CAP] = part[ROWS:FIELDS]
 
 
-def prep_kernel(groups, levels, tiles, pairs, got_hbm, idx_ref, w_ref, vr_ref, got, scr, columns, sem):
+def prep_kernel(
+    groups,
+    levels,
+    tiles,
+    pairs,
+    got_hbm,
+    uw_hbm,
+    vw_hbm,
+    idx_ref,
+    w_ref,
+    vr_ref,
+    uw_ref,
+    vw_ref,
+    got,
+    scr,
+    columns,
+    sem,
+    wind_sems,
+):
     last = got_hbm.shape[1] - ROWS
     load = pltpu.make_async_copy(got_hbm.at[:, pl.ds(last, ROWS), :], got, sem)
     load.start()
+    winds = [
+        pltpu.make_async_copy(uw_hbm, uw_ref, wind_sems.at[0]),
+        pltpu.make_async_copy(vw_hbm, vw_ref, wind_sems.at[1]),
+    ]
+    for copy in winds:
+        copy.start()
     scr[...] = jnp.zeros_like(scr)
     load.wait()
     lon = tiles * LANES
@@ -401,9 +425,11 @@
             here = columns[pl.ds(j, few, stride=8), :]
             index = jnp.where((narrow // 4) % 8 == j, pltpu.roll(here, 4 * j, 1) if j else here, index)
         idx_ref[pl.ds(b * few, few), :] = index.astype(I32)
-
-
-NSCRATCH = 13
+    for copy in winds:
+        copy.wait()
+
+
+NSCRATCH = 10
 
 
 def cycle_kernel(
@@ -412,8 +438,8 @@
     tiles,
     field,
     halo,
-    uw_hbm,
-    vw_hbm,
+    uw,
+    vw,
     idx_ref,
     w,
     vr,
@@ -421,7 +447,7 @@
     *refs,
 ):
     own_out, rim_out = refs[: -NSCRATCH]
-    (uw, vw, states, f0, f1, f2, f3, scr, acc, dep_ref, idx, sem, lsems) = refs[
+    (states, f0, f1, f2, f3, scr, acc, dep_ref, idx, sem) = refs[
         -NSCRATCH:
     ]
     forcing = (f0, f1, f2, f3)
@@ -429,15 +455,6 @@
     per = tiles // groups
     pairs = per % 2 == 0
     block = tiles * 16
-    def wind_loads(l):
-        return (
-            pltpu.make_async_copy(uw_hbm.at[l], uw.at[l], lsems.at[0, l]),
-            pltpu.make_async_copy(vw_hbm.at[l], vw.at[l], lsems.at[1, l]),
-        )
-
-    for l in range(levels):
-        for copy in wind_loads(l):
-            copy.start()
     load = pltpu.make_async_copy(idx_ref, idx, sem)
     load.start()
 
@@ -449,8 +466,6 @@
     zero = jnp.zeros((8, LANES), F32)
 
     def forward(l, carry):
-        for copy in wind_loads(l):
-            copy.wait()
         start = pl.multiple_of(l * block, block)
         for c in range(tiles):
             j, h = divmod(c, per)
@@ -460,8 +475,6 @@
         for c in range(tiles):
             states[pl.ds(start + c * 16, 8), :] = scr[pl.ds(c * 16, 8, stride=2), :]
             states[pl.ds(start + c * 16 + 8, 8), :] = scr[pl.ds(c * 16 + 1, 8, stride=2), :]
-        fstart = pl.multiple_of(l * tiles * 8, tiles * 8)
-        fstep = levels * tiles * 8
         for t in range(NT):
             src = pl.multiple_of(start + t * levels * block, block)
             dst = pl.multiple_of(start + (t + 1) * levels * block, block)
@@ -488,27 +501,33 @@
                     states[pl.ds(dst + c * 16 + side * 8, 8), :] = (
                         here + jnp.abs(u) * (lon - here) + jnp.abs(v) * (lat - here)
                     )
-                for f in forcing:
-                    f[pl.ds(pl.multiple_of(fstart + t * fstep, 8) + c * 8, 8), :] = zero
-                    if t == NT - 1:
-                        f[pl.ds(pl.multiple_of(fstart + NT * fstep, 8) + c * 8, 8), :] = zero
         return carry
 
     lax.fori_loop(0, levels, forward, 0)
 
     load.wait()
 
+    share = f0.shape[0] // (slots // 16)
+
     def gather(i, carry):
-        base = pl.multiple_of(i * 8, 8)
-        for j in range(8):
-            total = None
-            for k in range(4):
-                term = w[k, pl.ds(base + j, 1), :] * states[pl.ds(idx[i, j * 4 + k], 1), :]
-                total = term if total is None else total + term
-            acc[pl.ds(base + j, 1), :] = total
+        start = pl.multiple_of(i * share, 8)
+        for f in forcing:
+            for c in range(share // 8):
+                f[pl.ds(start + c * 8, 8), :] = zero
+        for half in range(2):
+            group = i * 2 + half
+            base = pl.multiple_of(group * 8, 8)
+            for j in range(8):
+                total = None
+                for k in range(4):
+                    term = (
+                        w[k, pl.ds(base + j, 1), :] * states[pl.ds(idx[group, j * 4 + k], 1), :]
+                    )
+                    total = term if total is None else total + term
+                acc[pl.ds(base + j, 1), :] = total
         return carry
 
-    lax.fori_loop(0, slots // 8, gather, 0, unroll=4)
+    lax.fori_loop(0, slots // 16, gather, 0, unroll=2)
 
     hx = jnp.sum(acc[...], axis=1, keepdims=True)
     dep_ref[...] = vr[1] * (hx - vr[0])
@@ -673,34 +692,35 @@
     field, uw, vw, front, back = lax.optimization_barrier((field, uw, vw, front, back))
 
     halo = exchange(field, True)
-    idx, weights, pair = call(
+    idx, weights, pair, uw, vw = call(
         functools.partial(prep_kernel, groups, levels, tiles, halves % 2 == 0),
         (
             jax.ShapeDtypeStruct((slots // 8, LANES), I32),
             jax.ShapeDtypeStruct((4, slots, LANES), F32),
             jax.ShapeDtypeStruct((2, slots, LANES), F32),
+            ring,
+            ring,
         ),
-        [ANY],
-        (VM, VM, VM),
+        [ANY] * 3,
+        (VM,) * 5,
         [
             vmem(groups, ROWS, LANES),
             vmem(LANES, slots),
             vmem(LANES, LANES),
             pltpu.SemaphoreType.DMA,
+            pltpu.SemaphoreType.DMA((2,)),
         ],
-        limit=8,
+        limit=44,
         cost=(1e6, 6e6),
-    )(field)
+    )(field, uw, vw)
 
     forcing = vmem((NT + 1) * levels * tiles * 8, LANES)
     adjoint, rim = call(
         functools.partial(cycle_kernel, groups, levels, tiles),
         (payload, jax.ShapeDtypeStruct((groups, rows, LANES), F32)),
-        [VM, VM, ANY, ANY] + [VM] * 4,
+        [VM] * 8,
         (VM, VM),
         [
-            vmem(levels, tiles * 16, LANES),
-            vmem(levels, tiles * 16, LANES),
             vmem((NT + 1) * levels * tiles * 16, LANES),
             forcing,
             forcing,
@@ -711,9 +731,8 @@
             vmem(slots, LANES),
             pltpu.SMEM((slots // 8, LANES), I32),
             pltpu.SemaphoreType.DMA,
-            pltpu.SemaphoreType.DMA((2, levels)),
         ],
-        limit=38,
+        limit=34,
         cost=(1e8, 16e6),
     )(field, halo, uw, vw, idx, weights, pair, front)
 

time: 107 us -> 105 us (0.981)
  local copies, waits for them, and re-layouts: 5.63 us -> 2.9 us
  waiting for transfers between devices: 42 us -> 43.1 us
    unnamed x21 -> x17, local copies, waits for them, and re-layouts: 5.49 us -> 2.76 us
    all_to_all x1, waiting for transfers between devices: 9.42 us -> 10.5 us  [per_device(): lax.all_to_all(outgoing, 'horiz', split_axis=0, concat_axis=0, tiled=True)]
where the time goes in v3:
time: 105 us
  waiting for transfers between devices  43.1 us (41%)
  Pallas kernels  42.6 us (41%)
  starting transfers between devices  15.3 us (15%)
  local copies, waits for them, and re-layouts  2.9 us (3%)
    all_to_all x1, waiting for transfers between devices, per_device(): lax.all_to_all(total, 'horiz', split_axis=0, concat_axis=0, tiled=True)  25.8 us
    pallas_call x1, Pallas kernels, per_device(): call(functools.partial(cycle_kernel, groups, levels, tiles), (payload, ja...  22.2 us
    all_to_all x1, waiting for transfers between devices, per_device(): lax.all_to_all(outgoing, 'horiz', split_axis=0, concat_axis=0, tiled=True)  10.5 us
    all_to_all x1, starting transfers between devices, per_device(): lax.all_to_all(outgoing, 'horiz', split_axis=0, concat_axis=0, tiled=True)  8.46 us
    pallas_call x1, Pallas kernels, per_device(): call(functools.partial(wind_kernel, tiles, halves % 2 == 0), (ring, ring)...  8.1 us
    ppermute x4, waiting for transfers between devices, exchange(): return lax.ppermute(tile_rows, 'obs', [(0, 1), (1, 0)])  6.78 us
    all_to_all x1, starting transfers between devices, per_device(): lax.all_to_all(total, 'horiz', split_axis=0, concat_axis=0, tiled=True)  6.07 us
    pallas_call x1, Pallas kernels, per_device(): call(functools.partial(start_kernel, groups), (payload, jax.ShapeDtypeStr...  5.09 us
  transfers between devices with their start and end apart: 6, of which 6 were waited for; matrix products, arithmetic and copies ran while one was open for 0% of the time, Pallas kernels for 10%

profile of v3, /device:TPU:0, one launch (start us, length us, event | category | flops | bytes accessed | tf_op | source)
XLA Modules:
  0.0 104.6 jit_solution(16148699663284637834)
XLA Ops:
  0.6 5.1 %shard_map.122 = (f32[16,136,128]{2,1,0:T(8,128)}, f32[8,128]{1,0:T(8,128)}) custom-call(f32[128,128]{1,0:T(8,128)} %root_hbm.1, f32[1024,256]{1,0:T(8,128)} %bitcast.9, f32[1024,256]{1,0:T(8,128)} %bitcast.11, s32[1,1024]{1,0:T(1,128)} %bitcast.14, s32[4,1024]{1,0:T(4,128)} %cells_hbm.1, s32[1,1024]{1,0:T(1,128)} %bitcast.15, f32[1,1024]{1,0:T(1,128)} %bitcast.16, ...), custom_call_target="tpu_custom_call" | custom-call | flops 400000000 | bytes 4000000 | tf_op jit(solution)/shard_map/pallas_call | solution.py:645
  5.7 0.0 copy-start.4
  5.7 0.0 copy-start.5
  5.7 8.5 %all-to-all-start = ((f32[16,136,128]{2,1,0:T(8,128)}), f32[16,136,128]{2,1,0:T(8,128)S(1)}, u32[]{:S(2)}, u32[]{:S(2)}) async-start(f32[16,136,128]{2,1,0:T(8,128)} %get-tuple-element.20), calls=%async_computation | async-start | bytes 2228224 | tf_op jit(solution)/shard_map/all_to_all | solution.py:680
  14.2 0.1 collective-permute-start
  14.3 0.5 collective-permute-start.1
  14.8 2.3 %collective-permute-done.uh_ref = f32[8,8,4096]{2,1,0:T(8,128)} collective-permute-done((f32[8,8,4096]{2,1,0:T(8,128)S(1)}, f32[8,8,4096]{2,1,0:T(8,128)}, u32[]{:S(2)}, u32[]{:S(2)}) %collective-permute-start) | collective-permute-done | bytes 1048608 | tf_op jit(solution)/shard_map/ppermute | solution.py:259
  17.1 1.5 %collective-permute-done.1.vh_ref = f32[8,8,4096]{2,1,0:T(8,128)} collective-permute-done((f32[8,8,4096]{2,1,0:T(8,128)S(1)}, f32[8,8,4096]{2,1,0:T(8,128)}, u32[]{:S(2)}, u32[]{:S(2)}) %collective-permute-start.1) | collective-permute-done | bytes 1048608 | tf_op jit(solution)/shard_map/ppermute | solution.py:259
  18.6 0.1 broadcast_in_dim.23.mask_ref.front_ref
  18.7 8.1 %shard_map.123 = (f32[8,512,128]{2,1,0:T(8,128)S(1)}, f32[8,512,128]{2,1,0:T(8,128)S(1)}) custom-call(f32[8,8,4096]{2,1,0:T(8,128)S(1)} %copy-done.4, f32[8,8,4096]{2,1,0:T(8,128)} %collective-permute-done.uh_ref, f32[8,8,4096]{2,1,0:T(8,128)S(1)} %copy-done.5, f32[8,8,4096]{2,1,0:T(8,128)} %collective-permute-done.1.vh_ref, ...), custom_call_target="tpu_custom_call" | custom-call | flops 1000000 | bytes 8000000 | tf_op jit(solution)/shard_map/pallas_call | solution.py:683
  26.8 1.3 %copy-done.2 = f32[8,512,128]{2,1,0:T(8,128)} copy-done((f32[8,512,128]{2,1,0:T(8,128)}, f32[8,512,128]{2,1,0:T(8,128)S(1)}, u32[]{:S(2)}) %copy-start.2) | copy-done | bytes 2097176
  28.1 1.3 %copy-done.3 = f32[8,512,128]{2,1,0:T(8,128)} copy-done((f32[8,512,128]{2,1,0:T(8,128)}, f32[8,512,128]{2,1,0:T(8,128)S(1)}, u32[]{:S(2)}) %copy-start.3) | copy-done | bytes 2097176
  29.4 10.5 %all-to-all-done.got_hbm.field = f32[16,136,128]{2,1,0:T(8,128)S(1)} async-done(((f32[16,136,128]{2,1,0:T(8,128)}), f32[16,136,128]{2,1,0:T(8,128)S(1)}, u32[]{:S(2)}, u32[]{:S(2)}) %all-to-all-start) | async-done | bytes 1114144 | tf_op jit(solution)/shard_map/all_to_all | solution.py:680
  40.0 0.1 broadcast_in_dim.24.mask_ref
  40.0 2.3 %shard_map.124 = (s32[128,128]{1,0:T(8,128)S(1)}, f32[4,1024,128]{2,1,0:T(8,128)S(1)}, f32[2,1024,128]{2,1,0:T(8,128)S(1)}, f32[8,512,128]{2,1,0:T(8,128)S(1)}, f32[8,512,128]{2,1,0:T(8,128)S(1)}) custom-call(f32[16,136,128]{2,1,0:T(8,128)S(1)} %all-to-all-done.got_hbm.field, f32[8,512,128]{2,1,0:T(8,128)} %copy-done.2, f32[8,512,128]{2,1,0:T(8,128)} %copy-done.3), custom_call_target="tpu_custom_call" | custom-call | flops 1000000 | bytes 6000000 | tf_op jit(solution)/shard_map/pallas_call | solution.py:695
  42.3 0.5 collective-permute-done.2.halo
  42.8 22.2 %shard_map.125 = (f32[16,136,128]{2,1,0:T(8,128)S(1)}, f32[16,128,128]{2,1,0:T(8,128)S(1)}) custom-call(f32[16,136,128]{2,1,0:T(8,128)S(1)} %all-to-all-done.got_hbm.field, f32[16,136,128]{2,1,0:T(8,128)S(1)} %collective-permute-done.2.halo, f32[8,512,128]{2,1,0:T(8,128)S(1)} %get-tuple-element.26.uw, f32[8,512,128]{2,1,0:T(8,128)S(1)} %get-tuple-element.27.vw, ...), custom_call_target="tpu_custom_call" | custom-call | flops 100000000 | bytes 16000000 | tf_op jit(solution)/shard_map/pallas_call | solution.py:718
  65.0 0.2 collective-permute-start.3
  65.2 2.5 %collective-permute-done.3.rim_ref = f32[16,128,128]{2,1,0:T(8,128)S(1)} collective-permute-done((f32[16,128,128]{2,1,0:T(8,128)S(1)}, f32[16,128,128]{2,1,0:T(8,128)S(1)}, u32[]{:S(2)}, u32[]{:S(2)}) %collective-permute-start.3) | collective-permute-done | bytes 1048608 | tf_op jit(solution)/shard_map/ppermute | solution.py:259
  67.7 1.6 %shard_map.126 = f32[16,136,128]{2,1,0:T(8,128)} custom-call(f32[16,136,128]{2,1,0:T(8,128)S(1)} %get-tuple-element.32.own_ref, f32[16,128,128]{2,1,0:T(8,128)S(1)} %collective-permute-done.3.rim_ref, f32[8,128]{1,0:T(8,128)S(1)} %broadcast_in_dim.24.mask_ref), custom_call_target="tpu_custom_call" | custom-call | flops 1000000 | bytes 3000000 | tf_op jit(solution)/shard_map/pallas_call | solution.py:740
  69.3 6.1 %all-to-all-start.1 = ((f32[16,136,128]{2,1,0:T(8,128)}), f32[16,136,128]{2,1,0:T(8,128)S(1)}, u32[]{:S(2)}, u32[]{:S(2)}) async-start(f32[16,136,128]{2,1,0:T(8,128)} %shard_map.126), calls=%async_computation.1 | async-start | bytes 2228224 | tf_op jit(solution)/shard_map/all_to_all | solution.py:753
  75.4 0.1 copy.13
  75.5 25.8 %all-to-all-done.1.got_ref = f32[16,136,128]{2,1,0:T(8,128)S(1)} async-done(((f32[16,136,128]{2,1,0:T(8,128)}), f32[16,136,128]{2,1,0:T(8,128)S(1)}, u32[]{:S(2)}, u32[]{:S(2)}) %all-to-all-start.1) | async-done | bytes 1114144 | tf_op jit(solution)/shard_map/all_to_all | solution.py:753
  101.3 3.3 %shard_map.127 = (f32[1024,256]{1,0:T(8,128)}, f32[8,128]{1,0:T(8,128)}) custom-call(f32[128,128]{1,0:T(8,128)S(1)} %bitcast.13, f32[1024,256]{1,0:T(8,128)S(1)} %bitcast.10, f32[1024,256]{1,0:T(8,128)S(1)} %bitcast.12, f32[16,136,128]{2,1,0:T(8,128)S(1)} %all-to-all-done.1.got_ref, f32[8,128]{1,0:T(8,128)S(1)} %copy-done.6), custom_call_target="tpu_custom_call" | custom-call | flops 400000000 | bytes 4000000 | tf_op jit(solution)/shard_map/pallas_call | solution.py:755
  (14 shorter events, 0.0 us)
Async XLA Ops:
  5.7 8.5 %copy-start.4 = (f32[8,8,4096]{2,1,0:T(8,128)S(1)}, f32[8,8,4096]{2,1,0:T(8,128)}, u32[]{:S(2)}) copy-start(f32[8,8,4096]{2,1,0:T(8,128)} %u_ref.1) | copy-start | bytes 3145732
  5.7 8.6 %copy-start.5 = (f32[8,8,4096]{2,1,0:T(8,128)S(1)}, f32[8,8,4096]{2,1,0:T(8,128)}, u32[]{:S(2)}) copy-start(f32[8,8,4096]{2,1,0:T(8,128)} %v_ref.1) | copy-start | bytes 3145732
  5.7 34.2 %all-to-all-start = ((f32[16,136,128]{2,1,0:T(8,128)}), f32[16,136,128]{2,1,0:T(8,128)S(1)}, u32[]{:S(2)}, u32[]{:S(2)}) async-start(f32[16,136,128]{2,1,0:T(8,128)} %get-tuple-element.20), calls=%async_computation | async-start | bytes 2228224 | tf_op jit(solution)/shard_map/all_to_all | solution.py:680
  14.2 2.9 %collective-permute-start = (f32[8,8,4096]{2,1,0:T(8,128)S(1)}, f32[8,8,4096]{2,1,0:T(8,128)}, u32[]{:S(2)}, u32[]{:S(2)}) collective-permute-start(f32[8,8,4096]{2,1,0:T(8,128)S(1)} %copy-done.4), channel_id=1, source_target_pairs={{0,16},{16,0},{1,17},{17,1},{2,18},{18,2},{3,19},{19,3},{4,20},{20... | collective-permute-start | bytes 3145736 | tf_op jit(solution)/shard_map/ppermute | solution.py:259
  14.3 4.3 %collective-permute-start.1 = (f32[8,8,4096]{2,1,0:T(8,128)S(1)}, f32[8,8,4096]{2,1,0:T(8,128)}, u32[]{:S(2)}, u32[]{:S(2)}) collective-permute-start(f32[8,8,4096]{2,1,0:T(8,128)S(1)} %copy-done.5), channel_id=1, source_target_pairs={{0,16},{16,0},{1,17},{17,1},{2,18},{18,2},{3,19},{19,3},{4,20},{20... | collective-permute-start | bytes 3145736 | tf_op jit(solution)/shard_map/ppermute | solution.py:259
  26.8 1.4 %copy-start.2 = (f32[8,512,128]{2,1,0:T(8,128)}, f32[8,512,128]{2,1,0:T(8,128)S(1)}, u32[]{:S(2)}) copy-start(f32[8,512,128]{2,1,0:T(8,128)S(1)} %get-tuple-element.24.uw_hbm) | copy-start | bytes 6291460
  28.1 1.3 %copy-start.3 = (f32[8,512,128]{2,1,0:T(8,128)}, f32[8,512,128]{2,1,0:T(8,128)S(1)}, u32[]{:S(2)}) copy-start(f32[8,512,128]{2,1,0:T(8,128)S(1)} %get-tuple-element.25.vw_hbm) | copy-start | bytes 6291460
  40.0 2.8 %collective-permute-start.2 = (f32[16,136,128]{2,1,0:T(8,128)S(1)}, f32[16,136,128]{2,1,0:T(8,128)S(1)}, u32[]{:S(2)}, u32[]{:S(2)}) collective-permute-start(f32[16,136,128]{2,1,0:T(8,128)S(1)} %all-to-all-done.got_hbm.field), channel_id=1, source_target_pairs={{0,16},{16,0},{1,17},{17,1},{2,18},{18,2},{3,19},{19,3},{4,20},{20... | collective-permute-start | bytes 3342344 | tf_op jit(solution)/shard_map/ppermute | solution.py:259
  65.0 2.7 %collective-permute-start.3 = (f32[16,128,128]{2,1,0:T(8,128)S(1)}, f32[16,128,128]{2,1,0:T(8,128)S(1)}, u32[]{:S(2)}, u32[]{:S(2)}) collective-permute-start(f32[16,128,128]{2,1,0:T(8,128)S(1)} %get-tuple-element.33), channel_id=1, source_target_pairs={{0,16},{16,0},{1,17},{17,1},{2,18},{18,2},{3,19},{19,3},{4,20},{20... | collective-permute-start | bytes 3145736 | tf_op jit(solution)/shard_map/ppermute | solution.py:259
  69.3 6.1 %copy-start.7 = (f32[128,128]{1,0:T(8,128)S(1)}, f32[128,128]{1,0:T(8,128)}, u32[]{:S(2)}) copy-start(f32[128,128]{1,0:T(8,128)} %root_hbm.1) | copy-start | bytes 196612
  69.3 32.0 %copy-start = (f32[128,8,256]{2,1,0:T(8,128)S(1)}, f32[128,8,256]{2,1,0:T(8,128)}, u32[]{:S(2)}) copy-start(f32[128,8,256]{2,1,0:T(8,128)} %param.11) | copy-start | bytes 3145732
  69.3 32.0 %copy-start.1 = (f32[128,8,256]{2,1,0:T(8,128)S(1)}, f32[128,8,256]{2,1,0:T(8,128)}, u32[]{:S(2)}) copy-start(f32[128,8,256]{2,1,0:T(8,128)} %param.12) | copy-start | bytes 3145732
  69.3 32.0 %copy-start.6 = (f32[8,128]{1,0:T(8,128)S(1)}, f32[8,128]{1,0:T(8,128)}, u32[]{:S(2)}) copy-start(f32[8,128]{1,0:T(8,128)} %get-tuple-element.35.placed_ref) | copy-start | bytes 12292
  69.3 31.9 %all-to-all-start.1 = ((f32[16,136,128]{2,1,0:T(8,128)}), f32[16,136,128]{2,1,0:T(8,128)S(1)}, u32[]{:S(2)}, u32[]{:S(2)}) async-start(f32[16,136,128]{2,1,0:T(8,128)} %shard_map.126), calls=%async_computation.1 | async-start | bytes 2228224 | tf_op jit(solution)/shard_map/all_to_all | solution.py:753

commit v4 on v3

--- a/solution.py
+++ b/solution.py
@@ -75,6 +75,7 @@
     weight,
     rinv,
     out,
+    mid,
     data,
     hit,
     small_sems,
@@ -119,29 +120,37 @@
     block = levels * ROWS
     outs = []
     pairs = halves % 2 == 0
+    step = 2 if pairs else 1
     for h in range(halves):
         parts[h][0].wait()
+    for m in range(0, halves, step):
+        for r in range(ROWS):
+            at = level_rows(r, levels_all)
+            columns = jnp.concatenate([control[m + i, at, :] for i in range(step)], axis=1)
+            mid[m // step, r] = apply_root(wide, columns)
     for h in range(halves):
         parts[h][1].wait()
-    for m in range(0, halves, 2 if pairs else 1):
-        for r in range(ROWS):
-            at = level_rows(r, levels_all)
-            if pairs:
-                both = apply_root(
-                    wide, jnp.concatenate([control[m, at, :], control[m + 1, at, :]], axis=1)
+    share = groups // 2
+    count = share * levels
+    for p in range(2):
+        for m in range(0, halves, step):
+            for r in range(ROWS):
+                at = pl.ds(p * count * ROWS + r, count, stride=ROWS)
+                both = mid[m // step, r, pl.ds(p * count, count), :] * jnp.concatenate(
+                    [spread[m + i, at, :] for i in range(step)], axis=1
                 )
-                both = both * jnp.concatenate([spread[m, at, :], spread[m + 1, at, :]], axis=1)
-                both = reorder(both, even_odd(), split2)
-                values = [both[:, 0:LANES], both[:, LANES:]]
-            else:
-                values = [spread[m, at, :] * apply_root(wide, control[m, at, :])]
-            for i, value_r in enumerate(values):
-                for g in range(groups):
-                    out[g, pl.ds((m + i) * block + r, levels, stride=ROWS), :] = value_r[
-                        g * levels : (g + 1) * levels
-                    ]
-    outs.append(pltpu.make_async_copy(out, out_hbm, out_sems.at[0]))
-    outs[-1].start()
+                if pairs:
+                    both = reorder(both, even_odd(), split2)
+                for i in range(step):
+                    for g in range(share):
+                        out[p * share + g, pl.ds((m + i) * block + r, levels, stride=ROWS), :] = both[
+                            g * levels : (g + 1) * levels, i * LANES : (i + 1) * LANES
+                        ]
+        part_groups = pl.ds(p * share, share)
+        outs.append(
+            pltpu.make_async_copy(out.at[part_groups], out_hbm.at[part_groups], out_sems.at[p])
+        )
+        outs[-1].start()
     for copy in outs:
         copy.wait()
 
@@ -201,12 +210,19 @@
         copy.wait()
 
 
-def rim_kernel(own_ref, rim_ref, mask_ref, out_ref):
+def rim_kernel(levels, packed, own_ref, rim_ref, mask_ref, out_ref):
     mask = mask_ref[...]
-    rows = rim_ref.shape[1]
+    rows = own_ref.shape[1] - ROWS
     for c in range(rows // ROWS):
         at = pl.ds(c * ROWS, ROWS)
-        out_ref[:, at, :] = own_ref[:, at, :] + rim_ref[:, at, :] * mask[None]
+        h, l = divmod(c, levels)
+        for g in range(own_ref.shape[0]):
+            if packed:
+                rim = rim_ref[g, pl.ds((h // 2 * levels + l) * ROWS, ROWS), :]
+                rim = pltpu.roll(rim, 4, 0) if h % 2 else rim
+            else:
+                rim = rim_ref[g, at, :]
+            out_ref[g, at, :] = own_ref[g, at, :] + rim * mask
     rest = pl.ds(rows, ROWS)
     out_ref[:, rest, :] = own_ref[:, rest, :]
 
@@ -436,6 +452,7 @@
     groups,
     levels,
     tiles,
+    packed,
     field,
     halo,
     uw,
@@ -609,7 +626,13 @@
             j, h = divmod(c, per)
             at = pl.ds(pl.multiple_of((h * levels + l) * 8, 8), 8)
             own_out[j, at, :] = scr[pl.ds(half + c * 16, 8), :]
-            rim_out[j, at, :] = scr[pl.ds(half + c * 16 + 8, 8), :]
+            rim = scr[pl.ds(half + c * 16 + 8, 8), :]
+            if not packed:
+                rim_out[j, at, :] = rim
+            elif h % 2:
+                earlier = scr[pl.ds(half + (c - 1) * 16 + 8, 8), :]
+                at = pl.ds(pl.multiple_of((h // 2 * levels + l) * 8, 8), 8)
+                rim_out[j, at, :] = jnp.where(front_ref[...] > 0, earlier, pltpu.roll(rim, 4, 0))
         return carry
 
     lax.fori_loop(0, levels, backward, 0)
@@ -636,6 +659,9 @@
     count = obs_value.shape[0]
     halves = width // LANES
     rows = halves * levels * ROWS
+    pair_step = 2 if halves % 2 == 0 else 1
+    packed = lax.axis_size("obs") == 2 and pair_step == 2
+    rim_rows = rows // 2 if packed else rows
     front, back = halo_masks()
     flat = (levels_all * ROWS, width)
     payload = jax.ShapeDtypeStruct((groups, rows + ROWS, LANES), F32)
@@ -658,11 +684,12 @@
             vmem(4, count),
             vmem(1, count),
             vmem(*payload.shape),
+            vmem(halves // pair_step, ROWS, levels_all, pair_step * LANES),
             vmem(FIELDS, count),
             pltpu.VMEM((count, slots), jnp.bfloat16),
             pltpu.SemaphoreType.DMA((7,)),
             pltpu.SemaphoreType.DMA((2, halves)),
-            pltpu.SemaphoreType.DMA((halves,)),
+            pltpu.SemaphoreType.DMA((2,)),
         ],
         limit=56,
         cost=(4e8, 4e6),
@@ -716,8 +743,8 @@
 
     forcing = vmem((NT + 1) * levels * tiles * 8, LANES)
     adjoint, rim = call(
-        functools.partial(cycle_kernel, groups, levels, tiles),
-        (payload, jax.ShapeDtypeStruct((groups, rows, LANES), F32)),
+        functools.partial(cycle_kernel, groups, levels, tiles, packed),
+        (payload, jax.ShapeDtypeStruct((groups, rim_rows, LANES), F32)),
         [VM] * 8,
         (VM, VM),
         [
@@ -738,11 +765,11 @@
 
     part = groups // 4
     total = call(
-        rim_kernel,
+        functools.partial(rim_kernel, levels, packed),
         payload,
         [
             pl.BlockSpec((part, rows + ROWS, LANES), lambda i: (i, 0, 0)),
-            pl.BlockSpec((part, rows, LANES), lambda i: (i, 0, 0)),
+            pl.BlockSpec((part, rim_rows, LANES), lambda i: (i, 0, 0)),
             pl.BlockSpec((ROWS, LANES), lambda i: (0, 0)),
         ],
         pl.BlockSpec((part, rows + ROWS, LANES), lambda i: (i, 0, 0)),

time: 105 us -> 105 us (level)
  no operation moved by 1% of the time
where the time goes in v4:
time: 105 us; the launch traced here: 104 us
  Pallas kernels  42.7 us (41%)
  waiting for transfers between devices  42.3 us (40%)
  starting transfers between devices  15.3 us (15%)
  local copies, waits for them, and re-layouts  2.9 us (3%)
    all_to_all x1, waiting for transfers between devices, per_device(): lax.all_to_all(total, 'horiz', split_axis=0, concat_axis=0, tiled=True)  25.8 us
    pallas_call x1, Pallas kernels, per_device(): call(functools.partial(cycle_kernel, groups, levels, tiles, packed), (pay...  22.4 us
    all_to_all x1, waiting for transfers between devices, per_device(): lax.all_to_all(outgoing, 'horiz', split_axis=0, concat_axis=0, tiled=True)  10.6 us
    all_to_all x1, starting transfers between devices, per_device(): lax.all_to_all(outgoing, 'horiz', split_axis=0, concat_axis=0, tiled=True)  8.46 us
    pallas_call x1, Pallas kernels, per_device(): call(functools.partial(wind_kernel, tiles, halves % 2 == 0), (ring, ring)...  8.09 us
    all_to_all x1, starting transfers between devices, per_device(): lax.all_to_all(total, 'horiz', split_axis=0, concat_axis=0, tiled=True)  6.07 us
    ppermute x4, waiting for transfers between devices, exchange(): return lax.ppermute(tile_rows, 'obs', [(0, 1), (1, 0)])  6.03 us
    pallas_call x1, Pallas kernels, per_device(): call(functools.partial(start_kernel, groups), (payload, jax.ShapeDtypeStr...  4.98 us
  transfers between devices with their start and end apart: 6, of which 6 were waited for; matrix products, arithmetic and copies ran while one was open for 0% of the time, Pallas kernels for 10%

profile of v4, /device:TPU:0, one launch (start us, length us, event | category | flops | bytes accessed | tf_op | source)
XLA Modules:
  0.0 104.0 jit_solution(7275728145851051226)
XLA Ops:
  0.6 5.0 %shard_map.122 = (f32[16,136,128]{2,1,0:T(8,128)}, f32[8,128]{1,0:T(8,128)}) custom-call(f32[128,128]{1,0:T(8,128)} %root_hbm.1, f32[1024,256]{1,0:T(8,128)} %bitcast.9, f32[1024,256]{1,0:T(8,128)} %bitcast.11, s32[1,1024]{1,0:T(1,128)} %bitcast.14, s32[4,1024]{1,0:T(4,128)} %cells_hbm.1, s32[1,1024]{1,0:T(1,128)} %bitcast.15, f32[1,1024]{1,0:T(1,128)} %bitcast.16, ...), custom_call_target="tpu_custom_call" | custom-call | flops 400000000 | bytes 4000000 | tf_op jit(solution)/shard_map/pallas_call | solution.py:671
  5.6 0.0 copy-start.4
  5.6 0.0 copy-start.5
  5.6 8.5 %all-to-all-start = ((f32[16,136,128]{2,1,0:T(8,128)}), f32[16,136,128]{2,1,0:T(8,128)S(1)}, u32[]{:S(2)}, u32[]{:S(2)}) async-start(f32[16,136,128]{2,1,0:T(8,128)} %get-tuple-element.20), calls=%async_computation | async-start | bytes 2228224 | tf_op jit(solution)/shard_map/all_to_all | solution.py:707
  14.1 0.1 collective-permute-start
  14.2 0.5 collective-permute-start.1
  14.7 2.3 %collective-permute-done.uh_ref = f32[8,8,4096]{2,1,0:T(8,128)} collective-permute-done((f32[8,8,4096]{2,1,0:T(8,128)S(1)}, f32[8,8,4096]{2,1,0:T(8,128)}, u32[]{:S(2)}, u32[]{:S(2)}) %collective-permute-start) | collective-permute-done | bytes 1048608 | tf_op jit(solution)/shard_map/ppermute | solution.py:275
  17.0 1.5 %collective-permute-done.1.vh_ref = f32[8,8,4096]{2,1,0:T(8,128)} collective-permute-done((f32[8,8,4096]{2,1,0:T(8,128)S(1)}, f32[8,8,4096]{2,1,0:T(8,128)}, u32[]{:S(2)}, u32[]{:S(2)}) %collective-permute-start.1) | collective-permute-done | bytes 1048608 | tf_op jit(solution)/shard_map/ppermute | solution.py:275
  18.5 0.1 broadcast_in_dim.23.mask_ref.front_ref
  18.5 8.1 %shard_map.123 = (f32[8,512,128]{2,1,0:T(8,128)S(1)}, f32[8,512,128]{2,1,0:T(8,128)S(1)}) custom-call(f32[8,8,4096]{2,1,0:T(8,128)S(1)} %copy-done.4, f32[8,8,4096]{2,1,0:T(8,128)} %collective-permute-done.uh_ref, f32[8,8,4096]{2,1,0:T(8,128)S(1)} %copy-done.5, f32[8,8,4096]{2,1,0:T(8,128)} %collective-permute-done.1.vh_ref, ...), custom_call_target="tpu_custom_call" | custom-call | flops 1000000 | bytes 8000000 | tf_op jit(solution)/shard_map/pallas_call | solution.py:710
  26.7 1.3 %copy-done.2 = f32[8,512,128]{2,1,0:T(8,128)} copy-done((f32[8,512,128]{2,1,0:T(8,128)}, f32[8,512,128]{2,1,0:T(8,128)S(1)}, u32[]{:S(2)}) %copy-start.2) | copy-done | bytes 2097176
  28.0 1.3 %copy-done.3 = f32[8,512,128]{2,1,0:T(8,128)} copy-done((f32[8,512,128]{2,1,0:T(8,128)}, f32[8,512,128]{2,1,0:T(8,128)S(1)}, u32[]{:S(2)}) %copy-start.3) | copy-done | bytes 2097176
  29.3 10.6 %all-to-all-done.got_hbm.field = f32[16,136,128]{2,1,0:T(8,128)S(1)} async-done(((f32[16,136,128]{2,1,0:T(8,128)}), f32[16,136,128]{2,1,0:T(8,128)S(1)}, u32[]{:S(2)}, u32[]{:S(2)}) %all-to-all-start) | async-done | bytes 1114144 | tf_op jit(solution)/shard_map/all_to_all | solution.py:707
  39.9 0.1 broadcast_in_dim.24.mask_ref
  39.9 2.3 %shard_map.124 = (s32[128,128]{1,0:T(8,128)S(1)}, f32[4,1024,128]{2,1,0:T(8,128)S(1)}, f32[2,1024,128]{2,1,0:T(8,128)S(1)}, f32[8,512,128]{2,1,0:T(8,128)S(1)}, f32[8,512,128]{2,1,0:T(8,128)S(1)}) custom-call(f32[16,136,128]{2,1,0:T(8,128)S(1)} %all-to-all-done.got_hbm.field, f32[8,512,128]{2,1,0:T(8,128)} %copy-done.2, f32[8,512,128]{2,1,0:T(8,128)} %copy-done.3), custom_call_target="tpu_custom_call" | custom-call | flops 1000000 | bytes 6000000 | tf_op jit(solution)/shard_map/pallas_call | solution.py:722
  42.2 0.5 collective-permute-done.2.halo
  42.7 22.4 %shard_map.125 = (f32[16,136,128]{2,1,0:T(8,128)S(1)}, f32[16,64,128]{2,1,0:T(8,128)S(1)}) custom-call(f32[16,136,128]{2,1,0:T(8,128)S(1)} %all-to-all-done.got_hbm.field, f32[16,136,128]{2,1,0:T(8,128)S(1)} %collective-permute-done.2.halo, f32[8,512,128]{2,1,0:T(8,128)S(1)} %get-tuple-element.26.uw, f32[8,512,128]{2,1,0:T(8,128)S(1)} %get-tuple-element.27.vw, ...), custom_call_target="tpu_custom_call" | custom-call | flops 100000000 | bytes 16000000 | tf_op jit(solution)/shard_map/pallas_call | solution.py:745
  65.1 0.2 collective-permute-start.3
  65.3 1.8 %collective-permute-done.3.rim_ref = f32[16,64,128]{2,1,0:T(8,128)S(1)} collective-permute-done((f32[16,64,128]{2,1,0:T(8,128)S(1)}, f32[16,64,128]{2,1,0:T(8,128)S(1)}, u32[]{:S(2)}, u32[]{:S(2)}) %collective-permute-start.3) | collective-permute-done | bytes 524320 | tf_op jit(solution)/shard_map/ppermute | solution.py:275
  67.1 1.6 %shard_map.126 = f32[16,136,128]{2,1,0:T(8,128)} custom-call(f32[16,136,128]{2,1,0:T(8,128)S(1)} %get-tuple-element.32.own_ref, f32[16,64,128]{2,1,0:T(8,128)S(1)} %collective-permute-done.3.rim_ref, f32[8,128]{1,0:T(8,128)S(1)} %broadcast_in_dim.24.mask_ref), custom_call_target="tpu_custom_call" | custom-call | flops 1000000 | bytes 3000000 | tf_op jit(solution)/shard_map/pallas_call | solution.py:767
  68.7 6.1 %all-to-all-start.1 = ((f32[16,136,128]{2,1,0:T(8,128)}), f32[16,136,128]{2,1,0:T(8,128)S(1)}, u32[]{:S(2)}, u32[]{:S(2)}) async-start(f32[16,136,128]{2,1,0:T(8,128)} %shard_map.126), calls=%async_computation.1 | async-start | bytes 2228224 | tf_op jit(solution)/shard_map/all_to_all | solution.py:780
  74.8 0.1 copy.13
  74.9 25.8 %all-to-all-done.1.got_ref = f32[16,136,128]{2,1,0:T(8,128)S(1)} async-done(((f32[16,136,128]{2,1,0:T(8,128)}), f32[16,136,128]{2,1,0:T(8,128)S(1)}, u32[]{:S(2)}, u32[]{:S(2)}) %all-to-all-start.1) | async-done | bytes 1114144 | tf_op jit(solution)/shard_map/all_to_all | solution.py:780
  100.7 3.3 %shard_map.127 = (f32[1024,256]{1,0:T(8,128)}, f32[8,128]{1,0:T(8,128)}) custom-call(f32[128,128]{1,0:T(8,128)S(1)} %bitcast.13, f32[1024,256]{1,0:T(8,128)S(1)} %bitcast.10, f32[1024,256]{1,0:T(8,128)S(1)} %bitcast.12, f32[16,136,128]{2,1,0:T(8,128)S(1)} %all-to-all-done.1.got_ref, f32[8,128]{1,0:T(8,128)S(1)} %copy-done.6), custom_call_target="tpu_custom_call" | custom-call | flops 400000000 | bytes 4000000 | tf_op jit(solution)/shard_map/pallas_call | solution.py:782
  (14 shorter events, 0.0 us)
Async XLA Ops:
  5.6 8.5 %copy-start.4 = (f32[8,8,4096]{2,1,0:T(8,128)S(1)}, f32[8,8,4096]{2,1,0:T(8,128)}, u32[]{:S(2)}) copy-start(f32[8,8,4096]{2,1,0:T(8,128)} %u_ref.1) | copy-start | bytes 3145732
  5.6 8.6 %copy-start.5 = (f32[8,8,4096]{2,1,0:T(8,128)S(1)}, f32[8,8,4096]{2,1,0:T(8,128)}, u32[]{:S(2)}) copy-start(f32[8,8,4096]{2,1,0:T(8,128)} %v_ref.1) | copy-start | bytes 3145732
  5.6 34.2 %all-to-all-start = ((f32[16,136,128]{2,1,0:T(8,128)}), f32[16,136,128]{2,1,0:T(8,128)S(1)}, u32[]{:S(2)}, u32[]{:S(2)}) async-start(f32[16,136,128]{2,1,0:T(8,128)} %get-tuple-element.20), calls=%async_computation | async-start | bytes 2228224 | tf_op jit(solution)/shard_map/all_to_all | solution.py:707
  14.1 2.9 %collective-permute-start = (f32[8,8,4096]{2,1,0:T(8,128)S(1)}, f32[8,8,4096]{2,1,0:T(8,128)}, u32[]{:S(2)}, u32[]{:S(2)}) collective-permute-start(f32[8,8,4096]{2,1,0:T(8,128)S(1)} %copy-done.4), channel_id=1, source_target_pairs={{0,16},{16,0},{1,17},{17,1},{2,18},{18,2},{3,19},{19,3},{4,20},{20... | collective-permute-start | bytes 3145736 | tf_op jit(solution)/shard_map/ppermute | solution.py:275
  14.2 4.3 %collective-permute-start.1 = (f32[8,8,4096]{2,1,0:T(8,128)S(1)}, f32[8,8,4096]{2,1,0:T(8,128)}, u32[]{:S(2)}, u32[]{:S(2)}) collective-permute-start(f32[8,8,4096]{2,1,0:T(8,128)S(1)} %copy-done.5), channel_id=1, source_target_pairs={{0,16},{16,0},{1,17},{17,1},{2,18},{18,2},{3,19},{19,3},{4,20},{20... | collective-permute-start | bytes 3145736 | tf_op jit(solution)/shard_map/ppermute | solution.py:275
  26.6 1.4 %copy-start.2 = (f32[8,512,128]{2,1,0:T(8,128)}, f32[8,512,128]{2,1,0:T(8,128)S(1)}, u32[]{:S(2)}) copy-start(f32[8,512,128]{2,1,0:T(8,128)S(1)} %get-tuple-element.24.uw_hbm) | copy-start | bytes 6291460
  28.0 1.3 %copy-start.3 = (f32[8,512,128]{2,1,0:T(8,128)}, f32[8,512,128]{2,1,0:T(8,128)S(1)}, u32[]{:S(2)}) copy-start(f32[8,512,128]{2,1,0:T(8,128)S(1)} %get-tuple-element.25.vw_hbm) | copy-start | bytes 6291460
  39.9 2.8 %collective-permute-start.2 = (f32[16,136,128]{2,1,0:T(8,128)S(1)}, f32[16,136,128]{2,1,0:T(8,128)S(1)}, u32[]{:S(2)}, u32[]{:S(2)}) collective-permute-start(f32[16,136,128]{2,1,0:T(8,128)S(1)} %all-to-all-done.got_hbm.field), channel_id=1, source_target_pairs={{0,16},{16,0},{1,17},{17,1},{2,18},{18,2},{3,19},{19,3},{4,20},{20... | collective-permute-start | bytes 3342344 | tf_op jit(solution)/shard_map/ppermute | solution.py:275
  65.1 2.0 %collective-permute-start.3 = (f32[16,64,128]{2,1,0:T(8,128)S(1)}, f32[16,64,128]{2,1,0:T(8,128)S(1)}, u32[]{:S(2)}, u32[]{:S(2)}) collective-permute-start(f32[16,64,128]{2,1,0:T(8,128)S(1)} %get-tuple-element.33), channel_id=1, source_target_pairs={{0,16},{16,0},{1,17},{17,1},{2,18},{18,2},{3,19},{19,3},{4,20},{20... | collective-permute-start | bytes 1572872 | tf_op jit(solution)/shard_map/ppermute | solution.py:275
  68.7 6.1 %copy-start.7 = (f32[128,128]{1,0:T(8,128)S(1)}, f32[128,128]{1,0:T(8,128)}, u32[]{:S(2)}) copy-start(f32[128,128]{1,0:T(8,128)} %root_hbm.1) | copy-start | bytes 196612
  68.7 32.0 %copy-start = (f32[128,8,256]{2,1,0:T(8,128)S(1)}, f32[128,8,256]{2,1,0:T(8,128)}, u32[]{:S(2)}) copy-start(f32[128,8,256]{2,1,0:T(8,128)} %param.11) | copy-start | bytes 3145732
  68.7 32.0 %copy-start.1 = (f32[128,8,256]{2,1,0:T(8,128)S(1)}, f32[128,8,256]{2,1,0:T(8,128)}, u32[]{:S(2)}) copy-start(f32[128,8,256]{2,1,0:T(8,128)} %param.12) | copy-start | bytes 3145732
  68.7 32.0 %copy-start.6 = (f32[8,128]{1,0:T(8,128)S(1)}, f32[8,128]{1,0:T(8,128)}, u32[]{:S(2)}) copy-start(f32[8,128]{1,0:T(8,128)} %get-tuple-element.35.placed_ref) | copy-start | bytes 12292
  68.7 31.9 %all-to-all-start.1 = ((f32[16,136,128]{2,1,0:T(8,128)}), f32[16,136,128]{2,1,0:T(8,128)S(1)}, u32[]{:S(2)}, u32[]{:S(2)}) async-start(f32[16,136,128]{2,1,0:T(8,128)} %shard_map.126), calls=%async_computation.1 | async-start | bytes 2228224 | tf_op jit(solution)/shard_map/all_to_all | solution.py:780

commit v5 on v4

--- a/solution.py
+++ b/solution.py
@@ -160,6 +160,7 @@
     levels = levels_all // groups
     halves = out.shape[0]
     block = levels * ROWS
+    share = halves * block + 1
     wide = wide_root(root_ref[...])
     outs = []
     pairs = halves % 2 == 0
@@ -173,7 +174,7 @@
             half = [
                 jnp.concatenate(
                     [
-                        got_ref[g, pl.ds(h * block + r, levels, stride=ROWS), :]
+                        got_ref[pl.ds(g * share + h * block + r, levels, stride=ROWS), :]
                         for g in range(groups)
                     ],
                     axis=0,
@@ -195,7 +196,7 @@
             outs.append(pltpu.make_async_copy(out.at[h], out_hbm.at[:, cols], sems.at[h]))
             outs[-1].start()
     for r in range(groups):
-        row[0:1, r * CAP : (r + 1) * CAP] = got_ref[r, pl.ds(halves * block, 1), 0:CAP]
+        row[0:1, r * CAP : (r + 1) * CAP] = got_ref[pl.ds(r * share + halves * block, 1), 0:CAP]
     lane = lax.broadcasted_iota(I32, (LANES, LANES), 1)
     for b in range(dep_ref.shape[0]):
         placed = to_column(placed_ref[pl.ds(b, 1), :]).astype(I32)
@@ -210,21 +211,28 @@
         copy.wait()
 
 
-def rim_kernel(levels, packed, own_ref, rim_ref, mask_ref, out_ref):
+def rim_kernel(levels, packed, own_ref, rim_ref, mask_ref, out_hbm, out, sems):
     mask = mask_ref[...]
-    rows = own_ref.shape[1] - ROWS
-    for c in range(rows // ROWS):
-        at = pl.ds(c * ROWS, ROWS)
-        h, l = divmod(c, levels)
-        for g in range(own_ref.shape[0]):
-            if packed:
-                rim = rim_ref[g, pl.ds((h // 2 * levels + l) * ROWS, ROWS), :]
-                rim = pltpu.roll(rim, 4, 0) if h % 2 else rim
-            else:
-                rim = rim_ref[g, at, :]
-            out_ref[g, at, :] = own_ref[g, at, :] + rim * mask
-    rest = pl.ds(rows, ROWS)
-    out_ref[:, rest, :] = own_ref[:, rest, :]
+    groups, rows = own_ref.shape[0], own_ref.shape[1] - ROWS
+    share = groups // 2
+    copies = []
+    for p in range(2):
+        for g in range(p * share, (p + 1) * share):
+            for c in range(rows // ROWS):
+                at = pl.ds(c * ROWS, ROWS)
+                h, l = divmod(c, levels)
+                if packed:
+                    rim = rim_ref[g, pl.ds((h // 2 * levels + l) * ROWS, ROWS), :]
+                    rim = pltpu.roll(rim, 4, 0) if h % 2 else rim
+                else:
+                    rim = rim_ref[g, at, :]
+                out[pl.ds(g * (rows + 1) + c * ROWS, ROWS), :] = own_ref[g, at, :] + rim * mask
+            out[pl.ds(g * (rows + 1) + rows, 1), :] = own_ref[g, pl.ds(rows, 1), :]
+        part = pl.ds(p * share * (rows + 1), share * (rows + 1))
+        copies.append(pltpu.make_async_copy(out.at[part], out_hbm.at[part], sems.at[p]))
+        copies[-1].start()
+    for copy in copies:
+        copy.wait()
 
 
 def even_odd(back=False):
@@ -763,21 +771,19 @@
         cost=(1e8, 16e6),
     )(field, halo, uw, vw, idx, weights, pair, front)
 
-    part = groups // 4
+    back_shape = (groups * (rows + 1), LANES)
     total = call(
         functools.partial(rim_kernel, levels, packed),
-        payload,
-        [
-            pl.BlockSpec((part, rows + ROWS, LANES), lambda i: (i, 0, 0)),
-            pl.BlockSpec((part, rim_rows, LANES), lambda i: (i, 0, 0)),
-            pl.BlockSpec((ROWS, LANES), lambda i: (0, 0)),
-        ],
-        pl.BlockSpec((part, rows + ROWS, LANES), lambda i: (i, 0, 0)),
+        jax.ShapeDtypeStruct(back_shape, F32),
+        [VM] * 3,
+        ANY,
+        [vmem(*back_shape), pltpu.SemaphoreType.DMA((2,))],
         limit=8,
         cost=(1e6, 3e6),
-        grid=(4,),
     )(adjoint, exchange(rim, False), back)
-    column = lax.all_to_all(total, "horiz", split_axis=0, concat_axis=0, tiled=True)
+    column = lax.all_to_all(
+        total.reshape(back_shape[0], 1, LANES), "horiz", split_axis=0, concat_axis=0, tiled=True
+    ).reshape(back_shape)
 
     gradient, departure = call(
         functools.partial(end_kernel, groups),

time: 105 us -> 102 us (0.971)
  Pallas kernels: 42.7 us -> 41.4 us
    all_to_all x1, waiting for transfers between devices: 25.8 us -> 24.7 us  [per_device(): lax.all_to_all(total.reshape(back_shape[0], 1, LANES), 'horiz', split_axi...]
where the time goes in v5:
time: 102 us
  Pallas kernels  41.4 us (41%)
  waiting for transfers between devices  41.3 us (40%)
  starting transfers between devices  15.3 us (15%)
  local copies, waits for them, and re-layouts  2.91 us (3%)
    all_to_all x1, waiting for transfers between devices, per_device(): lax.all_to_all(total.reshape(back_shape[0], 1, LANES), 'horiz', split_axi...  24.7 us
    pallas_call x1, Pallas kernels, per_device(): call(functools.partial(cycle_kernel, groups, levels, tiles, packed), (pay...  21.7 us
    all_to_all x1, waiting for transfers between devices, per_device(): lax.all_to_all(outgoing, 'horiz', split_axis=0, concat_axis=0, tiled=True)  10.6 us
    all_to_all x1, starting transfers between devices, per_device(): lax.all_to_all(outgoing, 'horiz', split_axis=0, concat_axis=0, tiled=True)  8.46 us
    pallas_call x1, Pallas kernels, per_device(): call(functools.partial(wind_kernel, tiles, halves % 2 == 0), (ring, ring)...  8.09 us
    all_to_all x1, starting transfers between devices, per_device(): lax.all_to_all(total.reshape(back_shape[0], 1, LANES), 'horiz', split_axi...  6.07 us
    ppermute x4, waiting for transfers between devices, exchange(): return lax.ppermute(tile_rows, 'obs', [(0, 1), (1, 0)])  6.03 us
    pallas_call x1, Pallas kernels, per_device(): call(functools.partial(start_kernel, groups), (payload, jax.ShapeDtypeStr...  4.98 us
  transfers between devices with their start and end apart: 6, of which 6 were waited for; matrix products, arithmetic and copies ran while one was open for 0% of the time, Pallas kernels for 10%

profile of v5, /device:TPU:0, one launch (start us, length us, event | category | flops | bytes accessed | tf_op | source)
XLA Modules:
  0.0 101.6 jit_solution(3373467249625644271)
XLA Ops:
  0.6 5.0 %shard_map.122 = (f32[16,136,128]{2,1,0:T(8,128)}, f32[8,128]{1,0:T(8,128)}) custom-call(f32[128,128]{1,0:T(8,128)} %root_hbm.1, f32[1024,256]{1,0:T(8,128)} %bitcast.14, f32[1024,256]{1,0:T(8,128)} %bitcast.16, s32[1,1024]{1,0:T(1,128)} %bitcast.19, s32[4,1024]{1,0:T(4,128)} %cells_hbm.1, s32[1,1024]{1,0:T(1,128)} %bitcast.20, f32[1,1024]{1,0:T(1,128)} %bitcast.21, ...), custom_call_target="tpu_custom_call" | custom-call | flops 400000000 | bytes 4000000 | tf_op jit(solution)/shard_map/pallas_call | solution.py:679
  5.6 0.0 copy-start.4
  5.6 0.0 copy-start.5
  5.6 8.5 %all-to-all-start = ((f32[16,136,128]{2,1,0:T(8,128)}), f32[16,136,128]{2,1,0:T(8,128)S(1)}, u32[]{:S(2)}, u32[]{:S(2)}) async-start(f32[16,136,128]{2,1,0:T(8,128)} %get-tuple-element.20), calls=%async_computation | async-start | bytes 2228224 | tf_op jit(solution)/shard_map/all_to_all | solution.py:715
  14.1 0.1 collective-permute-start
  14.2 0.5 collective-permute-start.1
  14.7 2.3 %collective-permute-done.uh_ref = f32[8,8,4096]{2,1,0:T(8,128)} collective-permute-done((f32[8,8,4096]{2,1,0:T(8,128)S(1)}, f32[8,8,4096]{2,1,0:T(8,128)}, u32[]{:S(2)}, u32[]{:S(2)}) %collective-permute-start) | collective-permute-done | bytes 1048608 | tf_op jit(solution)/shard_map/ppermute | solution.py:283
  17.0 1.5 %collective-permute-done.1.vh_ref = f32[8,8,4096]{2,1,0:T(8,128)} collective-permute-done((f32[8,8,4096]{2,1,0:T(8,128)S(1)}, f32[8,8,4096]{2,1,0:T(8,128)}, u32[]{:S(2)}, u32[]{:S(2)}) %collective-permute-start.1) | collective-permute-done | bytes 1048608 | tf_op jit(solution)/shard_map/ppermute | solution.py:283
  18.5 0.1 broadcast_in_dim.23.mask_ref.front_ref
  18.5 8.1 %shard_map.123 = (f32[8,512,128]{2,1,0:T(8,128)S(1)}, f32[8,512,128]{2,1,0:T(8,128)S(1)}) custom-call(f32[8,8,4096]{2,1,0:T(8,128)S(1)} %copy-done.4, f32[8,8,4096]{2,1,0:T(8,128)} %collective-permute-done.uh_ref, f32[8,8,4096]{2,1,0:T(8,128)S(1)} %copy-done.5, f32[8,8,4096]{2,1,0:T(8,128)} %collective-permute-done.1.vh_ref, ...), custom_call_target="tpu_custom_call" | custom-call | flops 1000000 | bytes 8000000 | tf_op jit(solution)/shard_map/pallas_call | solution.py:718
  26.7 1.3 %copy-done.2 = f32[8,512,128]{2,1,0:T(8,128)} copy-done((f32[8,512,128]{2,1,0:T(8,128)}, f32[8,512,128]{2,1,0:T(8,128)S(1)}, u32[]{:S(2)}) %copy-start.2) | copy-done | bytes 2097176
  28.0 1.3 %copy-done.3 = f32[8,512,128]{2,1,0:T(8,128)} copy-done((f32[8,512,128]{2,1,0:T(8,128)}, f32[8,512,128]{2,1,0:T(8,128)S(1)}, u32[]{:S(2)}) %copy-start.3) | copy-done | bytes 2097176
  29.3 10.6 %all-to-all-done.got_hbm.field = f32[16,136,128]{2,1,0:T(8,128)S(1)} async-done(((f32[16,136,128]{2,1,0:T(8,128)}), f32[16,136,128]{2,1,0:T(8,128)S(1)}, u32[]{:S(2)}, u32[]{:S(2)}) %all-to-all-start) | async-done | bytes 1114144 | tf_op jit(solution)/shard_map/all_to_all | solution.py:715
  39.9 0.1 broadcast_in_dim.24.mask_ref
  39.9 2.3 %shard_map.124 = (s32[128,128]{1,0:T(8,128)S(1)}, f32[4,1024,128]{2,1,0:T(8,128)S(1)}, f32[2,1024,128]{2,1,0:T(8,128)S(1)}, f32[8,512,128]{2,1,0:T(8,128)S(1)}, f32[8,512,128]{2,1,0:T(8,128)S(1)}) custom-call(f32[16,136,128]{2,1,0:T(8,128)S(1)} %all-to-all-done.got_hbm.field, f32[8,512,128]{2,1,0:T(8,128)} %copy-done.2, f32[8,512,128]{2,1,0:T(8,128)} %copy-done.3), custom_call_target="tpu_custom_call" | custom-call | flops 1000000 | bytes 6000000 | tf_op jit(solution)/shard_map/pallas_call | solution.py:730
  42.2 0.5 collective-permute-done.2.halo
  42.7 21.7 %shard_map.125 = (f32[16,136,128]{2,1,0:T(8,128)S(1)}, f32[16,64,128]{2,1,0:T(8,128)S(1)}) custom-call(f32[16,136,128]{2,1,0:T(8,128)S(1)} %all-to-all-done.got_hbm.field, f32[16,136,128]{2,1,0:T(8,128)S(1)} %collective-permute-done.2.halo, f32[8,512,128]{2,1,0:T(8,128)S(1)} %get-tuple-element.26.uw, f32[8,512,128]{2,1,0:T(8,128)S(1)} %get-tuple-element.27.vw, ...), custom_call_target="tpu_custom_call" | custom-call | flops 100000000 | bytes 16000000 | tf_op jit(solution)/shard_map/pallas_call | solution.py:753
  64.4 0.2 collective-permute-start.3
  64.6 1.8 %collective-permute-done.3.rim_ref = f32[16,64,128]{2,1,0:T(8,128)S(1)} collective-permute-done((f32[16,64,128]{2,1,0:T(8,128)S(1)}, f32[16,64,128]{2,1,0:T(8,128)S(1)}, u32[]{:S(2)}, u32[]{:S(2)}) %collective-permute-start.3) | collective-permute-done | bytes 524320 | tf_op jit(solution)/shard_map/ppermute | solution.py:283
  66.3 1.1 %shard_map.126 = f32[2064,128]{1,0:T(8,128)} custom-call(f32[16,136,128]{2,1,0:T(8,128)S(1)} %get-tuple-element.32.own_ref, f32[16,64,128]{2,1,0:T(8,128)S(1)} %collective-permute-done.3.rim_ref, f32[8,128]{1,0:T(8,128)S(1)} %broadcast_in_dim.24.mask_ref), custom_call_target="tpu_custom_call" | custom-call | flops 1000000 | bytes 3000000 | tf_op jit(solution)/shard_map/pallas_call | solution.py:775
  67.5 6.1 %all-to-all-start.1 = ((f32[2064,1,128]{2,1,0:T(1,128)}), f32[2064,1,128]{2,1,0:T(1,128)S(1)}, u32[]{:S(2)}, u32[]{:S(2)}) async-start(f32[2064,1,128]{2,1,0:T(1,128)} %bitcast.8), calls=%async_computation.1 | async-start | bytes 2113536 | tf_op jit(solution)/shard_map/all_to_all | solution.py:784
  73.5 0.1 copy.14
  73.6 24.7 %all-to-all-done.1 = f32[2064,1,128]{2,1,0:T(1,128)S(1)} async-done(((f32[2064,1,128]{2,1,0:T(1,128)}), f32[2064,1,128]{2,1,0:T(1,128)S(1)}, u32[]{:S(2)}, u32[]{:S(2)}) %all-to-all-start.1) | async-done | bytes 1056800 | tf_op jit(solution)/shard_map/all_to_all | solution.py:784
  98.3 3.3 %shard_map.127 = (f32[1024,256]{1,0:T(8,128)}, f32[8,128]{1,0:T(8,128)}) custom-call(f32[128,128]{1,0:T(8,128)S(1)} %bitcast.18, f32[1024,256]{1,0:T(8,128)S(1)} %bitcast.15, f32[1024,256]{1,0:T(8,128)S(1)} %bitcast.17, f32[2064,128]{1,0:T(8,128)S(1)} %bitcast.13, f32[8,128]{1,0:T(8,128)S(1)} %copy-done.6), custom_call_target="tpu_custom_call" | custom-call | flops 400000000 | bytes 4000000 | tf_op jit(solution)/shard_map/pallas_call | solution.py:788
  (14 shorter events, 0.0 us)
Async XLA Ops:
  5.6 8.5 %copy-start.4 = (f32[8,8,4096]{2,1,0:T(8,128)S(1)}, f32[8,8,4096]{2,1,0:T(8,128)}, u32[]{:S(2)}) copy-start(f32[8,8,4096]{2,1,0:T(8,128)} %u_ref.1) | copy-start | bytes 3145732
  5.6 8.6 %copy-start.5 = (f32[8,8,4096]{2,1,0:T(8,128)S(1)}, f32[8,8,4096]{2,1,0:T(8,128)}, u32[]{:S(2)}) copy-start(f32[8,8,4096]{2,1,0:T(8,128)} %v_ref.1) | copy-start | bytes 3145732
  5.6 34.2 %all-to-all-start = ((f32[16,136,128]{2,1,0:T(8,128)}), f32[16,136,128]{2,1,0:T(8,128)S(1)}, u32[]{:S(2)}, u32[]{:S(2)}) async-start(f32[16,136,128]{2,1,0:T(8,128)} %get-tuple-element.20), calls=%async_computation | async-start | bytes 2228224 | tf_op jit(solution)/shard_map/all_to_all | solution.py:715
  14.1 2.9 %collective-permute-start = (f32[8,8,4096]{2,1,0:T(8,128)S(1)}, f32[8,8,4096]{2,1,0:T(8,128)}, u32[]{:S(2)}, u32[]{:S(2)}) collective-permute-start(f32[8,8,4096]{2,1,0:T(8,128)S(1)} %copy-done.4), channel_id=1, source_target_pairs={{0,16},{16,0},{1,17},{17,1},{2,18},{18,2},{3,19},{19,3},{4,20},{20... | collective-permute-start | bytes 3145736 | tf_op jit(solution)/shard_map/ppermute | solution.py:283
  14.2 4.3 %collective-permute-start.1 = (f32[8,8,4096]{2,1,0:T(8,128)S(1)}, f32[8,8,4096]{2,1,0:T(8,128)}, u32[]{:S(2)}, u32[]{:S(2)}) collective-permute-start(f32[8,8,4096]{2,1,0:T(8,128)S(1)} %copy-done.5), channel_id=1, source_target_pairs={{0,16},{16,0},{1,17},{17,1},{2,18},{18,2},{3,19},{19,3},{4,20},{20... | collective-permute-start | bytes 3145736 | tf_op jit(solution)/shard_map/ppermute | solution.py:283
  26.6 1.4 %copy-start.2 = (f32[8,512,128]{2,1,0:T(8,128)}, f32[8,512,128]{2,1,0:T(8,128)S(1)}, u32[]{:S(2)}) copy-start(f32[8,512,128]{2,1,0:T(8,128)S(1)} %get-tuple-element.24.uw_hbm) | copy-start | bytes 6291460
  28.0 1.3 %copy-start.3 = (f32[8,512,128]{2,1,0:T(8,128)}, f32[8,512,128]{2,1,0:T(8,128)S(1)}, u32[]{:S(2)}) copy-start(f32[8,512,128]{2,1,0:T(8,128)S(1)} %get-tuple-element.25.vw_hbm) | copy-start | bytes 6291460
  39.9 2.8 %collective-permute-start.2 = (f32[16,136,128]{2,1,0:T(8,128)S(1)}, f32[16,136,128]{2,1,0:T(8,128)S(1)}, u32[]{:S(2)}, u32[]{:S(2)}) collective-permute-start(f32[16,136,128]{2,1,0:T(8,128)S(1)} %all-to-all-done.got_hbm.field), channel_id=1, source_target_pairs={{0,16},{16,0},{1,17},{17,1},{2,18},{18,2},{3,19},{19,3},{4,20},{20... | collective-permute-start | bytes 3342344 | tf_op jit(solution)/shard_map/ppermute | solution.py:283
  64.4 2.0 %collective-permute-start.3 = (f32[16,64,128]{2,1,0:T(8,128)S(1)}, f32[16,64,128]{2,1,0:T(8,128)S(1)}, u32[]{:S(2)}, u32[]{:S(2)}) collective-permute-start(f32[16,64,128]{2,1,0:T(8,128)S(1)} %get-tuple-element.33), channel_id=1, source_target_pairs={{0,16},{16,0},{1,17},{17,1},{2,18},{18,2},{3,19},{19,3},{4,20},{20... | collective-permute-start | bytes 1572872 | tf_op jit(solution)/shard_map/ppermute | solution.py:283
  67.4 6.1 %copy-start.7 = (f32[128,128]{1,0:T(8,128)S(1)}, f32[128,128]{1,0:T(8,128)}, u32[]{:S(2)}) copy-start(f32[128,128]{1,0:T(8,128)} %root_hbm.1) | copy-start | bytes 196612
  67.4 30.9 %copy-start = (f32[128,8,256]{2,1,0:T(8,128)S(1)}, f32[128,8,256]{2,1,0:T(8,128)}, u32[]{:S(2)}) copy-start(f32[128,8,256]{2,1,0:T(8,128)} %param.11) | copy-start | bytes 3145732
  67.4 30.9 %copy-start.1 = (f32[128,8,256]{2,1,0:T(8,128)S(1)}, f32[128,8,256]{2,1,0:T(8,128)}, u32[]{:S(2)}) copy-start(f32[128,8,256]{2,1,0:T(8,128)} %param.12) | copy-start | bytes 3145732
  67.4 30.9 %copy-start.6 = (f32[8,128]{1,0:T(8,128)S(1)}, f32[8,128]{1,0:T(8,128)}, u32[]{:S(2)}) copy-start(f32[8,128]{1,0:T(8,128)} %get-tuple-element.35.placed_ref) | copy-start | bytes 12292
  67.5 30.8 %all-to-all-start.1 = ((f32[2064,1,128]{2,1,0:T(1,128)}), f32[2064,1,128]{2,1,0:T(1,128)S(1)}, u32[]{:S(2)}, u32[]{:S(2)}) async-start(f32[2064,1,128]{2,1,0:T(1,128)} %bitcast.8), calls=%async_computation.1 | async-start | bytes 2113536 | tf_op jit(solution)/shard_map/all_to_all | solution.py:784

commit v6 on v5

--- a/solution.py
+++ b/solution.py
@@ -528,7 +528,7 @@
                     )
         return carry
 
-    lax.fori_loop(0, levels, forward, 0)
+    lax.fori_loop(0, levels, forward, 0, unroll=2)
 
     load.wait()
 
@@ -574,7 +574,7 @@
                 forcing[k][at, :] = forcing[k][at, :] + w[k, pl.ds(base + j, 1), :] * dep
         return carry
 
-    lax.fori_loop(0, slots // 8, scatter, 0, unroll=2)
+    lax.fori_loop(0, slots // 8, scatter, 0, unroll=4)
 
     def backward(l, carry):
         fstart = pl.multiple_of(l * tiles * 8, tiles * 8)

time: 102 us -> 102 us (level)
  no operation moved by 1% of the time
where the time goes in v6:
time: 102 us; the launch traced here: 101 us
  waiting for transfers between devices  41.3 us (40%)
  Pallas kernels  41.1 us (40%)
  starting transfers between devices  15.3 us (15%)
  local copies, waits for them, and re-layouts  2.91 us (3%)
    all_to_all x1, waiting for transfers between devices, per_device(): lax.all_to_all(total.reshape(back_shape[0], 1, LANES), 'horiz', split_axi...  24.7 us
    pallas_call x1, Pallas kernels, per_device(): call(functools.partial(cycle_kernel, groups, levels, tiles, packed), (pay...  21.4 us
    all_to_all x1, waiting for transfers between devices, per_device(): lax.all_to_all(outgoing, 'horiz', split_axis=0, concat_axis=0, tiled=True)  10.6 us
    all_to_all x1, starting transfers between devices, per_device(): lax.all_to_all(outgoing, 'horiz', split_axis=0, concat_axis=0, tiled=True)  8.46 us
    pallas_call x1, Pallas kernels, per_device(): call(functools.partial(wind_kernel, tiles, halves % 2 == 0), (ring, ring)...  8.09 us
    all_to_all x1, starting transfers between devices, per_device(): lax.all_to_all(total.reshape(back_shape[0], 1, LANES), 'horiz', split_axi...  6.07 us
    ppermute x4, waiting for transfers between devices, exchange(): return lax.ppermute(tile_rows, 'obs', [(0, 1), (1, 0)])  6.03 us
    pallas_call x1, Pallas kernels, per_device(): call(functools.partial(start_kernel, groups), (payload, jax.ShapeDtypeStr...  4.98 us
  transfers between devices with their start and end apart: 6, of which 6 were waited for; matrix products, arithmetic and copies ran while one was open for 0% of the time, Pallas kernels for 10%

profile of v6, /device:TPU:0, one launch (start us, length us, event | category | flops | bytes accessed | tf_op | source)
XLA Modules:
  0.0 101.4 jit_solution(12478299163104632650)
XLA Ops:
  0.6 5.0 %shard_map.122 = (f32[16,136,128]{2,1,0:T(8,128)}, f32[8,128]{1,0:T(8,128)}) custom-call(f32[128,128]{1,0:T(8,128)} %root_hbm.1, f32[1024,256]{1,0:T(8,128)} %bitcast.14, f32[1024,256]{1,0:T(8,128)} %bitcast.16, s32[1,1024]{1,0:T(1,128)} %bitcast.19, s32[4,1024]{1,0:T(4,128)} %cells_hbm.1, s32[1,1024]{1,0:T(1,128)} %bitcast.20, f32[1,1024]{1,0:T(1,128)} %bitcast.21, ...), custom_call_target="tpu_custom_call" | custom-call | flops 400000000 | bytes 4000000 | tf_op jit(solution)/shard_map/pallas_call | solution.py:679
  5.6 0.0 copy-start.4
  5.6 0.0 copy-start.5
  5.6 8.5 %all-to-all-start = ((f32[16,136,128]{2,1,0:T(8,128)}), f32[16,136,128]{2,1,0:T(8,128)S(1)}, u32[]{:S(2)}, u32[]{:S(2)}) async-start(f32[16,136,128]{2,1,0:T(8,128)} %get-tuple-element.20), calls=%async_computation | async-start | bytes 2228224 | tf_op jit(solution)/shard_map/all_to_all | solution.py:715
  14.1 0.1 collective-permute-start
  14.2 0.5 collective-permute-start.1
  14.7 2.3 %collective-permute-done.uh_ref = f32[8,8,4096]{2,1,0:T(8,128)} collective-permute-done((f32[8,8,4096]{2,1,0:T(8,128)S(1)}, f32[8,8,4096]{2,1,0:T(8,128)}, u32[]{:S(2)}, u32[]{:S(2)}) %collective-permute-start) | collective-permute-done | bytes 1048608 | tf_op jit(solution)/shard_map/ppermute | solution.py:283
  17.0 1.5 %collective-permute-done.1.vh_ref = f32[8,8,4096]{2,1,0:T(8,128)} collective-permute-done((f32[8,8,4096]{2,1,0:T(8,128)S(1)}, f32[8,8,4096]{2,1,0:T(8,128)}, u32[]{:S(2)}, u32[]{:S(2)}) %collective-permute-start.1) | collective-permute-done | bytes 1048608 | tf_op jit(solution)/shard_map/ppermute | solution.py:283
  18.5 0.1 broadcast_in_dim.23.mask_ref.front_ref
  18.5 8.1 %shard_map.123 = (f32[8,512,128]{2,1,0:T(8,128)S(1)}, f32[8,512,128]{2,1,0:T(8,128)S(1)}) custom-call(f32[8,8,4096]{2,1,0:T(8,128)S(1)} %copy-done.4, f32[8,8,4096]{2,1,0:T(8,128)} %collective-permute-done.uh_ref, f32[8,8,4096]{2,1,0:T(8,128)S(1)} %copy-done.5, f32[8,8,4096]{2,1,0:T(8,128)} %collective-permute-done.1.vh_ref, ...), custom_call_target="tpu_custom_call" | custom-call | flops 1000000 | bytes 8000000 | tf_op jit(solution)/shard_map/pallas_call | solution.py:718
  26.7 1.3 %copy-done.2 = f32[8,512,128]{2,1,0:T(8,128)} copy-done((f32[8,512,128]{2,1,0:T(8,128)}, f32[8,512,128]{2,1,0:T(8,128)S(1)}, u32[]{:S(2)}) %copy-start.2) | copy-done | bytes 2097176
  28.0 1.3 %copy-done.3 = f32[8,512,128]{2,1,0:T(8,128)} copy-done((f32[8,512,128]{2,1,0:T(8,128)}, f32[8,512,128]{2,1,0:T(8,128)S(1)}, u32[]{:S(2)}) %copy-start.3) | copy-done | bytes 2097176
  29.3 10.6 %all-to-all-done.got_hbm.field = f32[16,136,128]{2,1,0:T(8,128)S(1)} async-done(((f32[16,136,128]{2,1,0:T(8,128)}), f32[16,136,128]{2,1,0:T(8,128)S(1)}, u32[]{:S(2)}, u32[]{:S(2)}) %all-to-all-start) | async-done | bytes 1114144 | tf_op jit(solution)/shard_map/all_to_all | solution.py:715
  39.9 0.1 broadcast_in_dim.24.mask_ref
  39.9 2.3 %shard_map.124 = (s32[128,128]{1,0:T(8,128)S(1)}, f32[4,1024,128]{2,1,0:T(8,128)S(1)}, f32[2,1024,128]{2,1,0:T(8,128)S(1)}, f32[8,512,128]{2,1,0:T(8,128)S(1)}, f32[8,512,128]{2,1,0:T(8,128)S(1)}) custom-call(f32[16,136,128]{2,1,0:T(8,128)S(1)} %all-to-all-done.got_hbm.field, f32[8,512,128]{2,1,0:T(8,128)} %copy-done.2, f32[8,512,128]{2,1,0:T(8,128)} %copy-done.3), custom_call_target="tpu_custom_call" | custom-call | flops 1000000 | bytes 6000000 | tf_op jit(solution)/shard_map/pallas_call | solution.py:730
  42.2 0.5 collective-permute-done.2.halo
  42.7 21.4 %shard_map.125 = (f32[16,136,128]{2,1,0:T(8,128)S(1)}, f32[16,64,128]{2,1,0:T(8,128)S(1)}) custom-call(f32[16,136,128]{2,1,0:T(8,128)S(1)} %all-to-all-done.got_hbm.field, f32[16,136,128]{2,1,0:T(8,128)S(1)} %collective-permute-done.2.halo, f32[8,512,128]{2,1,0:T(8,128)S(1)} %get-tuple-element.26.uw, f32[8,512,128]{2,1,0:T(8,128)S(1)} %get-tuple-element.27.vw, ...), custom_call_target="tpu_custom_call" | custom-call | flops 100000000 | bytes 16000000 | tf_op jit(solution)/shard_map/pallas_call | solution.py:753
  64.1 0.2 collective-permute-start.3
  64.3 1.8 %collective-permute-done.3.rim_ref = f32[16,64,128]{2,1,0:T(8,128)S(1)} collective-permute-done((f32[16,64,128]{2,1,0:T(8,128)S(1)}, f32[16,64,128]{2,1,0:T(8,128)S(1)}, u32[]{:S(2)}, u32[]{:S(2)}) %collective-permute-start.3) | collective-permute-done | bytes 524320 | tf_op jit(solution)/shard_map/ppermute | solution.py:283
  66.1 1.1 %shard_map.126 = f32[2064,128]{1,0:T(8,128)} custom-call(f32[16,136,128]{2,1,0:T(8,128)S(1)} %get-tuple-element.32.own_ref, f32[16,64,128]{2,1,0:T(8,128)S(1)} %collective-permute-done.3.rim_ref, f32[8,128]{1,0:T(8,128)S(1)} %broadcast_in_dim.24.mask_ref), custom_call_target="tpu_custom_call" | custom-call | flops 1000000 | bytes 3000000 | tf_op jit(solution)/shard_map/pallas_call | solution.py:775
  67.2 6.1 %all-to-all-start.1 = ((f32[2064,1,128]{2,1,0:T(1,128)}), f32[2064,1,128]{2,1,0:T(1,128)S(1)}, u32[]{:S(2)}, u32[]{:S(2)}) async-start(f32[2064,1,128]{2,1,0:T(1,128)} %bitcast.8), calls=%async_computation.1 | async-start | bytes 2113536 | tf_op jit(solution)/shard_map/all_to_all | solution.py:784
  73.3 0.1 copy.14
  73.4 24.7 %all-to-all-done.1 = f32[2064,1,128]{2,1,0:T(1,128)S(1)} async-done(((f32[2064,1,128]{2,1,0:T(1,128)}), f32[2064,1,128]{2,1,0:T(1,128)S(1)}, u32[]{:S(2)}, u32[]{:S(2)}) %all-to-all-start.1) | async-done | bytes 1056800 | tf_op jit(solution)/shard_map/all_to_all | solution.py:784
  98.0 3.3 %shard_map.127 = (f32[1024,256]{1,0:T(8,128)}, f32[8,128]{1,0:T(8,128)}) custom-call(f32[128,128]{1,0:T(8,128)S(1)} %bitcast.18, f32[1024,256]{1,0:T(8,128)S(1)} %bitcast.15, f32[1024,256]{1,0:T(8,128)S(1)} %bitcast.17, f32[2064,128]{1,0:T(8,128)S(1)} %bitcast.13, f32[8,128]{1,0:T(8,128)S(1)} %copy-done.6), custom_call_target="tpu_custom_call" | custom-call | flops 400000000 | bytes 4000000 | tf_op jit(solution)/shard_map/pallas_call | solution.py:788
  (14 shorter events, 0.0 us)
Async XLA Ops:
  5.6 8.5 %copy-start.4 = (f32[8,8,4096]{2,1,0:T(8,128)S(1)}, f32[8,8,4096]{2,1,0:T(8,128)}, u32[]{:S(2)}) copy-start(f32[8,8,4096]{2,1,0:T(8,128)} %u_ref.1) | copy-start | bytes 3145732
  5.6 8.6 %copy-start.5 = (f32[8,8,4096]{2,1,0:T(8,128)S(1)}, f32[8,8,4096]{2,1,0:T(8,128)}, u32[]{:S(2)}) copy-start(f32[8,8,4096]{2,1,0:T(8,128)} %v_ref.1) | copy-start | bytes 3145732
  5.6 34.2 %all-to-all-start = ((f32[16,136,128]{2,1,0:T(8,128)}), f32[16,136,128]{2,1,0:T(8,128)S(1)}, u32[]{:S(2)}, u32[]{:S(2)}) async-start(f32[16,136,128]{2,1,0:T(8,128)} %get-tuple-element.20), calls=%async_computation | async-start | bytes 2228224 | tf_op jit(solution)/shard_map/all_to_all | solution.py:715
  14.1 2.9 %collective-permute-start = (f32[8,8,4096]{2,1,0:T(8,128)S(1)}, f32[8,8,4096]{2,1,0:T(8,128)}, u32[]{:S(2)}, u32[]{:S(2)}) collective-permute-start(f32[8,8,4096]{2,1,0:T(8,128)S(1)} %copy-done.4), channel_id=1, source_target_pairs={{0,16},{16,0},{1,17},{17,1},{2,18},{18,2},{3,19},{19,3},{4,20},{20... | collective-permute-start | bytes 3145736 | tf_op jit(solution)/shard_map/ppermute | solution.py:283
  14.2 4.3 %collective-permute-start.1 = (f32[8,8,4096]{2,1,0:T(8,128)S(1)}, f32[8,8,4096]{2,1,0:T(8,128)}, u32[]{:S(2)}, u32[]{:S(2)}) collective-permute-start(f32[8,8,4096]{2,1,0:T(8,128)S(1)} %copy-done.5), channel_id=1, source_target_pairs={{0,16},{16,0},{1,17},{17,1},{2,18},{18,2},{3,19},{19,3},{4,20},{20... | collective-permute-start | bytes 3145736 | tf_op jit(solution)/shard_map/ppermute | solution.py:283
  26.6 1.4 %copy-start.2 = (f32[8,512,128]{2,1,0:T(8,128)}, f32[8,512,128]{2,1,0:T(8,128)S(1)}, u32[]{:S(2)}) copy-start(f32[8,512,128]{2,1,0:T(8,128)S(1)} %get-tuple-element.24.uw_hbm) | copy-start | bytes 6291460
  28.0 1.3 %copy-start.3 = (f32[8,512,128]{2,1,0:T(8,128)}, f32[8,512,128]{2,1,0:T(8,128)S(1)}, u32[]{:S(2)}) copy-start(f32[8,512,128]{2,1,0:T(8,128)S(1)} %get-tuple-element.25.vw_hbm) | copy-start | bytes 6291460
  39.9 2.8 %collective-permute-start.2 = (f32[16,136,128]{2,1,0:T(8,128)S(1)}, f32[16,136,128]{2,1,0:T(8,128)S(1)}, u32[]{:S(2)}, u32[]{:S(2)}) collective-permute-start(f32[16,136,128]{2,1,0:T(8,128)S(1)} %all-to-all-done.got_hbm.field), channel_id=1, source_target_pairs={{0,16},{16,0},{1,17},{17,1},{2,18},{18,2},{3,19},{19,3},{4,20},{20... | collective-permute-start | bytes 3342344 | tf_op jit(solution)/shard_map/ppermute | solution.py:283
  64.1 2.0 %collective-permute-start.3 = (f32[16,64,128]{2,1,0:T(8,128)S(1)}, f32[16,64,128]{2,1,0:T(8,128)S(1)}, u32[]{:S(2)}, u32[]{:S(2)}) collective-permute-start(f32[16,64,128]{2,1,0:T(8,128)S(1)} %get-tuple-element.33), channel_id=1, source_target_pairs={{0,16},{16,0},{1,17},{17,1},{2,18},{18,2},{3,19},{19,3},{4,20},{20... | collective-permute-start | bytes 1572872 | tf_op jit(solution)/shard_map/ppermute | solution.py:283
  67.1 6.1 %copy-start.7 = (f32[128,128]{1,0:T(8,128)S(1)}, f32[128,128]{1,0:T(8,128)}, u32[]{:S(2)}) copy-start(f32[128,128]{1,0:T(8,128)} %root_hbm.1) | copy-start | bytes 196612
  67.1 30.9 %copy-start = (f32[128,8,256]{2,1,0:T(8,128)S(1)}, f32[128,8,256]{2,1,0:T(8,128)}, u32[]{:S(2)}) copy-start(f32[128,8,256]{2,1,0:T(8,128)} %param.11) | copy-start | bytes 3145732
  67.2 30.9 %copy-start.1 = (f32[128,8,256]{2,1,0:T(8,128)S(1)}, f32[128,8,256]{2,1,0:T(8,128)}, u32[]{:S(2)}) copy-start(f32[128,8,256]{2,1,0:T(8,128)} %param.12) | copy-start | bytes 3145732
  67.2 30.9 %copy-start.6 = (f32[8,128]{1,0:T(8,128)S(1)}, f32[8,128]{1,0:T(8,128)}, u32[]{:S(2)}) copy-start(f32[8,128]{1,0:T(8,128)} %get-tuple-element.35.placed_ref) | copy-start | bytes 12292
  67.2 30.8 %all-to-all-start.1 = ((f32[2064,1,128]{2,1,0:T(1,128)}), f32[2064,1,128]{2,1,0:T(1,128)S(1)}, u32[]{:S(2)}, u32[]{:S(2)}) async-start(f32[2064,1,128]{2,1,0:T(1,128)} %bitcast.8), calls=%async_computation.1 | async-start | bytes 2113536 | tf_op jit(solution)/shard_map/all_to_all | solution.py:784
